TPU v7x, 32 devices: a whole 2x2x4 slice. The times are simulated.
32 devices in a mesh: band: 8 (over z, y), batch: 4 (over x, core).
Axes of the slice: x: 2, y: 2, z: 4, core: 2. Of those that a mesh axis runs over, the one named last changes fastest.
Arguments:
- activations: bfloat16 [64, 1, 1024, 384], P('band', None, 'batch'), may hold values from -6 to 6
- cotangent: bfloat16 [64, 1, 1024, 384], P('band', None, 'batch'), may hold values from -6 to 6
- frame_counts: int32 [1], replicated, may hold values from 896 to 1024, as said below
- slot_bands: int32 [64], replicated, may hold values from -1 to 61, as said below
- time_prenorm: bfloat16 [384], replicated, may hold values from 0.5 to 1.5
- time_project: bfloat16 [384, 1536], replicated, may hold values from -0.3125 to 0.3125
- time_gating: bfloat16 [384, 8], replicated, may hold values from -0.3125 to 0.3125
- time_output: bfloat16 [512, 384], replicated, may hold values from -6 to 6
- time_midnorm: bfloat16 [384], replicated, may hold values from 0.5 to 1.5
- time_expand: bfloat16 [384, 1536], replicated, may hold values from -0.3125 to 0.3125
- time_shrink: bfloat16 [1536, 384], replicated, may hold values from -0.15625 to 0.15625
- band_prenorm: bfloat16 [384], replicated, may hold values from 0.5 to 1.5
- band_project: bfloat16 [384, 1536], replicated, may hold values from -0.3125 to 0.3125
- band_gating: bfloat16 [384, 8], replicated, may hold values from -0.3125 to 0.3125
- band_output: bfloat16 [512, 384], replicated, may hold values from -3 to 3
- band_midnorm: bfloat16 [384], replicated, may hold values from 0.5 to 1.5
- band_expand: bfloat16 [384, 1536], replicated, may hold values from -0.3125 to 0.3125
- band_shrink: bfloat16 [1536, 384], replicated, may hold values from -0.15625 to 0.15625
Outputs:
- layer_output: bfloat16 [64, 1, 1024, 384], P('band', None, 'batch')
- input_grad: float32 [64, 1, 1024, 384], P('band', None, 'batch')
- time_prenorm_grad: float32 [384], replicated
- time_project_grad: float32 [384, 1536], replicated
- time_gating_grad: float32 [384, 8], replicated
- time_output_grad: float32 [512, 384], replicated
- time_midnorm_grad: float32 [384], replicated
- time_expand_grad: float32 [384, 1536], replicated
- time_shrink_grad: float32 [1536, 384], replicated
- band_prenorm_grad: float32 [384], replicated
- band_project_grad: float32 [384, 1536], replicated
- band_gating_grad: float32 [384, 8], replicated
- band_output_grad: float32 [512, 384], replicated
- band_midnorm_grad: float32 [384], replicated
- band_expand_grad: float32 [384, 1536], replicated
- band_shrink_grad: float32 [1536, 384], replicated
Inputs may be any that keep to these rules, and one draw needn't show every extreme that they name: `frame_counts`: real frames come first. `slot_bands`: each band 0 to 61 stands in exactly one slot; the other 2 slots hold -1.
All inputs are finite; a program needn't handle non-finite values.
Results may differ from a plain program's by a relative error of at most 0.03.
Values may be sent and summed in bfloat16 or wider, within the bound.
A program may use at most 448 MiB of HBM per device.

v0:
```python
import math

import jax
import jax.numpy as jnp
from jax import lax
from jax.sharding import PartitionSpec as P

EPSILON = 1e-05
NEG_FILL = -1000000000.0
TIME_LAYOUT = ("bqhe", "bkhe")
BAND_LAYOUT = ("qbhe", "kbhe")


def rms_scale(residual, gain):
    return (
        residual * lax.rsqrt(jnp.mean(residual * residual, axis=-1, keepdims=True) + EPSILON) * gain
    )


def gelu_exact(values):
    return jax.nn.gelu(values, approximate=False)


def rotary_tables(positions, head_size):
    half_size = head_size // 2
    rates = jnp.exp(-math.log(10000.0) * jnp.arange(half_size, dtype=jnp.float32) / half_size)
    angles = positions[:, None] * rates[None, :]
    return (jnp.cos(angles), jnp.sin(angles))


def rotate(vectors, cos_table, sin_table):
    half_size = vectors.shape[-1] // 2
    first = vectors[..., :half_size]
    second = vectors[..., half_size:]
    return jnp.concatenate(
        [first * cos_table - second * sin_table, first * sin_table + second * cos_table], axis=-1
    )


def token_sum(left, right):
    return lax.dot_general(
        left.reshape(-1, left.shape[-1]),
        right.reshape(-1, right.shape[-1]),
        (((0,), (0,)), ((), ())),
        preferred_element_type=jnp.float32,
    )


def back_dot(gradient, weight):
    return lax.dot_general(
        gradient,
        weight,
        (((gradient.ndim - 1,), (1,)), ((), ())),
        preferred_element_type=jnp.float32,
    )


def block_forward(queries, key_rows, value_rows, key_valid, layout):
    query_form, key_form = layout
    scores = (
        jnp.einsum(
            query_form + "," + key_form + "->bhqk",
            queries,
            key_rows,
            preferred_element_type=jnp.float32,
        )
        * 0.125
    )
    scores = jnp.where(key_valid[:, None, None, :], scores, NEG_FILL)
    highest = jnp.max(scores, axis=-1, keepdims=True)
    exponents = jnp.exp(scores - highest)
    totals = jnp.sum(exponents, axis=-1, keepdims=True)
    soft_weights = (exponents / totals).astype(jnp.bfloat16)
    output = jnp.einsum(
        "bhqk," + key_form + "->" + query_form,
        soft_weights,
        value_rows,
        preferred_element_type=jnp.float32,
    )
    return (output, highest + jnp.log(totals))


def block_backward(queries, key_rows, value_rows, key_valid, log_totals, out_grad, layout):
    query_form, key_form = layout
    scores = (
        jnp.einsum(
            query_form + "," + key_form + "->bhqk",
            queries,
            key_rows,
            preferred_element_type=jnp.float32,
        )
        * 0.125
    )
    soft_weights = jnp.where(key_valid[:, None, None, :], jnp.exp(scores - log_totals), 0.0)
    weight_grad = jnp.einsum(
        query_form + "," + key_form + "->bhqk",
        out_grad,
        value_rows,
        preferred_element_type=jnp.float32,
    )
    score_grad = (
        soft_weights * (weight_grad - jnp.sum(soft_weights * weight_grad, axis=-1, keepdims=True))
    ).astype(jnp.bfloat16)
    query_grad = (
        jnp.einsum(
            "bhqk," + key_form + "->" + query_form,
            score_grad,
            key_rows,
            preferred_element_type=jnp.float32,
        )
        * 0.125
    )
    key_grad = (
        jnp.einsum(
            "bhqk," + query_form + "->" + key_form,
            score_grad,
            queries,
            preferred_element_type=jnp.float32,
        )
        * 0.125
    )
    value_grad = jnp.einsum(
        "bhqk," + query_form + "->" + key_form,
        soft_weights.astype(jnp.bfloat16),
        out_grad,
        preferred_element_type=jnp.float32,
    )
    return (query_grad, key_grad, value_grad)


def time_attend(queries, key_rows, value_rows, key_valid):
    keys_full, values_full = (
        lax.all_gather(key_rows, "batch", axis=1, tiled=True),
        lax.all_gather(value_rows, "batch", axis=1, tiled=True),
    )
    output, log_totals = block_forward(queries, keys_full, values_full, key_valid, TIME_LAYOUT)
    return (output, (log_totals, keys_full, values_full))


def time_attend_back(queries, key_rows, value_rows, key_valid, attn_kept, out_grad):
    log_totals, keys_full, values_full = attn_kept
    query_grad, key_full_grad, value_full_grad = block_backward(
        queries, keys_full, values_full, key_valid, log_totals, out_grad, TIME_LAYOUT
    )
    key_grad, value_grad = (
        lax.psum_scatter(
            key_full_grad.astype(jnp.bfloat16), "batch", scatter_dimension=1, tiled=True
        ).astype(jnp.float32),
        lax.psum_scatter(
            value_full_grad.astype(jnp.bfloat16), "batch", scatter_dimension=1, tiled=True
        ).astype(jnp.float32),
    )
    return (query_grad, key_grad, value_grad)


def band_attend(queries, key_rows, value_rows, key_valid):
    return block_forward(queries, key_rows, value_rows, key_valid, BAND_LAYOUT)


def band_attend_back(queries, key_rows, value_rows, key_valid, attn_kept, out_grad):
    return block_backward(
        queries, key_rows, value_rows, key_valid, attn_kept, out_grad, BAND_LAYOUT
    )


def layer_forward(residual, params, tables, key_valid, attend):
    prenorm, project, gating, output_weight, midnorm, expand, shrink = params
    cos_table, sin_table = tables
    normed = rms_scale(residual, prenorm.astype(jnp.float32)).astype(jnp.bfloat16)
    projected = jnp.dot(normed, project, preferred_element_type=jnp.float32)
    gate_logits = jnp.dot(normed, gating, preferred_element_type=jnp.float32)
    inner_width = output_weight.shape[0]
    head_count = gating.shape[1]
    head_shape = residual.shape[:-1] + (head_count, inner_width // head_count)
    queries = rotate(projected[..., :inner_width].reshape(head_shape), cos_table, sin_table).astype(
        jnp.bfloat16
    )
    key_rows = rotate(
        projected[..., inner_width : 2 * inner_width].reshape(head_shape), cos_table, sin_table
    ).astype(jnp.bfloat16)
    value_rows = projected[..., 2 * inner_width :].reshape(head_shape).astype(jnp.bfloat16)
    attended, attn_kept = attend(queries, key_rows, value_rows, key_valid)
    gate_values = jax.nn.sigmoid(gate_logits)
    mixed_heads = (
        (attended * gate_values[..., None])
        .reshape(residual.shape[:-1] + (inner_width,))
        .astype(jnp.bfloat16)
    )
    middle = residual + jnp.dot(mixed_heads, output_weight, preferred_element_type=jnp.float32)
    normed_ffn = rms_scale(middle, midnorm.astype(jnp.float32)).astype(jnp.bfloat16)
    hidden = jnp.dot(normed_ffn, expand, preferred_element_type=jnp.float32)
    active = gelu_exact(hidden).astype(jnp.bfloat16)
    result = middle + jnp.dot(active, shrink, preferred_element_type=jnp.float32)
    kept_values = (
        residual,
        normed,
        gate_logits,
        queries,
        key_rows,
        value_rows,
        attn_kept,
        attended,
        mixed_heads,
        middle,
        normed_ffn,
        hidden,
        active,
    )
    return (result, kept_values)


def layer_backward(result_grad, params, kept_values, tables, key_valid, attend_back):
    prenorm, project, gating, output_weight, midnorm, expand, shrink = params
    (
        residual,
        normed,
        gate_logits,
        queries,
        key_rows,
        value_rows,
        attn_kept,
        attended,
        mixed_heads,
        middle,
        normed_ffn,
        hidden,
        active,
    ) = kept_values
    cos_table, sin_table = tables
    branch_grad = result_grad.astype(jnp.bfloat16)
    shrink_grad = token_sum(active, branch_grad)
    active_grad = back_dot(branch_grad, shrink)
    hidden_grad = jax.vjp(gelu_exact, hidden)[1](active_grad)[0].astype(jnp.bfloat16)
    expand_grad = token_sum(normed_ffn, hidden_grad)
    normed_ffn_grad = back_dot(hidden_grad, expand)
    middle_norm_grad, midnorm_grad = jax.vjp(rms_scale, middle, midnorm.astype(jnp.float32))[1](
        normed_ffn_grad
    )
    middle_grad = result_grad + middle_norm_grad
    attn_branch = middle_grad.astype(jnp.bfloat16)
    output_grad = token_sum(mixed_heads, attn_branch)
    mixed_grad = back_dot(attn_branch, output_weight).reshape(attended.shape)
    gate_values = jax.nn.sigmoid(gate_logits)
    attended_grad = (mixed_grad * gate_values[..., None]).astype(jnp.bfloat16)
    logit_grad = (
        jnp.sum(mixed_grad * attended, axis=-1) * gate_values * (1.0 - gate_values)
    ).astype(jnp.bfloat16)
    query_grad, key_grad, value_grad = attend_back(
        queries, key_rows, value_rows, key_valid, attn_kept, attended_grad
    )
    flat_shape = residual.shape[:-1] + (-1,)
    projected_grad = jnp.concatenate(
        [
            rotate(query_grad, cos_table, -sin_table).reshape(flat_shape),
            rotate(key_grad, cos_table, -sin_table).reshape(flat_shape),
            value_grad.reshape(flat_shape),
        ],
        axis=-1,
    ).astype(jnp.bfloat16)
    project_grad = token_sum(normed, projected_grad)
    gating_grad = token_sum(normed, logit_grad)
    normed_grad = back_dot(projected_grad, project) + back_dot(logit_grad, gating)
    residual_norm_grad, prenorm_grad = jax.vjp(rms_scale, residual, prenorm.astype(jnp.float32))[1](
        normed_grad
    )
    return (
        middle_grad + residual_norm_grad,
        (
            prenorm_grad,
            project_grad,
            gating_grad,
            output_grad,
            midnorm_grad,
            expand_grad,
            shrink_grad,
        ),
    )


def shards(
    activations,
    cotangent,
    frame_counts,
    slot_bands,
    time_prenorm,
    time_project,
    time_gating,
    time_output,
    time_midnorm,
    time_expand,
    time_shrink,
    band_prenorm,
    band_project,
    band_gating,
    band_output,
    band_midnorm,
    band_expand,
    band_shrink,
):
    slot_dev, clip_count, frame_dev, model_width = activations.shape
    slot_count = slot_bands.shape[0]
    frames_all = frame_dev * lax.axis_size("batch")
    head_size = time_output.shape[0] // time_gating.shape[1]
    time_params = (
        time_prenorm,
        time_project,
        time_gating,
        time_output,
        time_midnorm,
        time_expand,
        time_shrink,
    )
    band_params = (
        band_prenorm,
        band_project,
        band_gating,
        band_output,
        band_midnorm,
        band_expand,
        band_shrink,
    )
    own_bands = lax.dynamic_slice_in_dim(slot_bands, lax.axis_index("band") * slot_dev, slot_dev)
    frame_start = lax.axis_index("batch") * frame_dev
    own_frames = frame_start + jnp.arange(frame_dev, dtype=jnp.int32)
    frame_valid = own_frames[None, :] < frame_counts[:, None]
    row_valid = (own_bands >= 0)[:, None, None] & frame_valid[None]
    full_valid = jnp.arange(frames_all, dtype=jnp.int32)[None, :] < frame_counts[:, None]
    time_valid = jnp.broadcast_to(full_valid[None], (slot_dev, clip_count, frames_all)).reshape(
        slot_dev * clip_count, frames_all
    )
    time_cos, time_sin = rotary_tables(own_frames.astype(jnp.float32), head_size)
    time_tables = (time_cos[None, :, None, :], time_sin[None, :, None, :])
    band_cos, band_sin = rotary_tables(jnp.maximum(slot_bands, 0).astype(jnp.float32), head_size)
    band_tables = (band_cos[:, None, None, :], band_sin[:, None, None, :])
    residual = activations.astype(jnp.float32).reshape(
        slot_dev * clip_count, frame_dev, model_width
    )
    time_result, time_kept = layer_forward(
        residual, time_params, time_tables, time_valid, time_attend
    )
    masked_cot = jnp.where(row_valid[..., None], cotangent, jnp.zeros((), jnp.bfloat16)).reshape(
        slot_dev, clip_count * frame_dev, model_width
    )
    frame_rows = lax.all_to_all(
        time_result.astype(jnp.bfloat16), "band", split_axis=1, concat_axis=0, tiled=True
    ).astype(time_result.dtype)
    band_valid = jnp.broadcast_to((slot_bands >= 0)[None, :], (frame_rows.shape[1], slot_count))
    band_result, band_kept = layer_forward(
        frame_rows, band_params, band_tables, band_valid, band_attend
    )
    back_rows = lax.all_to_all(
        band_result.astype(jnp.bfloat16), "band", split_axis=0, concat_axis=1, tiled=True
    ).astype(band_result.dtype)
    layer_output = jnp.where(
        row_valid[..., None], back_rows.reshape(activations.shape), 0.0
    ).astype(jnp.bfloat16)
    frame_cot = lax.all_to_all(masked_cot, "band", split_axis=1, concat_axis=0, tiled=True)
    frame_grad, band_grads = layer_backward(
        frame_cot.astype(jnp.float32),
        band_params,
        band_kept,
        band_tables,
        band_valid,
        band_attend_back,
    )
    slot_grad = lax.all_to_all(
        frame_grad.astype(jnp.bfloat16), "band", split_axis=0, concat_axis=1, tiled=True
    ).astype(frame_grad.dtype)
    input_grad, time_grads = layer_backward(
        slot_grad, time_params, time_kept, time_tables, time_valid, time_attend_back
    )
    input_grad = input_grad.reshape(activations.shape)
    all_grads = lax.psum(
        (
            time_grads[0],
            time_grads[1],
            time_grads[2],
            time_grads[3],
            time_grads[4],
            time_grads[5],
            time_grads[6],
            band_grads[0],
            band_grads[1],
            band_grads[2],
            band_grads[3],
            band_grads[4],
            band_grads[5],
            band_grads[6],
        ),
        ("band", "batch"),
    )
    return (
        layer_output,
        input_grad,
        all_grads[0],
        all_grads[1],
        all_grads[2],
        all_grads[3],
        all_grads[4],
        all_grads[5],
        all_grads[6],
        all_grads[7],
        all_grads[8],
        all_grads[9],
        all_grads[10],
        all_grads[11],
        all_grads[12],
        all_grads[13],
    )


def solution(mesh):
    return jax.shard_map(
        shards,
        mesh=mesh,
        in_specs=(
            P("band", None, "batch", None),
            P("band", None, "batch", None),
            P(),
            P(),
            P(),
            P(),
            P(),
            P(),
            P(),
            P(),
            P(),
            P(),
            P(),
            P(),
            P(),
            P(),
            P(),
            P(),
        ),
        out_specs=(
            P("band", None, "batch", None),
            P("band", None, "batch", None),
            P(),
            P(),
            P(),
            P(),
            P(),
            P(),
            P(),
            P(),
            P(),
            P(),
            P(),
            P(),
            P(),
            P(),
        ),
        check_vma=False,
    )
```

profile of v0, /device:TPU:0, one launch (start us, length us, event | category | flops | bytes accessed | tf_op | source)
XLA Modules:
  0.0 1339.1 jit_solution(8450229181337729063)
XLA Ops:
  51.6 52.7 %all-gather.5.cloned.1.call-done = bf16[8,1024,8,64]{1,3,2,0:T(8,128)(2,1)} async-done(((bf16[8,256,8,64]{1,3,2,0:T(8,128)(2,1)}), bf16[8,1024,8,64]{1,3,2,0:T(8,128)(2,1)}) %all-gather.5.cloned.1.call-update) | async-done | bytes 8388624 | tf_op jit(solution)/shard_map/all_gather | solution.py:133
  104.4 30.6 %select_reduce_fusion = (f32[8,8,256]{2,1,0:T(8,128)S(1)}, f32[8,8,256,1024]{3,2,1,0:T(8,128)}) fusion(pred[1024]{0:T(1024)(128)(4,1)S(1)} %iota_compare_fusion, bf16[8,1024,8,64]{1,3,2,0:T(8,128)(2,1)} %all-gather.5.cloned.1.call-done, bf16[8,256,8,32]{1,3,2,0:T(8,128)(2,1)} %get-tuple-element.145, bf16[8,256,8,32]{1,3,2,0:T(8,128)(2,1)} %get-tuple-element.144), kind=kOutput, calls=%fused_computation.5 | convolution fusion | flops 2201993216 | bytes 77661184 | tf_op jit(solution)/shard_map/bqhe,bkhe->bhqk/dot_general | solution.py:61
  135.0 21.8 %fusion = f32[8,8,256]{2,1,0:T(8,128)S(1)} fusion(f32[8,8,256,1024]{3,2,1,0:T(8,128)} %get-tuple-element.165, f32[8,8,256]{2,1,0:T(8,128)S(1)} %get-tuple-element.164, pred[1024]{0:T(1024)(128)(4,1)S(1)} %iota_compare_fusion), kind=kLoop, calls=%fused_computation.6 | loop fusion | flops 67092480 | bytes 67240960 | tf_op jit(solution)/shard_map/reduce_sum | solution.py:72
  166.0 29.5 %fusion.27 = (bf16[8,256,8,64]{1,3,2,0:T(8,128)(2,1)}, f32[8,8,64,256]{3,2,1,0:T(8,128)}) fusion(f32[8,256,8]{1,2,0:T(8,128)S(1)} %fusion.90, bf16[8,1024,8,64]{1,3,2,0:T(8,128)(2,1)} %all-gather.3.cloned.1.call-done, f32[8,8,256,1024]{3,2,1,0:T(8,128)} %get-tuple-element.165, f32[8,8,256]{2,1,0:T(8,128)S(1)} %fusion, ...), kind=kOutput, calls=%fused_computation.95 | convolution fusion | flops 2233466880 | bytes 81986560 | tf_op jit(solution)/shard_map/bhqk,bkhe->bqhe/dot_general | solution.py:74
  205.3 29.0 %multiply_convert_fusion.3 = (bf16[8,256,1536]{2,1,0:T(8,128)(2,1)S(1)}, f32[8,256,1536]{2,1,0:T(8,128)}) fusion(f32[8,256,1536]{2,1,0:T(8,128)S(1)} %get-tuple-element.170, u8[256,1536]{1,0:T(8,128)(4,1)S(1)} %get-tuple-element.97, u8[256,1536]{1,0:T(8,128)(4,1)S(1)} %get-tuple-element.96), kind=kLoop, calls=%fused_computation.36 | loop fusion | flops 220200960 | bytes 32243712 | tf_op jit(solution)/shard_map/convert_element_type | solution.py:192
  246.7 36.4 %all-to-all-done = bf16[8,256,384]{2,0,1:T(8,128)(2,1)S(1)} async-done(((bf16[8,256,384]{2,0,1:T(8,128)(2,1)}), bf16[8,256,384]{2,0,1:T(8,128)(2,1)S(1)}, u32[]{:S(2)}, u32[]{:S(2)}) %all-to-all-start) | async-done | bytes 1572896 | tf_op jit(solution)/shard_map/all_to_all | solution.py:344
  322.5 27.1 %fusion.140 = (f32[64,32,8,32]{3,2,1,0:T(8,128)}, f32[64,32,8,32]{3,2,1,0:T(8,128)}, f32[64,32,8,32]{3,2,1,0:T(8,128)}, f32[64,32,8,32]{3,2,1,0:T(8,128)}) fusion(f32[64,32,8,64]{3,2,1,0:T(8,128)} %reshape.481, f32[64,32,8,64]{3,2,1,0:T(8,128)} %reshape.482), kind=kLoop, calls=%fused_computation.265 | loop fusion | bytes 16777216 | tf_op jit(solution)/shard_map/slice | solution.py:33
  349.6 44.3 %subtract_convert_fusion.3 = (bf16[64,32,8,32]{3,0,2,1:T(8,128)(2,1)}, bf16[64,32,8,32]{3,0,2,1:T(8,128)(2,1)}, bf16[64,32,8,32]{3,0,2,1:T(8,128)(2,1)}, bf16[64,32,8,32]{3,0,2,1:T(8,128)(2,1)}) fusion(f32[64,32,8,32]{3,2,1,0:T(8,128)} %get-tuple-element.137, f32[64,32,8,32]{3,2,1,0:T(8,128)} %get-tuple-element.136, f32[64,32]{1,0:T(8,128)S(1)} %get-tuple-element.162, ...), kind=kLoop, calls=%fused_computation.70 | loop fusion | flops 8388608 | bytes 12599296 | tf_op jit(solution)/shard_map/convert.30
  393.9 14.8 %select_reduce_fusion.1 = (f32[32,8,64]{2,1,0:T(8,128)S(1)}, f32[32,8,64,64]{2,3,1,0:T(8,128)}) fusion(pred[64]{0:T(512)(128)(4,1)S(1)} %broadcast_compare_fusion, bf16[64,32,8,32]{3,0,2,1:T(8,128)(2,1)} %get-tuple-element.152, bf16[64,32,8,32]{3,0,2,1:T(8,128)(2,1)} %get-tuple-element.153, bf16[64,32,8,32]{3,0,2,1:T(8,128)(2,1)} %get-tuple-element.125, ...), kind=kOutput, calls=%fused_computation.71 | convolution fusion | flops 145735680 | bytes 8454208 | tf_op jit(solution)/shard_map/qbhe,kbhe->bhqk/dot_general | solution.py:61
  432.8 32.6 %multiply_convert_fusion.2 = (bf16[64,32,1536]{2,1,0:T(8,128)(2,1)S(1)}, f32[64,32,1536]{2,1,0:T(8,128)}, f32[64,32,1536]{2,1,0:T(8,128)}) fusion(bf16[384,1536]{1,0:T(8,128)(2,1)S(1)} %copy-done, f32[64,32,384]{2,1,0:T(8,128)S(1)} %get-tuple-element.176, f32[384]{0:T(512)S(1)} %convert_element_type.216, f32[64,32]{1,0:T(8,128)S(1)} %fusion.107), kind=kOutput, calls=%fused_computation.23 | convolution fusion | flops 2622750720 | bytes 35792384 | tf_op jit(solution)/shard_map/dot_general | solution.py:191
  476.4 37.0 %all-to-all-done.1 = bf16[64,32,384]{2,1,0:T(8,128)(2,1)S(1)} async-done(((bf16[64,32,384]{2,1,0:T(8,128)(2,1)}), bf16[64,32,384]{2,1,0:T(8,128)(2,1)S(1)}, u32[]{:S(2)}, u32[]{:S(2)}) %all-to-all-start.1) | async-done | bytes 1572896 | tf_op jit(solution)/shard_map/all_to_all | solution.py:351
  521.9 37.1 %all-to-all-done.2 = bf16[8,256,384]{2,0,1:T(8,128)(2,1)S(1)} async-done(((bf16[8,256,384]{2,0,1:T(8,128)(2,1)}), bf16[8,256,384]{2,0,1:T(8,128)(2,1)S(1)}, u32[]{:S(2)}, u32[]{:S(2)}) %all-to-all-start.2) | async-done | bytes 1572896 | tf_op jit(solution)/shard_map/all_to_all | solution.py:357
  587.4 13.4 %multiply_reduce_fusion.1 = (f32[32,8,64]{2,1,0:T(8,128)S(1)}, f32[32,8,64,64]{2,3,1,0:T(8,128)}) fusion(f32[32,8,64,64]{2,3,1,0:T(8,128)S(1)} %bitcast.235, f32[32,8,64]{2,1,0:T(8,128)S(1)} %log_add_fusion, pred[64]{0:T(512)(128)(4,1)S(1)} %copy-done.107, f32[64,32,8,64]{0,3,2,1:T(8,128)} %bitcast.238, f32[64,32,8]{0,2,1:T(8,128)S(1)} %copy-done.55, ...), kind=kOutput, calls=%fused_computation.62 | convolution fusion | flops 141541376 | bytes 14876736 | tf_op jit(solution)/shard_map/qbhe,kbhe->bhqk/dot_general | solution.py:95
  633.2 19.3 %subtract_convert_fusion.1 = (bf16[64,32,8,32]{3,0,2,1:T(8,128)(2,1)}, bf16[64,32,8,32]{3,0,2,1:T(8,128)(2,1)}, bf16[64,32,8,32]{3,0,2,1:T(8,128)(2,1)}, bf16[64,32,8,32]{3,0,2,1:T(8,128)(2,1)}) fusion(f32[64,32,8,64]{3,0,2,1:T(8,128)} %multiply_bitcast_fusion.1, f32[64,32]{1,0:T(8,128)S(1)} %copy-done.92, f32[64,32]{1,0:T(8,128)S(1)} %copy-done.79, ...), kind=kLoop, calls=%fused_computation.59 | loop fusion | flops 8388608 | bytes 12599296 | tf_op jit(solution)/shard_map/convert.26
  706.1 37.1 %all-to-all-done.3 = bf16[64,32,384]{2,1,0:T(8,128)(2,1)S(1)} async-done(((bf16[64,32,384]{2,1,0:T(8,128)(2,1)}), bf16[64,32,384]{2,1,0:T(8,128)(2,1)S(1)}, u32[]{:S(2)}, u32[]{:S(2)}) %all-to-all-start.3) | async-done | bytes 1572896 | tf_op jit(solution)/shard_map/all_to_all | solution.py:366
  746.0 12.6 add_convert_fusion
  773.5 46.8 %multiply_reduce_fusion = (f32[8,8,256]{2,1,0:T(8,128)S(1)}, f32[8,8,256,1024]{3,2,1,0:T(8,128)}) fusion(f32[8,8,256,1024]{3,2,1,0:T(8,128)} %get-tuple-element.165, f32[8,8,256]{2,1,0:T(8,128)S(1)} %log_add_fusion.1, pred[1024]{0:T(1024)(128)(4,1)S(1)} %copy-done.90, bf16[8,1024,8,64]{1,3,2,0:T(8,128)(2,1)S(1)} %bitcast.253, ...), kind=kOutput, calls=%fused_computation.1 | convolution fusion | flops 2233450496 | bytes 146998272 | tf_op jit(solution)/shard_map/bqhe,bkhe->bhqk/dot_general | solution.py:95
  820.4 53.3 %multiply_convert_fusion = bf16[8,8,256,1024]{3,2,1,0:T(8,128)(2,1)} fusion(f32[8,8,256,1024]{3,2,1,0:T(8,128)} %get-tuple-element.186, f32[8,8,256,1024]{3,2,1,0:T(8,128)} %get-tuple-element.165, f32[8,8,256]{2,1,0:T(8,128)S(1)} %get-tuple-element.185, f32[8,8,256]{2,1,0:T(8,128)S(1)} %log_add_fusion.1, pred[1024]{0:T(1024)(128)(4,1)S(1)} %copy-done.90), kind=kLoop, calls=%fused_computation | loop fusion | flops 100663296 | bytes 167904256 | tf_op jit(solution)/shard_map/convert_element_type | solution.py:103
  873.7 17.3 %fusion.23 = bf16[8,1024,8,64]{1,3,2,0:T(8,128)(2,1)} fusion(bf16[8,8,256,1024]{3,2,1,0:T(8,128)(2,1)} %multiply_convert_fusion, bf16[8,256,8,32]{1,3,2,0:T(8,128)(2,1)S(1)} %copy-done.33, bf16[8,256,8,32]{1,3,2,0:T(8,128)(2,1)S(1)} %copy-done.32), kind=kOutput, calls=%fused_computation.80 | convolution fusion | flops 2160066560 | bytes 44040192 | tf_op jit(solution)/shard_map/bhqk,bqhe->bkhe/dot_general | solution.py:114
  891.1 33.9 %convert_bitcast_fusion = bf16[8,1024,8,64]{1,3,2,0:T(8,128)(2,1)} fusion(f32[8,8,256,1024]{3,2,1,0:T(8,128)} %get-tuple-element.165, f32[8,8,256]{2,1,0:T(8,128)S(1)} %log_add_fusion.1, pred[1024]{0:T(1024)(128)(4,1)S(1)} %copy-done.90, f32[8,256,8,64]{1,3,2,0:T(8,128)} %bitcast.243, f32[8,256,8]{1,2,0:T(8,128)S(1)} %copy-done.85), kind=kOutput, calls=%fused_computation.54 | convolution fusion | flops 2220883968 | bytes 79823872 | tf_op jit(solution)/shard_map/bhqk,bqhe->bkhe/dot_general | solution.py:122
  958.9 19.1 %multiply_bitcast_fusion.2 = f32[8,256,8,64]{1,3,2,0:T(8,128)} fusion(bf16[8,1024,8,64]{1,3,2,0:T(8,128)(2,1)S(1)} %bitcast.241, bf16[8,8,256,1024]{3,2,1,0:T(8,128)(2,1)} %multiply_convert_fusion), kind=kOutput, calls=%fused_computation.97 | convolution fusion | flops 2148532224 | bytes 46137344 | tf_op jit(solution)/shard_map/bhqk,bkhe->bqhe/dot_general | solution.py:105
  993.3 42.1 %reduce-scatter.5.cloned.1.call-done = bf16[8,256,8,64]{1,3,2,0:T(8,128)(2,1)} async-done(((bf16[8,1024,8,64]{1,3,2,0:T(8,128)(2,1)}), bf16[8,256,8,64]{1,3,2,0:T(8,128)(2,1)}) %reduce-scatter.5.cloned.1.call-update) | async-done | bytes 2097168 | tf_op jit(solution)/shard_map/reduce_scatter | solution.py:149
  1058.6 42.4 %all-reduce = (f32[384]{0:T(512)}, f32[384,8]{0,1:T(8,128)}, f32[384]{0:T(512)}, f32[384]{0:T(512)}, f32[384,8]{0,1:T(8,128)}, /*index=5*/f32[384]{0:T(512)}) all-reduce(f32[384]{0:T(512)S(1)} %get-tuple-element.102, f32[384,8]{0,1:T(8,128)S(1)} %convolution_bitcast_fusion.5, ...), channel_id=1, replica_groups=mesh['band'=8,'batch'=4] {'band','batch'}, use_global_device_ids=true, to_apply=%region_19.20 | all-reduce | flops 7680 | bytes 61440 | tf_op jit(solution)/shard_map/psum | solution.py:373
  1105.5 213.6 %all-reduce.4.cloned.1.call-done = (f32[384,1536]{1,0:T(8,128)}, f32[512,384]{1,0:T(8,128)}, f32[384,1536]{1,0:T(8,128)}, f32[1536,384]{1,0:T(8,128)}, f32[384,1...) async-done(((f32[384,1536]{1,0:T(8,128)}, f32[512,384]{1,0:T(8,128)}, f32[384,1536]{1,0:T(8,128)}, f32[1536,384]{1,0:T(8,128)}, ...) | async-done | bytes 15728656 | tf_op jit(solution)/shard_map/psum | solution.py:373
  (416 shorter events, 379.1 us)
Async XLA Ops:
  7.2 425.6 %copy-start = (bf16[384,1536]{1,0:T(8,128)(2,1)S(1)}, bf16[384,1536]{1,0:T(8,128)(2,1)}, u32[]{:S(2)}) copy-start(bf16[384,1536]{1,0:T(8,128)(2,1)} %param.34) | copy-start | bytes 3538948
  7.2 97.2 %all-gather.5.cloned.1.call-start = ((), (), s32[]{:S(2)}) async-start(), calls=%async_computation.7 | async-start | bytes 10485760 | tf_op jit(solution)/shard_map/all_gather | solution.py:133
  42.1 123.8 %all-gather.3.cloned.1.call-start = ((), (), s32[]{:S(2)}) async-start(), calls=%async_computation.6 | async-start | bytes 10485760 | tf_op jit(solution)/shard_map/all_gather | solution.py:134
  50.9 147.7 %copy-start.97 = (f32[384]{0:T(512)}, f32[384]{0:T(512)S(1)}, u32[]{:S(2)}) copy-start(f32[384]{0:T(512)S(1)} %convert_element_type.200) | copy-start | bytes 4612
  51.0 114.9 %copy-start.89 = (pred[1024]{0:T(1024)(128)(4,1)}, pred[1024]{0:T(1024)(128)(4,1)S(1)}, u32[]{:S(2)}) copy-start(pred[1024]{0:T(1024)(128)(4,1)S(1)} %iota_compare_fusion) | copy-start | bytes 3076
  51.6 114.3 %copy-start.84 = (f32[8,256,8]{1,2,0:T(8,128)}, f32[8,256,8]{1,2,0:T(8,128)S(1)}, u32[]{:S(2)}) copy-start(f32[8,256,8]{1,2,0:T(8,128)S(1)} %fusion.90) | copy-start | bytes 196612
  240.0 43.1 %all-to-all-start = ((bf16[8,256,384]{2,0,1:T(8,128)(2,1)}), bf16[8,256,384]{2,0,1:T(8,128)(2,1)S(1)}, u32[]{:S(2)}, u32[]{:S(2)}) async-start(bf16[8,256,384]{2,0,1:T(8,128)(2,1)} %copy.223), calls=%async_computation | async-start | bytes 3145728 | tf_op jit(solution)/shard_map/all_to_all | solution.py:344
  245.8 452.3 %copy-start.104 = (f32[384]{0:T(512)}, f32[384]{0:T(512)S(1)}, u32[]{:S(2)}) copy-start(f32[384]{0:T(512)S(1)} %convert_element_type.216) | copy-start | bytes 4612
  245.8 169.1 %copy-start.106 = (pred[64]{0:T(512)(128)(4,1)}, pred[64]{0:T(512)(128)(4,1)S(1)}, u32[]{:S(2)}) copy-start(pred[64]{0:T(512)(128)(4,1)S(1)} %broadcast_compare_fusion) | copy-start | bytes 196
  246.7 102.9 %copy-start.78 = (f32[64,32]{1,0:T(8,128)}, f32[64,32]{1,0:T(8,128)S(1)}, u32[]{:S(2)}) copy-start(f32[64,32]{1,0:T(8,128)S(1)} %get-tuple-element.163) | copy-start | bytes 24580
  322.5 92.4 %copy-start.54 = (f32[64,32,8]{0,2,1:T(8,128)}, f32[64,32,8]{0,2,1:T(8,128)S(1)}, u32[]{:S(2)}) copy-start(f32[64,32,8]{0,2,1:T(8,128)S(1)} %copy.233) | copy-start | bytes 196612
  432.8 265.3 %copy-start.80 = (f32[64,32]{1,0:T(8,128)}, f32[64,32]{1,0:T(8,128)S(1)}, u32[]{:S(2)}) copy-start(f32[64,32]{1,0:T(8,128)S(1)} %fusion.107) | copy-start | bytes 24580
  472.5 40.8 %all-to-all-start.1 = ((bf16[64,32,384]{2,1,0:T(8,128)(2,1)}), bf16[64,32,384]{2,1,0:T(8,128)(2,1)S(1)}, u32[]{:S(2)}, u32[]{:S(2)}) async-start(bf16[64,32,384]{2,1,0:T(8,128)(2,1)} %add_convert_fusion.6), calls=%async_computation.1 | async-start | bytes 3145728 | tf_op jit(solution)/shard_map/all_to_all | solution.py:351
  518.0 41.1 %all-to-all-start.2 = ((bf16[8,256,384]{2,0,1:T(8,128)(2,1)}), bf16[8,256,384]{2,0,1:T(8,128)(2,1)S(1)}, u32[]{:S(2)}, u32[]{:S(2)}) async-start(bf16[8,256,384]{2,0,1:T(8,128)(2,1)} %get-tuple-element.156), calls=%async_computation.2 | async-start | bytes 3145728 | tf_op jit(solution)/shard_map/all_to_all | solution.py:357
  702.3 40.9 %all-to-all-start.3 = ((bf16[64,32,384]{2,1,0:T(8,128)(2,1)}), bf16[64,32,384]{2,1,0:T(8,128)(2,1)S(1)}, u32[]{:S(2)}, u32[]{:S(2)}) async-start(bf16[64,32,384]{2,1,0:T(8,128)(2,1)} %fusion.44), calls=%async_computation.3 | async-start | bytes 3145728 | tf_op jit(solution)/shard_map/all_to_all | solution.py:366
  706.0 272.0 %reduce-scatter.3.cloned.1.call-start = ((), (), s32[]{:S(2)}) async-start(), calls=%async_computation.8 | async-start | bytes 10485760 | tf_op jit(solution)/shard_map/reduce_scatter | solution.py:146
  770.4 50.0 %copy-start.21 = (f32[8,256,512]{1,2,0:T(8,128)}, f32[8,256,512]{1,2,0:T(8,128)S(1)}, u32[]{:S(2)}) copy-start(f32[8,256,512]{1,2,0:T(8,128)S(1)} %get-tuple-element.188) | copy-start | bytes 12582916
  820.4 53.3 %copy-start.32 = (bf16[8,256,8,32]{1,3,2,0:T(8,128)(2,1)S(1)}, bf16[8,256,8,32]{1,3,2,0:T(8,128)(2,1)}, u32[]{:S(2)}) copy-start(bf16[8,256,8,32]{1,3,2,0:T(8,128)(2,1)} %get-tuple-element.144) | copy-start | bytes 3145732
  820.4 53.3 %copy-start.33 = (bf16[8,256,8,32]{1,3,2,0:T(8,128)(2,1)S(1)}, bf16[8,256,8,32]{1,3,2,0:T(8,128)(2,1)}, u32[]{:S(2)}) copy-start(bf16[8,256,8,32]{1,3,2,0:T(8,128)(2,1)} %get-tuple-element.145) | copy-start | bytes 3145732
  891.0 144.4 %reduce-scatter.5.cloned.1.call-start = ((), (), s32[]{:S(2)}) async-start(), calls=%async_computation.9 | async-start | bytes 10485760 | tf_op jit(solution)/shard_map/reduce_scatter | solution.py:149
  925.0 394.1 %all-reduce.4.cloned.1.call-start = ((), (), s32[]{:S(2)}) async-start(), calls=%async_computation.10 | async-start | bytes 31457280 | tf_op jit(solution)/shard_map/psum | solution.py:373
  989.2 50.1 %copy-start.11 = (bf16[8,1,256,384]{3,2,1,0:T(8,128)(2,1)S(1)}, bf16[8,1,256,384]{3,2,1,0:T(8,128)(2,1)}, u32[]{:S(2)}) copy-start(bf16[8,1,256,384]{3,2,1,0:T(8,128)(2,1)} %param.18) | copy-start | bytes 4718596
  989.2 50.1 %copy-start.70 = (f32[8,256]{1,0:T(8,128)S(1)}, f32[8,256]{1,0:T(8,128)}, u32[]{:S(2)}) copy-start(f32[8,256]{1,0:T(8,128)} %copy-done.69) | copy-start | bytes 24580
  989.2 50.1 %copy-start.96 = (f32[384]{0:T(512)S(1)}, f32[384]{0:T(512)}, u32[]{:S(2)}) copy-start(f32[384]{0:T(512)} %copy-done.95) | copy-start | bytes 4612
  (125 other events, 1185.1 us)
Sparse Core Ops, SparseCore 0:
  42.2 62.0 all-gather.4
  106.5 59.3 all-gather.2
  891.1 69.8 reduce-scatter.2
  963.6 71.7 reduce-scatter.4
  1046.5 272.5 all-reduce.3
where the time goes:
time: 1350 us; the launch traced here: 1340 us
  waiting for transfers between devices  465 us (34%)
  matrix products  411 us (30%)
  other arithmetic  227 us (17%)
  local copies, waits for them, and re-layouts  160 us (12%)
  blocking collectives  42.4 us (3%)
  starting transfers between devices  17.4 us (1%)
  between operations  16.3 us (1%)
    psum x1, waiting for transfers between devices, shards(): lax.psum((time_grads[0], time_grads[1], time_grads[2], time_grads[3], tim...  214 us
    another operation x4, other arithmetic  72.3 us
    dot_general x10, matrix products, back_dot(): lax.dot_general(gradient, weight, (((gradient.ndim - 1,), (1,)), ((), ())...  61.6 us
    dot_general x2, matrix products, block_backward(): jnp.einsum(query_form + ',' + key_form + '->bhqk', out_grad, value_rows,...  60.3 us
    convert_element_type x2, other arithmetic, block_backward(): score_grad = (soft_weights * (weight_grad - jnp.sum(soft_weights * weight...  58.8 us
    all_gather x1, waiting for transfers between devices, time_attend(): lax.all_gather(key_rows, 'batch', axis=1, tiled=True)  52.7 us
    dot_general x2, matrix products, block_forward(): jnp.einsum(query_form + ',' + key_form + '->bhqk', queries, key_rows, pre...  45.4 us
    dot_general x2, matrix products, block_backward(): jnp.einsum('bhqk,' + query_form + '->' + key_form, soft_weights.astype(jn...  44 us
  transfers between devices with their start and end apart: 9, of which 8 were waited for; matrix products, arithmetic and copies ran while one was open for 13% of the time, Pallas kernels for 0%

commit v1 on v0

--- a/solution.py
+++ b/solution.py
@@ -3,6 +3,8 @@
 import jax
 import jax.numpy as jnp
 from jax import lax
+from jax.experimental import pallas as pl
+from jax.experimental.pallas import tpu as pltpu
 from jax.sharding import PartitionSpec as P
 
 EPSILON = 1e-05
@@ -277,7 +279,7 @@
     )
 
 
-def shards(
+def generic_shards(
     activations,
     cotangent,
     frame_counts,
@@ -409,6 +411,793 @@
     )
 
 
+BLOCK = 256
+LOG2E = 1.4426950408889634
+F32 = jnp.float32
+BF16 = jnp.bfloat16
+NN = (((1,), (0,)), ((), ()))
+NT = (((1,), (1,)), ((), ()))
+TN = (((0,), (0,)), ((), ()))
+VMEM_BYTES = 60 * 2**20
+
+
+def dg(left, right, dims):
+    return lax.dot_general(left, right, dims, preferred_element_type=F32)
+
+
+def norm_forward(rows, gain):
+    scale = lax.rsqrt(jnp.mean(rows * rows, axis=0, keepdims=True) + EPSILON)
+    return (rows * scale * gain).astype(BF16)
+
+
+def norm_backward(rows, gain, grad):
+    scale = lax.rsqrt(jnp.mean(rows * rows, axis=0, keepdims=True) + EPSILON)
+    unit = rows * scale
+    scaled = grad * gain
+    inner = jnp.mean(scaled * unit, axis=0, keepdims=True)
+    return scale * (scaled - unit * inner), grad * unit
+
+
+def gelu_pair(values):
+    size = jnp.abs(values)
+    denominator = 1.0 + (0.3275911 * math.sqrt(0.5)) * size
+    t = pl.reciprocal(denominator, approx=True)
+    t = t * (2.0 - denominator * t)
+    bell = jnp.exp2(values * values * (-0.5 * LOG2E))
+    poly = 0.5 * 1.061405429
+    for coefficient in (-1.453152027, 1.421413741, -0.284496736, 0.254829592):
+        poly = poly * t + 0.5 * coefficient
+    tail = poly * t * bell
+    upper = jnp.where(values < 0.0, tail, 1.0 - tail)
+    slope = upper + values * bell * (1.0 / math.sqrt(2.0 * math.pi))
+    return values * upper, slope
+
+
+def turn(vectors, cos, sin):
+    half = cos.shape[0]
+    split = vectors.reshape(-1, 2 * half, vectors.shape[-1])
+    first = split[:, :half]
+    second = split[:, half:]
+    turned = jnp.concatenate([first * cos - second * sin, first * sin + second * cos], axis=1)
+    return turned.reshape(vectors.shape)
+
+
+def three_parts(values):
+    top = values.astype(BF16).astype(F32)
+    rest = values - top
+    middle = rest.astype(BF16).astype(F32)
+    return top, middle, rest - middle
+
+
+def extra_rows(rows, width):
+    tile = jnp.concatenate(rows + [jnp.zeros((8 - len(rows), width), F32)], axis=0)
+    return jnp.concatenate([tile, jnp.zeros((8, width), F32)], axis=0).astype(BF16)
+
+
+def project_block(normed, wpt_ref, cos, sin, inner, scale):
+    queries = turn(dg(wpt_ref[0:inner, :], normed, NN), cos, sin) * scale
+    keys = turn(dg(wpt_ref[inner : 2 * inner, :], normed, NN), cos, sin)
+    values = dg(wpt_ref[2 * inner : 3 * inner, :], normed, NN)
+    return queries.astype(BF16), keys.astype(BF16), values.astype(BF16)
+
+
+def time_forward_kernel(
+    heads,
+    x_ref,
+    bias_ref,
+    cos_ref,
+    sin_ref,
+    g1_ref,
+    g2_ref,
+    wpt_ref,
+    wgt_ref,
+    wot_ref,
+    w1t_ref,
+    w2t_ref,
+    result_ref,
+    n_ref,
+    q_ref,
+    k_ref,
+    v_ref,
+    p_ref,
+    linv_ref,
+    gate_ref,
+    att_ref,
+    mixed_ref,
+    mid_ref,
+    nf_ref,
+    act_ref,
+    slope_ref,
+    xt_ref,
+):
+    head = pl.program_id(1)
+    frames, model = x_ref.shape[1:]
+    inner = q_ref.shape[1]
+    size = inner // heads
+
+    @pl.when(head == 0)
+    def before():
+        def block(i, carry):
+            at = pl.ds(pl.multiple_of(i * BLOCK, BLOCK), BLOCK)
+            rows = x_ref[0, at, :].astype(F32).T
+            xt_ref[:, at] = rows
+            normed = norm_forward(rows, g1_ref[...])
+            n_ref[0, :, at] = normed
+            queries, keys, values = project_block(
+                normed, wpt_ref, cos_ref[:, at], sin_ref[:, at], inner, LOG2E * size**-0.5
+            )
+            q_ref[0, :, at] = queries
+            k_ref[0, :, at] = keys
+            v_ref[0, :, at] = values
+            gate_ref[0, :, at] = dg(wgt_ref[...], normed, NN)
+            return carry
+
+        lax.fori_loop(0, frames // BLOCK, block, 0)
+
+    at_head = pl.ds(pl.multiple_of(head * size, size), size)
+    ones = jnp.ones((1, frames), F32)
+    queries = jnp.concatenate([q_ref[0, at_head, :], extra_rows([ones], frames)], axis=0)
+    keys = jnp.concatenate([k_ref[0, at_head, :], extra_rows([bias_ref[...]], frames)], axis=0)
+    values = jnp.concatenate([v_ref[0, at_head, :], extra_rows([ones], frames)], axis=0)
+    scores = dg(keys, queries, TN)
+    weights = jnp.exp2(scores - jnp.max(scores, axis=0, keepdims=True)).astype(BF16)
+    p_ref[0, 0] = weights
+    sums = dg(values, weights, NN)
+    inverse = 1.0 / sums[size : size + 1]
+    attended = sums[:size] * inverse
+    linv_ref[0, pl.ds(head, 1), :] = inverse
+    att_ref[0, at_head, :] = attended
+    gate = jax.nn.sigmoid(gate_ref[0, pl.ds(head, 1), :])
+    mixed_ref[0, at_head, :] = (attended * gate).astype(BF16)
+
+    @pl.when(head == heads - 1)
+    def after():
+        def block(i, carry):
+            at = pl.ds(pl.multiple_of(i * BLOCK, BLOCK), BLOCK)
+            middle = xt_ref[:, at] + dg(wot_ref[...], mixed_ref[0, :, at], NN)
+            mid_ref[0, :, at] = middle
+            normed = norm_forward(middle, g2_ref[...])
+            nf_ref[0, :, at] = normed
+            active, slope = gelu_pair(dg(w1t_ref[...], normed, NN))
+            active = active.astype(BF16)
+            act_ref[0, :, at] = active
+            slope_ref[0, :, at] = slope.astype(BF16)
+            result = middle + dg(w2t_ref[...], active, NN)
+            result_ref[0, at, :] = result.T.astype(BF16)
+            return carry
+
+        lax.fori_loop(0, frames // BLOCK, block, 0)
+
+
+def whole_spec(array):
+    nd = array.ndim
+    return pl.BlockSpec(array.shape, lambda *ids: (0,) * nd, pipeline_mode=pl.Buffered(1))
+
+
+def time_forward(rows, bias, cos, sin, g1, g2, wpt, wgt, wot, w1t, w2t):
+    slots, frames, model = rows.shape
+    heads = wgt.shape[0]
+    inner = wot.shape[1]
+    hidden = w1t.shape[0]
+
+    def per_slot(*shape):
+        return pl.BlockSpec((1,) + shape, lambda s, h: (s,) + (0,) * len(shape))
+
+    outs = [
+        ((frames, model), BF16),
+        ((model, frames), BF16),
+        ((inner, frames), BF16),
+        ((inner, frames), BF16),
+        ((inner, frames), BF16),
+        None,
+        ((heads, frames), F32),
+        ((heads, frames), F32),
+        ((inner, frames), F32),
+        ((inner, frames), BF16),
+        ((model, frames), F32),
+        ((model, frames), BF16),
+        ((hidden, frames), BF16),
+        ((hidden, frames), BF16),
+    ]
+    shapes, specs = [], []
+    for entry in outs:
+        if entry is None:
+            shapes.append(jax.ShapeDtypeStruct((slots, heads, frames, frames), BF16))
+            specs.append(pl.BlockSpec((1, 1, frames, frames), lambda s, h: (s, h, 0, 0)))
+        else:
+            shapes.append(jax.ShapeDtypeStruct((slots,) + entry[0], entry[1]))
+            specs.append(per_slot(*entry[0]))
+    consts = (bias, cos, sin, g1, g2, wpt, wgt, wot, w1t, w2t)
+    return pl.pallas_call(
+        lambda *refs: time_forward_kernel(heads, *refs),
+        grid=(slots, heads),
+        out_shape=shapes,
+        in_specs=[per_slot(frames, model)] + [whole_spec(c) for c in consts],
+        out_specs=specs,
+        scratch_shapes=[pltpu.VMEM((model, frames), F32)],
+        compiler_params=pltpu.CompilerParams(vmem_limit_bytes=VMEM_BYTES),
+        name="time_forward",
+    )(rows, *consts)
+
+
+def ffn_backward(grad, act, slope, normed, middle, gain, w1_ref, w2_ref, dw1_ref, dw2t_ref, dg2_ref):
+    branch = grad.astype(BF16)
+    d_hidden = (dg(w2_ref[...], branch, NN) * slope.astype(F32)).astype(BF16)
+    dw2t_ref[...] += dg(branch, act, NT)
+    dw1_ref[...] += dg(normed, d_hidden, NT)
+    d_normed = dg(w1_ref[...], d_hidden, NN)
+    d_rows, terms = norm_backward(middle, gain, d_normed)
+    dg2_ref[...] += jnp.sum(terms, axis=1, keepdims=True)
+    return grad + d_rows
+
+
+def head_backward(d_mixed, attended, gate_logit, inverse):
+    gate = jax.nn.sigmoid(gate_logit)
+    d_logit = jnp.sum(d_mixed * attended, axis=0, keepdims=True) * gate * (1.0 - gate)
+    d_att = (d_mixed * (gate * inverse)).astype(BF16)
+    minus = -jnp.sum(d_att.astype(F32) * attended, axis=0, keepdims=True)
+    return d_att, minus, d_logit
+
+
+def scores_backward(queries, keys, values, weights, d_att, minus, cos, sin, scale):
+    width = queries.shape[1]
+    ones = jnp.ones((1, width), F32)
+    d_weights = dg(
+        jnp.concatenate([values, extra_rows([ones, ones, ones], width)], axis=0),
+        jnp.concatenate([d_att, extra_rows(list(three_parts(minus)), width)], axis=0),
+        TN,
+    )
+    d_scores = (weights.astype(F32) * d_weights).astype(BF16)
+    d_values = dg(d_att, weights, NT)
+    d_queries = dg(keys, d_scores, NN) * scale
+    d_keys = dg(queries, d_scores, NT) * (1.0 / LOG2E)
+    return turn(d_queries, cos, -sin), turn(d_keys, cos, -sin), d_values
+
+
+def time_ffn_backward_kernel(
+    heads,
+    grad_ref,
+    act_ref,
+    slope_ref,
+    nf_ref,
+    mid_ref,
+    mixed_ref,
+    att_ref,
+    gate_ref,
+    linv_ref,
+    g2_ref,
+    w1_ref,
+    w2_ref,
+    wo_ref,
+    dmid_ref,
+    datt_ref,
+    minus_ref,
+    dlogit_ref,
+    sums_ref,
+    dw1_ref,
+    dw2t_ref,
+    dwot_ref,
+    dg2_ref,
+):
+    step = pl.program_id(0) * pl.num_programs(1) + pl.program_id(1)
+    last = pl.num_programs(0) * pl.num_programs(1) - 1
+    size = wo_ref.shape[0] // heads
+
+    @pl.when(step == 0)
+    def clear():
+        for ref in (dw1_ref, dw2t_ref, dwot_ref, dg2_ref):
+            ref[...] = jnp.zeros_like(ref)
+
+    grad = grad_ref[0].astype(F32).T
+    d_middle = ffn_backward(
+        grad, act_ref[0], slope_ref[0], nf_ref[0], mid_ref[0], g2_ref[...], w1_ref, w2_ref, dw1_ref, dw2t_ref, dg2_ref
+    )
+    dmid_ref[0] = d_middle
+    branch = d_middle.astype(BF16)
+    dwot_ref[...] += dg(branch, mixed_ref[0], NT)
+    d_mixed = dg(wo_ref[...], branch, NN)
+    logits, minuses = [], []
+    for head in range(heads):
+        at = slice(head * size, (head + 1) * size)
+        d_att, minus, d_logit = head_backward(
+            d_mixed[at], att_ref[0, at], gate_ref[0, head : head + 1], linv_ref[0, head : head + 1]
+        )
+        datt_ref[0, at] = d_att
+        minuses.append(minus)
+        logits.append(d_logit)
+    minus_ref[0] = jnp.concatenate(minuses, axis=0)
+    dlogit_ref[0] = jnp.concatenate(logits, axis=0)
+
+    @pl.when(step == last)
+    def finish():
+        pack_sums(sums_ref, (dw1_ref, dw2t_ref, dwot_ref, dg2_ref))
+
+
+def pack_sums(sums_ref, parts):
+    at = 0
+    narrow = []
+    for ref in parts:
+        width = ref.shape[1]
+        if width % 128 == 0:
+            sums_ref[:, at : at + width] = ref[...].astype(BF16)
+            at += width
+        else:
+            narrow.append(ref[...])
+    used = sum(part.shape[1] for part in narrow)
+    narrow.append(jnp.zeros((sums_ref.shape[0], 128 - used), F32))
+    sums_ref[:, at : at + 128] = jnp.concatenate(narrow, axis=1).astype(BF16)
+
+
+def time_ffn_backward(grad, act, slope, nf, mid, mixed, att, gate, linv, g2, w1, w2, wo):
+    slots, frames, model = grad.shape
+    heads = gate.shape[1]
+    inner, hidden = wo.shape[0], w1.shape[1]
+    tokens = min(frames, 512)
+
+    def cut(rows):
+        return pl.BlockSpec((1, rows, tokens), lambda s, c: (s, 0, c))
+
+    consts = (g2, w1, w2, wo)
+    width = 2 * hidden + inner + 128
+    return pl.pallas_call(
+        lambda *refs: time_ffn_backward_kernel(heads, *refs),
+        grid=(slots, frames // tokens),
+        out_shape=[
+            jax.ShapeDtypeStruct((slots, model, frames), F32),
+            jax.ShapeDtypeStruct((slots, inner, frames), BF16),
+            jax.ShapeDtypeStruct((slots, heads, frames), F32),
+            jax.ShapeDtypeStruct((slots, heads, frames), F32),
+            jax.ShapeDtypeStruct((model, width), BF16),
+        ],
+        in_specs=[pl.BlockSpec((1, tokens, model), lambda s, c: (s, c, 0))]
+        + [cut(a.shape[1]) for a in (act, slope, nf, mid, mixed, att, gate, linv)]
+        + [whole_spec(c) for c in consts],
+        out_specs=[cut(model), cut(inner), cut(heads), cut(heads), pl.BlockSpec((model, width), lambda s, c: (0, 0))],
+        scratch_shapes=[
+            pltpu.VMEM((model, hidden), F32),
+            pltpu.VMEM((model, hidden), F32),
+            pltpu.VMEM((model, inner), F32),
+            pltpu.VMEM((model, 1), F32),
+        ],
+        compiler_params=pltpu.CompilerParams(vmem_limit_bytes=VMEM_BYTES),
+        name="time_ffn_backward",
+    )(grad, act, slope, nf, mid, mixed, att, gate, linv, *consts)
+
+
+def time_attention_backward_kernel(
+    heads,
+    p_ref,
+    q_ref,
+    k_ref,
+    v_ref,
+    datt_ref,
+    minus_ref,
+    dlogit_ref,
+    n_ref,
+    x_ref,
+    dmid_ref,
+    cos_ref,
+    sin_ref,
+    g1_ref,
+    wp_ref,
+    wg_ref,
+    out_ref,
+    sums_ref,
+    dproj_ref,
+    dwp_ref,
+    dwg_ref,
+    dg1_ref,
+):
+    slot, head = pl.program_id(0), pl.program_id(1)
+    inner = q_ref.shape[1]
+    size = inner // heads
+    frames = q_ref.shape[2]
+
+    @pl.when((slot == 0) & (head == 0))
+    def clear():
+        for ref in (dwp_ref, dwg_ref, dg1_ref):
+            ref[...] = jnp.zeros_like(ref)
+
+    start = pl.multiple_of(head * size, size)
+    at = pl.ds(start, size)
+    d_queries, d_keys, d_values = scores_backward(
+        q_ref[0, at, :],
+        k_ref[0, at, :],
+        v_ref[0, at, :],
+        p_ref[0, 0],
+        datt_ref[0, at, :],
+        minus_ref[0, pl.ds(head, 1), :],
+        cos_ref[...],
+        sin_ref[...],
+        size**-0.5,
+    )
+    dproj_ref[at, :] = d_queries.astype(BF16)
+    dproj_ref[pl.ds(inner + start, size), :] = d_keys.astype(BF16)
+    dproj_ref[pl.ds(2 * inner + start, size), :] = d_values.astype(BF16)
+
+    @pl.when(head == heads - 1)
+    def after():
+        d_logit = jnp.concatenate([dlogit_ref[0], jnp.zeros_like(dlogit_ref[0])], axis=0).astype(BF16)
+        dwp_ref[...] += dg(n_ref[0], dproj_ref[...], NT)
+        dwg_ref[...] += dg(n_ref[0], d_logit, NT)[:, :heads]
+
+        def block(i, carry):
+            at = pl.ds(pl.multiple_of(i * BLOCK, BLOCK), BLOCK)
+            logit = dlogit_ref[0, :, at].astype(BF16)
+            d_normed = dg(wp_ref[...], dproj_ref[:, at], NN) + dg(wg_ref[...], logit, NN)
+            d_rows, terms = norm_backward(x_ref[0, at, :].astype(F32).T, g1_ref[...], d_normed)
+            dg1_ref[...] += jnp.sum(terms, axis=1, keepdims=True)
+            out_ref[0, at, :] = (dmid_ref[0, :, at] + d_rows).T.astype(BF16)
+            return carry
+
+        lax.fori_loop(0, frames // BLOCK, block, 0)
+
+    @pl.when((slot == pl.num_programs(0) - 1) & (head == heads - 1))
+    def finish():
+        pack_sums(sums_ref, (dwp_ref, dwg_ref, dg1_ref))
+
+
+def time_attention_backward(p, q, k, v, datt, minus, dlogit, n, x, dmid, cos, sin, g1, wp, wg):
+    slots, inner, frames = q.shape
+    heads = minus.shape[1]
+    model = n.shape[1]
+
+    def per_slot(array):
+        return pl.BlockSpec((1,) + array.shape[1:], lambda s, h: (s, 0, 0))
+
+    consts = (cos, sin, g1, wp, wg)
+    width = 3 * inner + 128
+    return pl.pallas_call(
+        lambda *refs: time_attention_backward_kernel(heads, *refs),
+        grid=(slots, heads),
+        out_shape=[
+            jax.ShapeDtypeStruct((slots, frames, model), BF16),
+            jax.ShapeDtypeStruct((model, width), BF16),
+        ],
+        in_specs=[pl.BlockSpec((1, 1, frames, frames), lambda s, h: (s, h, 0, 0))]
+        + [per_slot(a) for a in (q, k, v, datt, minus, dlogit, n, x, dmid)]
+        + [whole_spec(c) for c in consts],
+        out_specs=[
+            pl.BlockSpec((1, frames, model), lambda s, h: (s, 0, 0)),
+            pl.BlockSpec((model, width), lambda s, h: (0, 0)),
+        ],
+        scratch_shapes=[
+            pltpu.VMEM((3 * inner, frames), BF16),
+            pltpu.VMEM((model, 3 * inner), F32),
+            pltpu.VMEM((model, heads), F32),
+            pltpu.VMEM((model, 1), F32),
+        ],
+        compiler_params=pltpu.CompilerParams(vmem_limit_bytes=VMEM_BYTES),
+        name="time_attention_backward",
+    )(p, q, k, v, datt, minus, dlogit, n, x, dmid, *consts)
+
+
+def band_kernel(
+    heads,
+    x_ref,
+    cot_ref,
+    mask_ref,
+    bias_ref,
+    cos_ref,
+    sin_ref,
+    g1_ref,
+    g2_ref,
+    wpt_ref,
+    wgt_ref,
+    wot_ref,
+    w1t_ref,
+    w2t_ref,
+    wp_ref,
+    wg_ref,
+    wo_ref,
+    w1_ref,
+    w2_ref,
+    y_ref,
+    dx_ref,
+    sums_ref,
+    q_ref,
+    k_ref,
+    v_ref,
+    p_ref,
+    gate_ref,
+    linv_ref,
+    att_ref,
+    mixed_ref,
+    act_ref,
+    slope_ref,
+    datt_ref,
+    dmixed_ref,
+    dlogit_ref,
+    dproj_ref,
+    dwp_ref,
+    dw1_ref,
+    dw2t_ref,
+    dwot_ref,
+    dwg_ref,
+    dg1_ref,
+    dg2_ref,
+):
+    step = pl.program_id(0)
+    tokens, model = x_ref.shape
+    inner = q_ref.shape[0]
+    size = inner // heads
+    groups = tokens // BLOCK
+
+    @pl.when(step == 0)
+    def clear():
+        for ref in (dwp_ref, dw1_ref, dw2t_ref, dwot_ref, dwg_ref, dg1_ref, dg2_ref):
+            ref[...] = jnp.zeros_like(ref)
+
+    rows = x_ref[...].astype(F32).T
+    normed = norm_forward(rows, g1_ref[...])
+    q_ref[...], k_ref[...], v_ref[...] = project_block(
+        normed, wpt_ref, cos_ref[...], sin_ref[...], inner, LOG2E * size**-0.5
+    )
+    gate_ref[...] = dg(wgt_ref[...], normed, NN)
+    ones = extra_rows([jnp.ones((1, BLOCK), F32)], BLOCK)
+
+    def attend(head, carry):
+        at = pl.ds(pl.multiple_of(head * size, size), size)
+        row = pl.ds(head, 1)
+        for group in range(groups):
+            lanes = slice(group * BLOCK, (group + 1) * BLOCK)
+            scores = dg(k_ref[at, lanes], q_ref[at, lanes], TN) + bias_ref[...]
+            weights = jnp.exp2(scores - jnp.max(scores, axis=0, keepdims=True)).astype(BF16)
+            p_ref[head * groups + group] = weights
+            sums = dg(jnp.concatenate([v_ref[at, lanes], ones], axis=0), weights, NN)
+            inverse = 1.0 / sums[size : size + 1]
+            attended = sums[:size] * inverse
+            linv_ref[row, lanes] = inverse
+            att_ref[at, lanes] = attended
+            gate = jax.nn.sigmoid(gate_ref[row, lanes])
+            mixed_ref[at, lanes] = (attended * gate).astype(BF16)
+        return carry
+
+    lax.fori_loop(0, heads, attend, 0)
+    middle = rows + dg(wot_ref[...], mixed_ref[...], NN)
+    normed_ffn = norm_forward(middle, g2_ref[...])
+
+    hidden = w1t_ref.shape[0]
+    part = hidden // 4
+
+    def expand(i, carry):
+        at = pl.ds(pl.multiple_of(i * part, part), part)
+        active, slope = gelu_pair(dg(w1t_ref[at, :], normed_ffn, NN))
+        act_ref[at, :] = active.astype(BF16)
+        slope_ref[at, :] = slope.astype(BF16)
+        return carry
+
+    lax.fori_loop(0, 4, expand, 0)
+    mask = mask_ref[0]
+    result = (middle + dg(w2t_ref[...], act_ref[...], NN)) * mask
+    y_ref[...] = result.T.astype(BF16)
+
+    grad = cot_ref[...].astype(F32).T * mask
+    d_middle = ffn_backward(
+        grad, act_ref[...], slope_ref[...], normed_ffn, middle, g2_ref[...], w1_ref, w2_ref, dw1_ref, dw2t_ref, dg2_ref
+    )
+    branch = d_middle.astype(BF16)
+    dwot_ref[...] += dg(branch, mixed_ref[...], NT)
+    dmixed_ref[...] = dg(wo_ref[...], branch, NN)
+
+    def attend_back(head, carry):
+        start = pl.multiple_of(head * size, size)
+        at = pl.ds(start, size)
+        row = pl.ds(head, 1)
+        d_att, minus, d_logit = head_backward(dmixed_ref[at, :], att_ref[at, :], gate_ref[row, :], linv_ref[row, :])
+        dlogit_ref[row, :] = d_logit
+        for group in range(groups):
+            lanes = slice(group * BLOCK, (group + 1) * BLOCK)
+            d_queries, d_keys, d_values = scores_backward(
+                q_ref[at, lanes],
+                k_ref[at, lanes],
+                v_ref[at, lanes],
+                p_ref[head * groups + group],
+                d_att[:, lanes],
+                minus[:, lanes],
+                cos_ref[:, lanes],
+                sin_ref[:, lanes],
+                size**-0.5,
+            )
+            dproj_ref[at, lanes] = d_queries.astype(BF16)
+            dproj_ref[pl.ds(inner + start, size), lanes] = d_keys.astype(BF16)
+            dproj_ref[pl.ds(2 * inner + start, size), lanes] = d_values.astype(BF16)
+        return carry
+
+    lax.fori_loop(0, heads, attend_back, 0)
+    d_logit = jnp.concatenate([dlogit_ref[...], jnp.zeros_like(dlogit_ref)], axis=0).astype(BF16)
+    dwp_ref[...] += dg(normed, dproj_ref[...], NT)
+    dwg_ref[...] += dg(normed, d_logit, NT)[:, :heads]
+    d_normed = dg(wp_ref[...], dproj_ref[...], NN) + dg(wg_ref[...], dlogit_ref[...].astype(BF16), NN)
+    d_rows, terms = norm_backward(rows, g1_ref[...], d_normed)
+    dg1_ref[...] += jnp.sum(terms, axis=1, keepdims=True)
+    dx_ref[...] = (d_middle + d_rows).T.astype(BF16)
+
+    @pl.when(step == pl.num_programs(0) - 1)
+    def finish():
+        pack_sums(sums_ref, (dwp_ref, dw1_ref, dw2t_ref, dwot_ref, dwg_ref, dg1_ref, dg2_ref))
+
+
+def band_layer(x, cot, mask, bias, cos, sin, params, turned):
+    prenorm, project, gating, output_weight, midnorm, expand, shrink = params
+    wpt, wgt, wot, w1t, w2t, g1, g2 = turned
+    total, model = x.shape
+    steps, _, tokens = mask.shape
+    heads, inner, hidden = gating.shape[1], output_weight.shape[0], expand.shape[1]
+    groups = tokens // BLOCK
+    consts = (bias, cos, sin, g1, g2, wpt, wgt, wot, w1t, w2t, project, gating, output_weight, expand, shrink)
+    width = 3 * inner + 2 * hidden + inner + 128
+    rows = pl.BlockSpec((tokens, model), lambda i: (i, 0))
+    return pl.pallas_call(
+        lambda *refs: band_kernel(heads, *refs),
+        grid=(steps,),
+        out_shape=[
+            jax.ShapeDtypeStruct((total, model), BF16),
+            jax.ShapeDtypeStruct((total, model), BF16),
+            jax.ShapeDtypeStruct((model, width), BF16),
+        ],
+        in_specs=[rows, rows, pl.BlockSpec((1, 1, tokens), lambda i: (i, 0, 0))] + [whole_spec(c) for c in consts],
+        out_specs=[rows, rows, pl.BlockSpec((model, width), lambda i: (0, 0))],
+        scratch_shapes=[
+            pltpu.VMEM((inner, tokens), BF16),
+            pltpu.VMEM((inner, tokens), BF16),
+            pltpu.VMEM((inner, tokens), BF16),
+            pltpu.VMEM((heads * groups, BLOCK, BLOCK), BF16),
+            pltpu.VMEM((heads, tokens), F32),
+            pltpu.VMEM((heads, tokens), F32),
+            pltpu.VMEM((inner, tokens), F32),
+            pltpu.VMEM((inner, tokens), BF16),
+            pltpu.VMEM((hidden, tokens), BF16),
+            pltpu.VMEM((hidden, tokens), BF16),
+            pltpu.VMEM((inner, tokens), BF16),
+            pltpu.VMEM((inner, tokens), F32),
+            pltpu.VMEM((heads, tokens), F32),
+            pltpu.VMEM((3 * inner, tokens), BF16),
+            pltpu.VMEM((model, 3 * inner), F32),
+            pltpu.VMEM((model, hidden), F32),
+            pltpu.VMEM((model, hidden), F32),
+            pltpu.VMEM((model, inner), F32),
+            pltpu.VMEM((model, heads), F32),
+            pltpu.VMEM((model, 1), F32),
+            pltpu.VMEM((model, 1), F32),
+        ],
+        compiler_params=pltpu.CompilerParams(vmem_limit_bytes=VMEM_BYTES),
+        name="band_layer",
+    )(x, cot, mask, *consts)
+
+
+def turned_params(params):
+    prenorm, project, gating, output_weight, midnorm, expand, shrink = params
+    return (
+        project.T,
+        gating.T,
+        output_weight.T,
+        expand.T,
+        shrink.T,
+        prenorm.astype(F32)[:, None],
+        midnorm.astype(F32)[:, None],
+    )
+
+
+def slot_shards(activations, cotangent, frame_counts, slot_bands, *weights):
+    slot_dev, _, frame_dev, model = activations.shape
+    slot_count = slot_bands.shape[0]
+    batch, band = lax.axis_size("batch"), lax.axis_size("band")
+    frames = frame_dev * batch
+    piece = frame_dev // band
+    slots = slot_dev // batch
+    time_params, band_params = weights[:7], weights[7:]
+    heads, inner, hidden = time_params[2].shape[1], time_params[3].shape[0], time_params[5].shape[1]
+    size = inner // heads
+
+    positions = jnp.arange(frames, dtype=jnp.int32)
+    time_cos, time_sin = rotary_tables(positions.astype(F32), size)
+    time_bias = jnp.where(positions[None, :] < frame_counts[:, None], 0.0, NEG_FILL).astype(F32)
+    band_cos, band_sin = rotary_tables(jnp.maximum(slot_bands, 0).astype(F32), size)
+    tokens = min(2 * BLOCK, piece * slot_count)
+    copies = tokens // slot_count
+    slot_valid = slot_bands >= 0
+    index = jnp.arange(BLOCK, dtype=jnp.int32)
+    together = (index[:, None] // slot_count == index[None, :] // slot_count) & jnp.tile(
+        slot_valid, BLOCK // slot_count
+    )[:, None]
+    band_bias = jnp.where(together, 0.0, NEG_FILL).astype(F32)
+    own_start = lax.axis_index("batch") * frame_dev + lax.axis_index("band") * piece
+    own_frames = own_start + jnp.arange(piece, dtype=jnp.int32)
+    mask = ((own_frames < frame_counts[0])[:, None] & slot_valid[None, :]).astype(F32)
+    mask = mask.reshape(piece * slot_count // tokens, 1, tokens)
+
+    time_turned = turned_params(time_params)
+    band_turned = turned_params(band_params)
+    rows = lax.all_to_all(
+        activations.reshape(slot_dev, frame_dev, model), "batch", split_axis=0, concat_axis=1, tiled=True
+    )
+    cot_rows = lax.all_to_all(
+        cotangent.reshape(slot_dev, frame_dev, model), "band", split_axis=1, concat_axis=0, tiled=True
+    )
+    cot_rows = cot_rows.transpose(1, 0, 2).reshape(piece * slot_count, model)
+    wpt, wgt, wot, w1t, w2t, g1, g2 = time_turned
+    result, n, q, k, v, p, linv, gate, att, mixed, mid, nf, act, slope = time_forward(
+        rows, time_bias, time_cos.T, time_sin.T, g1, g2, wpt, wgt, wot, w1t, w2t
+    )
+    result = result.reshape(slots, batch, band, piece, model).transpose(0, 2, 1, 3, 4)
+    frame_rows = lax.all_to_all(
+        result.reshape(slots, frames, model), ("band", "batch"), split_axis=1, concat_axis=0, tiled=True
+    )
+    frame_rows = frame_rows.transpose(1, 0, 2).reshape(piece * slot_count, model)
+    y, dx, band_sums = band_layer(
+        frame_rows,
+        cot_rows,
+        mask,
+        band_bias,
+        jnp.tile(band_cos.T, (1, copies)),
+        jnp.tile(band_sin.T, (1, copies)),
+        band_params,
+        band_turned,
+    )
+    band_sums = lax.psum(band_sums, ("band", "batch"))
+    dx = dx.reshape(piece, slot_count, model).transpose(1, 0, 2)
+    slot_grad = lax.all_to_all(dx, ("band", "batch"), split_axis=0, concat_axis=1, tiled=True)
+    slot_grad = slot_grad.reshape(slots, band, batch, piece, model).transpose(0, 2, 1, 3, 4)
+    slot_grad = slot_grad.reshape(slots, frames, model)
+    y = y.reshape(piece, slot_count, model).transpose(1, 0, 2)
+    layer_output = lax.all_to_all(y, "band", split_axis=0, concat_axis=1, tiled=True)
+    dmid, datt, minus, dlogit, ffn_sums = time_ffn_backward(
+        slot_grad, act, slope, nf, mid, mixed, att, gate, linv, g2, time_params[5], time_params[6], time_params[3]
+    )
+    ffn_sums = lax.psum(ffn_sums, ("band", "batch"))
+    grads, attn_sums = time_attention_backward(
+        p, q, k, v, datt, minus, dlogit, n, rows, dmid, time_cos.T, time_sin.T, g1, time_params[1], time_params[2]
+    )
+    input_grad = lax.all_to_all(grads, "batch", split_axis=1, concat_axis=0, tiled=True)
+    attn_sums = lax.psum(attn_sums, ("band", "batch"))
+
+    def cut(sums, widths):
+        parts, at = [], 0
+        for width in widths:
+            parts.append(sums[:, at : at + width].astype(F32))
+            at += width
+        return parts
+
+    dwp, dwg, dg1 = cut(attn_sums, (3 * inner, heads, 1))
+    dw1, dw2t, dwot, dg2 = cut(ffn_sums, (hidden, hidden, inner, 1))
+    bwp, bw1, bw2t, bwot, bwg, bg1, bg2 = cut(band_sums, (3 * inner, hidden, hidden, inner, heads, 1, 1))
+    return (
+        layer_output.reshape(activations.shape),
+        input_grad.astype(F32).reshape(activations.shape),
+        dg1[:, 0],
+        dwp,
+        dwg,
+        dwot.T,
+        dg2[:, 0],
+        dw1,
+        dw2t.T,
+        bg1[:, 0],
+        bwp,
+        bwg,
+        bwot.T,
+        bg2[:, 0],
+        bw1,
+        bw2t.T,
+    )
+
+
+def shards(activations, cotangent, frame_counts, slot_bands, *weights):
+    slot_dev, clips, frame_dev, _ = activations.shape
+    batch, band = lax.axis_size("batch"), lax.axis_size("band")
+    fits = (
+        clips == 1
+        and slot_dev % batch == 0
+        and frame_dev % band == 0
+        and (frame_dev * batch) % (2 * BLOCK) == 0
+        and BLOCK % slot_bands.shape[0] == 0
+        and (frame_dev // band * slot_bands.shape[0]) % (2 * BLOCK) == 0
+        and weights[2].shape[1] == 8
+    )
+    form = slot_shards if fits else generic_shards
+    return form(activations, cotangent, frame_counts, slot_bands, *weights)
+
+
 def solution(mesh):
     return jax.shard_map(
         shards,

time: 1350 us -> 619 us (0.46)
  matrix products: 411 us -> 0 us
  Pallas kernels: 0 us -> 245 us
  waiting for transfers between devices: 465 us -> 241 us
  other arithmetic: 227 us -> 20.6 us
  local copies, waits for them, and re-layouts: 160 us -> 60.9 us
  blocking collectives: 42.4 us -> 0 us
    dot_general x42 -> x0, matrix products: 411 us -> none  [the longest x10 61.6 us: back_dot(): lax.dot_general(gradient, weight, (((gradient.ndim - 1,), (1,)), ((), ())...]
    pallas_call x0 -> x4, Pallas kernels: none -> 245 us  [the longest x1 97.2 us: band_layer(): pl.pallas_call(lambda *refs: band_kernel(heads, *refs), grid=(steps,), ou...]
    convert_element_type x15 -> x6, other arithmetic: 97.4 us -> 4.97 us  [the longest x2 2.62 us: cut(): parts.append(sums[:, at:at + width].astype(F32))]
    psum x1, waiting for transfers between devices: 214 us -> 135 us  [slot_shards(): attn_sums = lax.psum(attn_sums, ('band', 'batch'))]
    another operation x4 -> x0, other arithmetic: 72.3 us -> none
    all_gather x2 -> x0, waiting for transfers between devices: 61.9 us -> none  [the longest x1 52.7 us: time_attend(): lax.all_gather(key_rows, 'batch', axis=1, tiled=True)]
    slice x8 -> x0, local copies, waits for them, and re-layouts: 56.8 us -> none  [the longest x1 27.1 us: rotate(): first = vectors[..., :half_size]]
    psum x1 -> x0, blocking collectives: 42.4 us -> none  [shards(): lax.psum((time_grads[0], time_grads[1], time_grads[2], time_grads[3], tim...]
  transfers between devices with their start and end apart: 9 -> 7, of which waited for: 8 -> 5; matrix products, arithmetic and copies ran while one was open for 13% -> 8% of each run, Pallas kernels for 0% -> 24%
where the time goes in v1:
time: 619 us; the launch traced here: 611 us
  Pallas kernels  245 us (40%)
  waiting for transfers between devices  241 us (39%)
  local copies, waits for them, and re-layouts  60.9 us (10%)
  starting transfers between devices  27.7 us (4%)
  other arithmetic  20.6 us (3%)
  between operations  15.3 us (2%)
    psum x1, waiting for transfers between devices, slot_shards(): attn_sums = lax.psum(attn_sums, ('band', 'batch'))  135 us
    pallas_call x1, Pallas kernels, band_layer(): pl.pallas_call(lambda *refs: band_kernel(heads, *refs), grid=(steps,), ou...  97.2 us
    pallas_call x1, Pallas kernels, time_forward(): pl.pallas_call(lambda *refs: time_forward_kernel(heads, *refs), grid=(slo...  70.6 us
    pallas_call x1, Pallas kernels, time_attention_backward(): pl.pallas_call(lambda *refs: time_attention_backward_kernel(heads, *refs)...  54.1 us
    all_to_all x1, waiting for transfers between devices, slot_shards(): lax.all_to_all(dx, ('band', 'batch'), split_axis=0, concat_axis=1, tiled=...  35.6 us
    all_to_all x1, waiting for transfers between devices, slot_shards(): lax.all_to_all(grads, 'batch', split_axis=1, concat_axis=0, tiled=True)  33.4 us
    unnamed x39, local copies, waits for them, and re-layouts  31.2 us
    pallas_call x1, Pallas kernels, time_ffn_backward(): pl.pallas_call(lambda *refs: time_ffn_backward_kernel(heads, *refs), grid...  23.1 us
  transfers between devices with their start and end apart: 7, of which 5 were waited for; matrix products, arithmetic and copies ran while one was open for 8% of the time, Pallas kernels for 24%

profile of v1, /device:TPU:0, one launch (start us, length us, event | category | flops | bytes accessed | tf_op | source)
XLA Modules:
  0.0 610.5 jit_solution(8470285480059682609)
XLA Ops:
  7.2 4.4 all-to-all-start
  13.6 18.0 %all-to-all-done = bf16[8,256,384]{2,1,0:T(8,128)(2,1)S(1)} async-done(((bf16[8,256,384]{2,1,0:T(8,128)(2,1)}), bf16[8,256,384]{2,1,0:T(8,128)(2,1)S(1)}, u32[]{:S(2)}, u32[]{:S(2)}) %all-to-all-start) | async-done | bytes 1572896 | tf_op jit(solution)/shard_map/all_to_all | solution.py:1112
  31.6 6.7 %all-to-all-start.2 = ((bf16[8,256,384]{2,0,1:T(8,128)(2,1)}), bf16[8,256,384]{2,0,1:T(8,128)(2,1)S(1)}, u32[]{:S(2)}, u32[]{:S(2)}) async-start(bf16[8,256,384]{2,0,1:T(8,128)(2,1)} %bitcast.70), calls=%async_computation.2 | async-start | bytes 3145728 | tf_op jit(solution)/shard_map/all_to_all | solution.py:1115
  43.0 2.4 copy.119
  45.4 2.5 copy.120
  52.0 70.6 %time_forward.1 = (bf16[2,1024,384]{2,1,0:T(8,128)(2,1)}, bf16[2,384,1024]{2,1,0:T(8,128)(2,1)}, bf16[2,512,1024]{2,1,0:T(8,128)(2,1)}, bf16[2,512,1024]{2,1,0:T...) custom-call(bf16[2,1024,384]{2,1,0:T(8,128)(2,1)} %bitcast.73, ...), custom_call_target="tpu_custom_call" | custom-call | tf_op jit(solution)/shard_map/time_forward/pallas_call | solution.py:611
  124.3 2.8 copy.124
  127.0 5.3 all-to-all-start.1
  135.3 2.4 copy.131
  140.1 2.5 copy.134
  151.4 18.6 %all-to-all-done.1 = bf16[2,1024,384]{2,0,1:T(2,128)(2,1)S(1)} async-done(((bf16[2,1024,384]{2,0,1:T(2,128)(2,1)}), bf16[2,1024,384]{2,0,1:T(2,128)(2,1)S(1)}, u32[]{:S(2)}, u32[]{:S(2)}) %all-to-all-start.1) | async-done | bytes 1572896 | tf_op jit(solution)/shard_map/all_to_all | solution.py:1124
  172.2 97.2 %band_layer.1 = (bf16[2048,384]{1,0:T(8,128)(2,1)}, bf16[2048,384]{1,0:T(8,128)(2,1)}, bf16[384,5248]{1,0:T(8,128)(2,1)}) custom-call(bf16[2048,384]{1,0:T(8,128)(2,1)} %bitcast.85, bf16[2048,384]{1,0:T(8,128)(2,1)} %bitcast.84, f32[4,1,512]{2,1,0:T(1,128)} %and_convert_fusion.refs_2_, f32[256,256]{1,0:T(8,128)} %and_select_fusion.refs_3_, ...), custom_call_target="tpu_custom_call" | custom-call | tf_op jit(solution)/shard_map/band_layer/pallas_call | solution.py:1031
  269.4 3.5 copy.158
  272.9 3.8 all-to-all-start.4
  278.8 35.6 %all-to-all-done.4 = bf16[64,32,384]{2,1,0:T(8,128)(2,1)S(1)} async-done(((bf16[64,32,384]{2,1,0:T(8,128)(2,1)}), bf16[64,32,384]{2,1,0:T(8,128)(2,1)S(1)}, u32[]{:S(2)}, u32[]{:S(2)}) %all-to-all-start.4) | async-done | bytes 1572896 | tf_op jit(solution)/shard_map/all_to_all | solution.py:1140
  314.4 3.7 all-to-all-start.3
  320.3 23.1 %time_ffn_backward.1 = (f32[2,384,1024]{2,1,0:T(8,128)}, bf16[2,512,1024]{2,1,0:T(8,128)(2,1)}, f32[2,8,1024]{2,1,0:T(8,128)}, f32[2,8,1024]{2,1,0:T(8,128)}, bf16[384,3712]{1,0:T(8,128)(2,1)}) custom-call(bf16[2,1024,384]{2,1,0:T(8,128)(2,1)} %bitcast.79, bf16[2,1536,1024]{2,1,0:T(8,128)(2,1)} %get-tuple-element.47.refs_1_, ...), custom_call_target="tpu_custom_call" | custom-call | tf_op jit(solution)/shard_map/time_ffn_backward/pallas_call | solution.py:742
  343.4 54.1 %time_attention_backward.1 = (bf16[2,1024,384]{2,1,0:T(8,128)(2,1)}, bf16[384,1664]{1,0:T(8,128)(2,1)}) custom-call(bf16[2,8,1024,1024]{3,2,1,0:T(8,128)(2,1)} %get-tuple-element.42.refs_0_, bf16[2,512,1024]{2,1,0:T(8,128)(2,1)} %get-tuple-element.43.refs_1_, bf16[2,512,1024]{2,1,0:T(8,128)(2,1)} %get-tuple-element.44.refs_2_, ...), custom_call_target="tpu_custom_call" | custom-call | tf_op jit(solution)/shard_map/time_attention_backward/pallas_call | solution.py:850
  398.9 2.8 copy.146
  401.7 3.8 all-to-all-start.5
  406.9 33.4 %all-to-all-done.5 = bf16[2,1024,384]{2,0,1:T(2,128)(2,1)S(1)} async-done(((bf16[2,1024,384]{2,0,1:T(2,128)(2,1)}), bf16[2,1024,384]{2,0,1:T(2,128)(2,1)S(1)}, u32[]{:S(2)}, u32[]{:S(2)}) %all-to-all-start.5) | async-done | bytes 1572896 | tf_op jit(solution)/shard_map/all_to_all | solution.py:1152
  443.2 135.4 %all-reduce.3.cloned.1.call-done = (bf16[384,1664]{1,0:T(8,128)(2,1)}, bf16[384,3712]{1,0:T(8,128)(2,1)}, bf16[384,5248]{1,0:T(8,128)(2,1)}) async-done(((bf16[384,1664]{1,0:T(8,128)(2,1)}, bf16[384,3712]{1,0:T(8,128)(2,1)}, bf16[384,5248]{1,0:T(8,128)(2,1)}), (bf16[384,1664]{1,0:T(8,128)(2,1)}, bf16[384,3712]{1,0:T(8,128)(2,1)}, bf16[384,5248]{1,0:T(8,128)(2,1)})) %all-reduce.3.cloned.1.call-update) | async-done | bytes 8159248 | tf_op jit(solution)/shard_map/psum | solution.py:1153
  578.6 7.2 %convert_bitcast_fusion.1 = (f32[1536,384]{0,1:T(8,128)S(1)}, f32[384,1536]{1,0:T(8,128)}, f32[384,1536]{1,0:T(8,128)}, f32[384,1536]{1,0:T(8,128)}, f32[1536,384]{0,1:T(8,128)}) fusion(bf16[384,5248]{1,0:T(8,128)(2,1)} %get-tuple-element.132, bf16[384,3712]{1,0:T(8,128)(2,1)} %get-tuple-element.131), kind=kLoop, calls=%fused_computation.1 | loop fusion | flops 2949120 | bytes 17694720 | tf_op jit(solution)/shard_map/transpose | solution.py:1181
  593.4 3.0 copy.150
  (79 shorter events, 52.6 us)
Async XLA Ops:
  7.2 4.4 copy-start.1
  7.2 24.4 %all-to-all-start = ((bf16[8,256,384]{2,1,0:T(8,128)(2,1)}), bf16[8,256,384]{2,1,0:T(8,128)(2,1)S(1)}, u32[]{:S(2)}, u32[]{:S(2)}) async-start(bf16[8,256,384]{2,1,0:T(8,128)(2,1)} %bitcast.93), calls=%async_computation | async-start | bytes 3145728 | tf_op jit(solution)/shard_map/all_to_all | solution.py:1112
  31.6 6.7 %copy-start.8 = (bf16[384]{0:T(512)(128)(2,1)S(1)}, bf16[384]{0:T(512)(128)(2,1)}, u32[]{:S(2)}) copy-start(bf16[384]{0:T(512)(128)(2,1)} %param.22) | copy-start | bytes 2308
  31.6 7.5 %copy-start.9 = (bf16[384]{0:T(512)(128)(2,1)S(1)}, bf16[384]{0:T(512)(128)(2,1)}, u32[]{:S(2)}) copy-start(bf16[384]{0:T(512)(128)(2,1)} %param.26) | copy-start | bytes 2308
  31.6 95.4 %all-to-all-start.2 = ((bf16[8,256,384]{2,0,1:T(8,128)(2,1)}), bf16[8,256,384]{2,0,1:T(8,128)(2,1)S(1)}, u32[]{:S(2)}, u32[]{:S(2)}) async-start(bf16[8,256,384]{2,0,1:T(8,128)(2,1)} %bitcast.70), calls=%async_computation.2 | async-start | bytes 3145728 | tf_op jit(solution)/shard_map/all_to_all | solution.py:1115
  45.4 2.5 copy-start
  127.0 5.5 copy-start.10
  127.0 43.0 %all-to-all-start.1 = ((bf16[2,1024,384]{2,0,1:T(2,128)(2,1)}), bf16[2,1024,384]{2,0,1:T(2,128)(2,1)S(1)}, u32[]{:S(2)}, u32[]{:S(2)}) async-start(bf16[2,1024,384]{2,0,1:T(2,128)(2,1)} %copy.124), calls=%async_computation.1 | async-start | bytes 3145728 | tf_op jit(solution)/shard_map/all_to_all | solution.py:1124
  140.1 2.5 copy-start.4
  140.1 6.4 %copy-start.7 = (bf16[384,8]{0,1:T(8,128)(2,1)S(1)}, bf16[384,8]{0,1:T(8,128)(2,1)}, u32[]{:S(2)}) copy-start(bf16[384,8]{0,1:T(8,128)(2,1)} %param.31) | copy-start | bytes 18436
  272.9 3.8 copy-start.3
  272.9 41.5 %all-to-all-start.4 = ((bf16[64,32,384]{2,1,0:T(8,128)(2,1)}), bf16[64,32,384]{2,1,0:T(8,128)(2,1)S(1)}, u32[]{:S(2)}, u32[]{:S(2)}) async-start(bf16[64,32,384]{2,1,0:T(8,128)(2,1)} %bitcast.68), calls=%async_computation.4 | async-start | bytes 3145728 | tf_op jit(solution)/shard_map/all_to_all | solution.py:1140
  314.4 3.8 copy-start.6
  314.4 87.3 %all-to-all-start.3 = ((bf16[64,32,384]{2,1,0:T(8,128)(2,1)}), bf16[64,32,384]{2,1,0:T(8,128)(2,1)S(1)}, u32[]{:S(2)}, u32[]{:S(2)}) async-start(bf16[64,32,384]{2,1,0:T(8,128)(2,1)} %bitcast.69), calls=%async_computation.3 | async-start | bytes 3145728 | tf_op jit(solution)/shard_map/all_to_all | solution.py:1144
  318.1 260.5 %all-reduce.3.cloned.1.call-start = ((), (), s32[]{:S(2)}) async-start(), calls=%async_computation.6 | async-start | bytes 16318464 | tf_op jit(solution)/shard_map/psum | solution.py:1153
  397.5 1.4 copy-start.2
  401.7 38.6 %all-to-all-start.5 = ((bf16[2,1024,384]{2,0,1:T(2,128)(2,1)}), bf16[2,1024,384]{2,0,1:T(2,128)(2,1)S(1)}, u32[]{:S(2)}, u32[]{:S(2)}) async-start(bf16[2,1024,384]{2,0,1:T(2,128)(2,1)} %copy.146), calls=%async_computation.5 | async-start | bytes 3145728 | tf_op jit(solution)/shard_map/all_to_all | solution.py:1152
  585.9 4.2 copy-start.5
Sparse Core Ops, SparseCore 0:
  397.7 180.9 all-reduce.2

commit v2 on v1

--- a/solution.py
+++ b/solution.py
@@ -569,6 +569,18 @@
         lax.fori_loop(0, frames // BLOCK, block, 0)
 
 
+def sum_shapes(*shapes):
+    return [jax.ShapeDtypeStruct(shape, BF16) for shape in shapes]
+
+
+def sum_specs(*shapes):
+    return [pl.BlockSpec(shape, lambda *ids: (0, 0)) for shape in shapes]
+
+
+def cost(flops, exps=0, moved=0):
+    return pl.CostEstimate(flops=int(flops), bytes_accessed=int(moved), transcendentals=int(exps))
+
+
 def whole_spec(array):
     nd = array.ndim
     return pl.BlockSpec(array.shape, lambda *ids: (0,) * nd, pipeline_mode=pl.Buffered(1))
@@ -616,6 +628,7 @@
         out_specs=specs,
         scratch_shapes=[pltpu.VMEM((model, frames), F32)],
         compiler_params=pltpu.CompilerParams(vmem_limit_bytes=VMEM_BYTES),
+        cost_estimate=cost(2.0e6 * 4 * slots * frames, 2 * slots * heads * frames * frames, 60e6),
         name="time_forward",
     )(rows, *consts)
 
@@ -673,12 +686,9 @@
     datt_ref,
     minus_ref,
     dlogit_ref,
-    sums_ref,
-    dw1_ref,
-    dw2t_ref,
-    dwot_ref,
-    dg2_ref,
+    *refs,
 ):
+    sums_refs, (dw1_ref, dw2t_ref, dwot_ref, dg2_ref) = refs[:4], refs[4:]
     step = pl.program_id(0) * pl.num_programs(1) + pl.program_id(1)
     last = pl.num_programs(0) * pl.num_programs(1) - 1
     size = wo_ref.shape[0] // heads
@@ -710,22 +720,18 @@
 
     @pl.when(step == last)
     def finish():
-        pack_sums(sums_ref, (dw1_ref, dw2t_ref, dwot_ref, dg2_ref))
-
-
-def pack_sums(sums_ref, parts):
-    at = 0
+        finish_sums(sums_refs, ((dw1_ref, False), (dw2t_ref, True), (dwot_ref, True), dg2_ref))
+
+
+def finish_sums(outs, parts):
     narrow = []
-    for ref in parts:
-        width = ref.shape[1]
-        if width % 128 == 0:
-            sums_ref[:, at : at + width] = ref[...].astype(BF16)
-            at += width
-        else:
-            narrow.append(ref[...])
+    for out_ref, (ref, flipped) in zip(outs[:-1], parts):
+        out_ref[...] = (ref[...].T if flipped else ref[...]).astype(BF16)
+    for ref in parts[len(outs) - 1 :]:
+        narrow.append(ref[...])
     used = sum(part.shape[1] for part in narrow)
-    narrow.append(jnp.zeros((sums_ref.shape[0], 128 - used), F32))
-    sums_ref[:, at : at + 128] = jnp.concatenate(narrow, axis=1).astype(BF16)
+    narrow.append(jnp.zeros((outs[-1].shape[0], 128 - used), F32))
+    outs[-1][...] = jnp.concatenate(narrow, axis=1).astype(BF16)
 
 
 def time_ffn_backward(grad, act, slope, nf, mid, mixed, att, gate, linv, g2, w1, w2, wo):
@@ -738,7 +744,7 @@
         return pl.BlockSpec((1, rows, tokens), lambda s, c: (s, 0, c))
 
     consts = (g2, w1, w2, wo)
-    width = 2 * hidden + inner + 128
+    sums = ((model, hidden), (hidden, model), (inner, model), (model, 128))
     return pl.pallas_call(
         lambda *refs: time_ffn_backward_kernel(heads, *refs),
         grid=(slots, frames // tokens),
@@ -747,12 +753,12 @@
             jax.ShapeDtypeStruct((slots, inner, frames), BF16),
             jax.ShapeDtypeStruct((slots, heads, frames), F32),
             jax.ShapeDtypeStruct((slots, heads, frames), F32),
-            jax.ShapeDtypeStruct((model, width), BF16),
-        ],
+        ]
+        + sum_shapes(*sums),
         in_specs=[pl.BlockSpec((1, tokens, model), lambda s, c: (s, c, 0))]
         + [cut(a.shape[1]) for a in (act, slope, nf, mid, mixed, att, gate, linv)]
         + [whole_spec(c) for c in consts],
-        out_specs=[cut(model), cut(inner), cut(heads), cut(heads), pl.BlockSpec((model, width), lambda s, c: (0, 0))],
+        out_specs=[cut(model), cut(inner), cut(heads), cut(heads)] + sum_specs(*sums),
         scratch_shapes=[
             pltpu.VMEM((model, hidden), F32),
             pltpu.VMEM((model, hidden), F32),
@@ -760,6 +766,7 @@
             pltpu.VMEM((model, 1), F32),
         ],
         compiler_params=pltpu.CompilerParams(vmem_limit_bytes=VMEM_BYTES),
+        cost_estimate=cost(8.0e6 * slots * frames, 0, 30e6),
         name="time_ffn_backward",
     )(grad, act, slope, nf, mid, mixed, att, gate, linv, *consts)
 
@@ -782,12 +789,9 @@
     wp_ref,
     wg_ref,
     out_ref,
-    sums_ref,
-    dproj_ref,
-    dwp_ref,
-    dwg_ref,
-    dg1_ref,
+    *refs,
 ):
+    sums_refs, (dproj_ref, dwp_ref, dwg_ref, dg1_ref) = refs[:2], refs[2:]
     slot, head = pl.program_id(0), pl.program_id(1)
     inner = q_ref.shape[1]
     size = inner // heads
@@ -834,7 +838,7 @@
 
     @pl.when((slot == pl.num_programs(0) - 1) & (head == heads - 1))
     def finish():
-        pack_sums(sums_ref, (dwp_ref, dwg_ref, dg1_ref))
+        finish_sums(sums_refs, ((dwp_ref, False), dwg_ref, dg1_ref))
 
 
 def time_attention_backward(p, q, k, v, datt, minus, dlogit, n, x, dmid, cos, sin, g1, wp, wg):
@@ -846,21 +850,21 @@
         return pl.BlockSpec((1,) + array.shape[1:], lambda s, h: (s, 0, 0))
 
     consts = (cos, sin, g1, wp, wg)
-    width = 3 * inner + 128
+    sums = ((model, 3 * inner), (model, 128))
     return pl.pallas_call(
         lambda *refs: time_attention_backward_kernel(heads, *refs),
         grid=(slots, heads),
         out_shape=[
             jax.ShapeDtypeStruct((slots, frames, model), BF16),
-            jax.ShapeDtypeStruct((model, width), BF16),
-        ],
+        ]
+        + sum_shapes(*sums),
         in_specs=[pl.BlockSpec((1, 1, frames, frames), lambda s, h: (s, h, 0, 0))]
         + [per_slot(a) for a in (q, k, v, datt, minus, dlogit, n, x, dmid)]
         + [whole_spec(c) for c in consts],
         out_specs=[
             pl.BlockSpec((1, frames, model), lambda s, h: (s, 0, 0)),
-            pl.BlockSpec((model, width), lambda s, h: (0, 0)),
-        ],
+        ]
+        + sum_specs(*sums),
         scratch_shapes=[
             pltpu.VMEM((3 * inner, frames), BF16),
             pltpu.VMEM((model, 3 * inner), F32),
@@ -868,6 +872,7 @@
             pltpu.VMEM((model, 1), F32),
         ],
         compiler_params=pltpu.CompilerParams(vmem_limit_bytes=VMEM_BYTES),
+        cost_estimate=cost(20.0e6 * slots * frames, 0, 60e6),
         name="time_attention_backward",
     )(p, q, k, v, datt, minus, dlogit, n, x, dmid, *consts)
 
@@ -894,7 +899,11 @@
     w2_ref,
     y_ref,
     dx_ref,
-    sums_ref,
+    dwp_out,
+    dw1_out,
+    dw2_out,
+    dwo_out,
+    narrow_out,
     q_ref,
     k_ref,
     v_ref,
@@ -922,6 +931,7 @@
     inner = q_ref.shape[0]
     size = inner // heads
     groups = tokens // BLOCK
+    sums_refs = (dwp_out, dw1_out, dw2_out, dwo_out, narrow_out)
 
     @pl.when(step == 0)
     def clear():
@@ -1015,7 +1025,10 @@
 
     @pl.when(step == pl.num_programs(0) - 1)
     def finish():
-        pack_sums(sums_ref, (dwp_ref, dw1_ref, dw2t_ref, dwot_ref, dwg_ref, dg1_ref, dg2_ref))
+        finish_sums(
+            sums_refs,
+            ((dwp_ref, False), (dw1_ref, False), (dw2t_ref, True), (dwot_ref, True), dwg_ref, dg1_ref, dg2_ref),
+        )
 
 
 def band_layer(x, cot, mask, bias, cos, sin, params, turned):
@@ -1026,7 +1039,7 @@
     heads, inner, hidden = gating.shape[1], output_weight.shape[0], expand.shape[1]
     groups = tokens // BLOCK
     consts = (bias, cos, sin, g1, g2, wpt, wgt, wot, w1t, w2t, project, gating, output_weight, expand, shrink)
-    width = 3 * inner + 2 * hidden + inner + 128
+    sums = ((model, 3 * inner), (model, hidden), (hidden, model), (inner, model), (model, 128))
     rows = pl.BlockSpec((tokens, model), lambda i: (i, 0))
     return pl.pallas_call(
         lambda *refs: band_kernel(heads, *refs),
@@ -1034,10 +1047,10 @@
         out_shape=[
             jax.ShapeDtypeStruct((total, model), BF16),
             jax.ShapeDtypeStruct((total, model), BF16),
-            jax.ShapeDtypeStruct((model, width), BF16),
-        ],
+        ]
+        + sum_shapes(*sums),
         in_specs=[rows, rows, pl.BlockSpec((1, 1, tokens), lambda i: (i, 0, 0))] + [whole_spec(c) for c in consts],
-        out_specs=[rows, rows, pl.BlockSpec((model, width), lambda i: (0, 0))],
+        out_specs=[rows, rows] + sum_specs(*sums),
         scratch_shapes=[
             pltpu.VMEM((inner, tokens), BF16),
             pltpu.VMEM((inner, tokens), BF16),
@@ -1062,6 +1075,7 @@
             pltpu.VMEM((model, 1), F32),
         ],
         compiler_params=pltpu.CompilerParams(vmem_limit_bytes=VMEM_BYTES),
+        cost_estimate=cost(30.0e6 * total, 0, 60e6),
         name="band_layer",
     )(x, cot, mask, *consts)
 
@@ -1125,7 +1139,7 @@
         result.reshape(slots, frames, model), ("band", "batch"), split_axis=1, concat_axis=0, tiled=True
     )
     frame_rows = frame_rows.transpose(1, 0, 2).reshape(piece * slot_count, model)
-    y, dx, band_sums = band_layer(
+    y, dx, *band_sums = band_layer(
         frame_rows,
         cot_rows,
         mask,
@@ -1142,43 +1156,38 @@
     slot_grad = slot_grad.reshape(slots, frames, model)
     y = y.reshape(piece, slot_count, model).transpose(1, 0, 2)
     layer_output = lax.all_to_all(y, "band", split_axis=0, concat_axis=1, tiled=True)
-    dmid, datt, minus, dlogit, ffn_sums = time_ffn_backward(
+    dmid, datt, minus, dlogit, *ffn_sums = time_ffn_backward(
         slot_grad, act, slope, nf, mid, mixed, att, gate, linv, g2, time_params[5], time_params[6], time_params[3]
     )
+    ffn_sums, band_sums = lax.optimization_barrier((ffn_sums, band_sums))
     ffn_sums = lax.psum(ffn_sums, ("band", "batch"))
-    grads, attn_sums = time_attention_backward(
+    grads, *attn_sums = time_attention_backward(
         p, q, k, v, datt, minus, dlogit, n, rows, dmid, time_cos.T, time_sin.T, g1, time_params[1], time_params[2]
     )
     input_grad = lax.all_to_all(grads, "batch", split_axis=1, concat_axis=0, tiled=True)
+    attn_sums, ffn_sums = lax.optimization_barrier((attn_sums, ffn_sums))
     attn_sums = lax.psum(attn_sums, ("band", "batch"))
 
-    def cut(sums, widths):
-        parts, at = [], 0
-        for width in widths:
-            parts.append(sums[:, at : at + width].astype(F32))
-            at += width
-        return parts
-
-    dwp, dwg, dg1 = cut(attn_sums, (3 * inner, heads, 1))
-    dw1, dw2t, dwot, dg2 = cut(ffn_sums, (hidden, hidden, inner, 1))
-    bwp, bw1, bw2t, bwot, bwg, bg1, bg2 = cut(band_sums, (3 * inner, hidden, hidden, inner, heads, 1, 1))
+    dwp, attn_narrow = (part.astype(F32) for part in attn_sums)
+    dw1, dw2, dwo, ffn_narrow = (part.astype(F32) for part in ffn_sums)
+    bwp, bw1, bw2, bwo, band_narrow = (part.astype(F32) for part in band_sums)
     return (
         layer_output.reshape(activations.shape),
         input_grad.astype(F32).reshape(activations.shape),
-        dg1[:, 0],
+        attn_narrow[:, heads],
         dwp,
-        dwg,
-        dwot.T,
-        dg2[:, 0],
+        attn_narrow[:, :heads],
+        dwo,
+        ffn_narrow[:, 0],
         dw1,
-        dw2t.T,
-        bg1[:, 0],
+        dw2,
+        band_narrow[:, heads],
         bwp,
-        bwg,
-        bwot.T,
-        bg2[:, 0],
+        band_narrow[:, :heads],
+        bwo,
+        band_narrow[:, heads + 1],
         bw1,
-        bw2t.T,
+        bw2,
     )
 
 

time: 619 us -> 765 us (1.24)
  waiting for transfers between devices: 241 us -> 393 us
    psum x0 -> x2, waiting for transfers between devices: none -> 190 us  [the longest x1 109 us: slot_shards(): band_sums = lax.psum(band_sums, ('band', 'batch'))]
    all_to_all x1, waiting for transfers between devices: 33.4 us -> 0.01 us  [slot_shards(): lax.all_to_all(grads, 'batch', split_axis=1, concat_axis=0, tiled=True)]
    psum x1, waiting for transfers between devices: 135 us -> 120 us  [slot_shards(): attn_sums = lax.psum(attn_sums, ('band', 'batch'))]
    convert_element_type x2 -> x10, other arithmetic: 2.62 us -> 14 us  [the longest x5 5.89 us: slot_shards(): bwp, bw1, bw2, bwo, band_narrow = (part.astype(F32) for part in band_sums)]
    all_to_all x1, waiting for transfers between devices: 35.6 us -> 45.2 us  [slot_shards(): lax.all_to_all(dx, ('band', 'batch'), split_axis=0, concat_axis=1, tiled=...]
    unnamed x39 -> x49, local copies, waits for them, and re-layouts: 31.2 us -> 21.7 us
    transpose x2 -> x0, other arithmetic: 9.43 us -> none  [slot_shards(): return (layer_output.reshape(activations.shape), input_grad.astype(F32).r...]
  transfers between devices with their start and end apart: 7 -> 9, of which waited for: 5 -> 6; matrix products, arithmetic and copies ran while one was open for 8% -> 8% of each run, Pallas kernels for 24% -> 20%
where the time goes in v2:
time: 765 us; the launch traced here: 757 us
  waiting for transfers between devices  393 us (51%)
  Pallas kernels  245 us (32%)
  local copies, waits for them, and re-layouts  54.5 us (7%)
  starting transfers between devices  28.4 us (4%)
  other arithmetic  20.7 us (3%)
  between operations  15.1 us (2%)
    psum x1, waiting for transfers between devices, slot_shards(): attn_sums = lax.psum(attn_sums, ('band', 'batch'))  120 us
    psum x1, waiting for transfers between devices, slot_shards(): band_sums = lax.psum(band_sums, ('band', 'batch'))  109 us
    pallas_call x1, Pallas kernels, band_layer(): pl.pallas_call(lambda *refs: band_kernel(heads, *refs), grid=(steps,), ou...  97.3 us
    psum x1, waiting for transfers between devices, slot_shards(): ffn_sums = lax.psum(ffn_sums, ('band', 'batch'))  81.4 us
    pallas_call x1, Pallas kernels, time_forward(): pl.pallas_call(lambda *refs: time_forward_kernel(heads, *refs), grid=(slo...  70.6 us
    pallas_call x1, Pallas kernels, time_attention_backward(): pl.pallas_call(lambda *refs: time_attention_backward_kernel(heads, *refs)...  54 us
    all_to_all x1, waiting for transfers between devices, slot_shards(): lax.all_to_all(dx, ('band', 'batch'), split_axis=0, concat_axis=1, tiled=...  45.2 us
    pallas_call x1, Pallas kernels, time_ffn_backward(): pl.pallas_call(lambda *refs: time_ffn_backward_kernel(heads, *refs), grid...  23.4 us
  transfers between devices with their start and end apart: 9, of which 6 were waited for; matrix products, arithmetic and copies ran while one was open for 8% of the time, Pallas kernels for 20%

profile of v2, /device:TPU:0, one launch (start us, length us, event | category | flops | bytes accessed | tf_op | source)
XLA Modules:
  0.0 756.7 jit_solution(10139473691754027016)
XLA Ops:
  7.2 4.4 all-to-all-start
  13.6 18.0 %all-to-all-done = bf16[8,256,384]{2,1,0:T(8,128)(2,1)S(1)} async-done(((bf16[8,256,384]{2,1,0:T(8,128)(2,1)}), bf16[8,256,384]{2,1,0:T(8,128)(2,1)S(1)}, u32[]{:S(2)}, u32[]{:S(2)}) %all-to-all-start) | async-done | bytes 1572896 | tf_op jit(solution)/shard_map/all_to_all | solution.py:1126
  31.6 6.7 all-to-all-start.2
  45.4 2.5 copy.108
  51.9 70.6 %time_forward.1 = (bf16[2,1024,384]{2,1,0:T(8,128)(2,1)}, bf16[2,384,1024]{2,1,0:T(8,128)(2,1)}, bf16[2,512,1024]{2,1,0:T(8,128)(2,1)}, bf16[2,512,1024]{2,1,0:T...) custom-call(bf16[2,1024,384]{2,1,0:T(8,128)(2,1)} %bitcast.75, ...), custom_call_target="tpu_custom_call" | custom-call | flops 16384000000 | bytes 60000000 | tf_op jit(solution)/shard_map/time_forward/pallas_call | solution.py:623
  124.2 2.8 copy.112
  127.0 5.3 all-to-all-start.1
  135.3 2.4 copy.119
  137.7 2.4 copy.121
  140.0 2.5 copy.122
  151.4 18.6 %all-to-all-done.1 = bf16[2,1024,384]{2,0,1:T(2,128)(2,1)S(1)} async-done(((bf16[2,1024,384]{2,0,1:T(2,128)(2,1)}), bf16[2,1024,384]{2,0,1:T(2,128)(2,1)S(1)}, u32[]{:S(2)}, u32[]{:S(2)}) %all-to-all-start.1) | async-done | bytes 1572896 | tf_op jit(solution)/shard_map/all_to_all | solution.py:1138
  172.2 97.3 %band_layer.1 = (bf16[2048,384]{1,0:T(8,128)(2,1)}, bf16[2048,384]{1,0:T(8,128)(2,1)}, bf16[384,1536]{1,0:T(8,128)(2,1)}, bf16[384,1536]{1,0:T(8,128)(2,1)}, bf1...) custom-call(bf16[2048,384]{1,0:T(8,128)(2,1)} %bitcast.80, bf16[2048,384]{1,0:T(8,128)(2,1)} %bitcast.79, ...), custom_call_target="tpu_custom_call" | custom-call | flops 61440000000 | bytes 60000000 | tf_op jit(solution)/shard_map/band_layer/pallas_call | solution.py:1044
  269.5 3.5 copy.142
  273.0 3.8 all-to-all-start.4
  280.4 45.2 %all-to-all-done.4 = bf16[64,32,384]{2,1,0:T(8,128)(2,1)S(1)} async-done(((bf16[64,32,384]{2,1,0:T(8,128)(2,1)}), bf16[64,32,384]{2,1,0:T(8,128)(2,1)S(1)}, u32[]{:S(2)}, u32[]{:S(2)}) %all-to-all-start.4) | async-done | bytes 1572896 | tf_op jit(solution)/shard_map/all_to_all | solution.py:1154
  325.6 4.4 all-to-all-start.3
  331.3 23.4 %time_ffn_backward.1 = (f32[2,384,1024]{2,1,0:T(8,128)}, bf16[2,512,1024]{2,1,0:T(8,128)(2,1)}, f32[2,8,1024]{2,1,0:T(8,128)}, f32[2,8,1024]{2,1,0:T(8,128)}, bf...) custom-call(bf16[2,1024,384]{2,1,0:T(8,128)(2,1)} %bitcast.83, ...), custom_call_target="tpu_custom_call" | custom-call | flops 16384000000 | bytes 30000000 | tf_op jit(solution)/shard_map/time_ffn_backward/pallas_call | solution.py:748
  354.8 108.9 %all-reduce.11.cloned.1.call-done = (bf16[384,1536]{1,0:T(8,128)(2,1)}, bf16[384,1536]{1,0:T(8,128)(2,1)}, bf16[1536,384]{1,0:T(8,128)(2,1)}, bf16[512,384]{1,0:T(8,128)(2,1)}, bf16[384,128]{1,0:T(8,128)(2,1)}) async-done(((bf16[384,1536]{1,0:T(8,128)(2,1)}, bf16[384,1536]{1,0:T(8,128)(2,1)}, bf16[1536,384]{1,0:T(8,128)(2,1)}, bf16[512,384]{1,0:T(8,128)(2,1)}, bf16[384,128]{1,0:T(8,128)(2,1)}), ...) | async-done | bytes 4030480 | tf_op jit(solution)/shard_map/psum | solution.py:1152
  463.7 54.0 %time_attention_backward.1 = (bf16[2,1024,384]{2,1,0:T(8,128)(2,1)}, bf16[384,1536]{1,0:T(8,128)(2,1)}, bf16[384,128]{1,0:T(8,128)(2,1)}) custom-call(bf16[2,8,1024,1024]{3,2,1,0:T(8,128)(2,1)} %get-tuple-element.65.refs_0_, bf16[2,512,1024]{2,1,0:T(8,128)(2,1)} %get-tuple-element.66.refs_1_, bf16[2,512,1024]{2,1,0:T(8,128)(2,1)} %get-tuple-element.67.refs_2_, ...), custom_call_target="tpu_custom_call" | custom-call | flops 40960000000 | bytes 60000000 | tf_op jit(solution)/shard_map/time_attention_backward/pallas_call | solution.py:854
  517.7 4.2 copy.134
  521.9 3.6 all-to-all-start.5
  525.8 81.4 %all-reduce.9.cloned.1.call-done = (bf16[384,1536]{1,0:T(8,128)(2,1)}, bf16[1536,384]{1,0:T(8,128)(2,1)}, bf16[512,384]{1,0:T(8,128)(2,1)}, bf16[384,128]{1,0:T(8,128)(2,1)}) async-done(((bf16[384,1536]{1,0:T(8,128)(2,1)}, bf16[1536,384]{1,0:T(8,128)(2,1)}, bf16[512,384]{1,0:T(8,128)(2,1)}, bf16[384,128]{1,0:T(8,128)(2,1)}), (bf16[384,1536]{1,0:T(8,128)(2,1)}, bf16[1536,384]{1,0:T(8,128)(2,1)}, ...) | async-done | bytes 2850832 | tf_op jit(solution)/shard_map/psum | solution.py:1163
  623.6 119.8 %all-reduce.7.cloned.1.call-done = (bf16[384,128]{1,0:T(8,128)(2,1)}, bf16[384,1536]{1,0:T(8,128)(2,1)}) async-done(((bf16[384,128]{1,0:T(8,128)(2,1)}, bf16[384,1536]{1,0:T(8,128)(2,1)}), (bf16[384,128]{1,0:T(8,128)(2,1)}, bf16[384,1536]{1,0:T(8,128)(2,1)})) %all-reduce.7.cloned.1.call-update) | async-done | bytes 1277968 | tf_op jit(solution)/shard_map/psum | solution.py:1169
  745.2 3.0 convert_element_type.88
  (103 shorter events, 53.1 us)
Async XLA Ops:
  7.2 4.4 copy-start
  7.2 24.4 %all-to-all-start = ((bf16[8,256,384]{2,1,0:T(8,128)(2,1)}), bf16[8,256,384]{2,1,0:T(8,128)(2,1)S(1)}, u32[]{:S(2)}, u32[]{:S(2)}) async-start(bf16[8,256,384]{2,1,0:T(8,128)(2,1)} %bitcast.74), calls=%async_computation | async-start | bytes 3145728 | tf_op jit(solution)/shard_map/all_to_all | solution.py:1126
  31.6 6.7 copy-start.15
  31.6 7.6 copy-start.16
  31.6 95.4 %all-to-all-start.2 = ((bf16[8,256,384]{2,0,1:T(8,128)(2,1)}), bf16[8,256,384]{2,0,1:T(8,128)(2,1)S(1)}, u32[]{:S(2)}, u32[]{:S(2)}) async-start(bf16[8,256,384]{2,0,1:T(8,128)(2,1)} %bitcast.62), calls=%async_computation.2 | async-start | bytes 3145728 | tf_op jit(solution)/shard_map/all_to_all | solution.py:1129
  45.4 2.5 copy-start.9
  127.0 5.5 copy-start.17
  127.0 43.0 %all-to-all-start.1 = ((bf16[2,1024,384]{2,0,1:T(2,128)(2,1)}), bf16[2,1024,384]{2,0,1:T(2,128)(2,1)S(1)}, u32[]{:S(2)}, u32[]{:S(2)}) async-start(bf16[2,1024,384]{2,0,1:T(2,128)(2,1)} %copy.112), calls=%async_computation.1 | async-start | bytes 3145728 | tf_op jit(solution)/shard_map/all_to_all | solution.py:1138
  140.0 2.5 copy-start.8
  140.0 6.4 copy-start.13
  273.0 52.6 %all-to-all-start.4 = ((bf16[64,32,384]{2,1,0:T(8,128)(2,1)}), bf16[64,32,384]{2,1,0:T(8,128)(2,1)S(1)}, u32[]{:S(2)}, u32[]{:S(2)}) async-start(bf16[64,32,384]{2,1,0:T(8,128)(2,1)} %bitcast.60), calls=%async_computation.4 | async-start | bytes 3145728 | tf_op jit(solution)/shard_map/all_to_all | solution.py:1154
  276.8 186.9 %all-reduce.11.cloned.1.call-start = ((), (), s32[]{:S(2)}) async-start(), calls=%async_computation.8 | async-start | bytes 8060928 | tf_op jit(solution)/shard_map/psum | solution.py:1152
  325.6 196.3 %all-to-all-start.3 = ((bf16[64,32,384]{2,1,0:T(8,128)(2,1)}), bf16[64,32,384]{2,1,0:T(8,128)(2,1)S(1)}, u32[]{:S(2)}, u32[]{:S(2)}) async-start(bf16[64,32,384]{2,1,0:T(8,128)(2,1)} %bitcast.61), calls=%async_computation.3 | async-start | bytes 3145728 | tf_op jit(solution)/shard_map/all_to_all | solution.py:1158
  329.9 277.2 %all-reduce.9.cloned.1.call-start = ((), (), s32[]{:S(2)}) async-start(), calls=%async_computation.7 | async-start | bytes 5701632 | tf_op jit(solution)/shard_map/psum | solution.py:1163
  521.9 93.6 %all-to-all-start.5 = ((bf16[2,1024,384]{2,0,1:T(2,128)(2,1)}), bf16[2,1024,384]{2,0,1:T(2,128)(2,1)S(1)}, u32[]{:S(2)}, u32[]{:S(2)}) async-start(bf16[2,1024,384]{2,0,1:T(2,128)(2,1)} %copy.134), calls=%async_computation.5 | async-start | bytes 3145728 | tf_op jit(solution)/shard_map/all_to_all | solution.py:1167
  525.5 218.0 %all-reduce.7.cloned.1.call-start = ((), (), s32[]{:S(2)}) async-start(), calls=%async_computation.6 | async-start | bytes 2555904 | tf_op jit(solution)/shard_map/psum | solution.py:1169
  607.2 1.7 copy-start.4
  608.9 1.7 copy-start.3
  610.6 1.7 copy-start.2
  612.3 1.6 copy-start.10
  616.6 1.9 copy-start.6
  618.5 1.7 copy-start.5
  620.2 1.6 copy-start.11
  620.2 2.5 copy-start.12
  (3 other events, 3.5 us)
Sparse Core Ops, SparseCore 0:
  284.6 178.9 all-reduce.10
  470.2 136.9 all-reduce.8
  612.7 130.7 all-reduce.6

commit v3 on v2

--- a/solution.py
+++ b/solution.py
@@ -481,20 +481,73 @@
     return queries.astype(BF16), keys.astype(BF16), values.astype(BF16)
 
 
+def column(row_ref):
+    row = row_ref[...].astype(F32)
+    return jnp.broadcast_to(row, (8, row.shape[1])).T[:, :1]
+
+
+def flipped(ref):
+    return ref[...].astype(F32).T.astype(BF16)
+
+
+def greet_all(band_count, batch_count):
+    count = band_count * batch_count
+    me = lax.axis_index("band") * batch_count + lax.axis_index("batch")
+    barrier = pltpu.get_barrier_semaphore()
+
+    def signal(i, carry):
+        other = lax.rem(me + i, count)
+        pl.semaphore_signal(
+            barrier,
+            inc=1,
+            device_id=(other // batch_count, lax.rem(other, batch_count)),
+            device_id_type=pl.DeviceIdType.MESH,
+        )
+        return carry
+
+    lax.fori_loop(1, count, signal, 0)
+    pl.semaphore_wait(barrier, count - 1)
+
+
+def send(source, target, send_sem, recv_sem, band, batch):
+    pltpu.make_async_remote_copy(
+        src_ref=source,
+        dst_ref=target,
+        send_sem=send_sem,
+        recv_sem=recv_sem,
+        device_id=(band, batch),
+        device_id_type=pl.DeviceIdType.MESH,
+    ).start()
+
+
+def await_bytes(ref, sem):
+    pltpu.make_async_copy(ref, ref, sem).wait()
+
+
 def time_forward_kernel(
     heads,
-    x_ref,
+    batch_count,
+    band_count,
+    act_in,
+    cot_in,
     bias_ref,
     cos_ref,
     sin_ref,
     g1_ref,
     g2_ref,
-    wpt_ref,
-    wgt_ref,
-    wot_ref,
-    w1t_ref,
-    w2t_ref,
-    result_ref,
+    wp_ref,
+    wg_ref,
+    wo_ref,
+    w1_ref,
+    w2_ref,
+    band_wp_ref,
+    band_wg_ref,
+    band_wo_ref,
+    band_w1_ref,
+    band_w2_ref,
+    band_rows,
+    band_cot,
+    rows_ref,
     n_ref,
     q_ref,
     k_ref,
@@ -508,20 +561,110 @@
     nf_ref,
     act_ref,
     slope_ref,
+    band_wpt_ref,
+    band_wgt_ref,
+    band_wot_ref,
+    band_w1t_ref,
+    band_w2t_ref,
     xt_ref,
+    x_ref,
+    result_ref,
+    wpt_ref,
+    wgt_ref,
+    wot_ref,
+    w1t_ref,
+    w2t_ref,
+    row_send,
+    row_recv,
+    cot_send,
+    cot_recv,
+    result_send,
+    result_recv,
+    local_sem,
 ):
-    head = pl.program_id(1)
-    frames, model = x_ref.shape[1:]
+    slot, head = pl.program_id(0), pl.program_id(1)
+    slots = pl.num_programs(0)
+    slot_dev = cot_in.shape[0]
+    frames, model = rows_ref.shape[1:]
     inner = q_ref.shape[1]
     size = inner // heads
+    my_band, my_batch = lax.axis_index("band"), lax.axis_index("batch")
+    frame_dev = frames // batch_count
+    piece = frame_dev // band_count
+    own_rows = pl.ds(pl.multiple_of(my_batch * frame_dev, frame_dev), frame_dev)
+    held = x_ref.shape[0]
+
+    def own_row_copy(j):
+        return pltpu.make_async_copy(
+            act_in.at[batch_count * j + my_batch], x_ref.at[j, own_rows], local_sem.at[j]
+        )
+
+    def own_cot_copy():
+        return pltpu.make_async_copy(
+            cot_in.at[:, pl.ds(pl.multiple_of(my_band * piece, piece), piece)],
+            band_cot.at[pl.ds(my_band * slot_dev, slot_dev)],
+            local_sem.at[held],
+        )
+
+    @pl.when((slot == 0) & (head == 0))
+    def start():
+        greet_all(band_count, batch_count)
+        for j in range(held):
+            for i in range(1, batch_count):
+                other = lax.rem(my_batch + i, batch_count)
+                send(
+                    act_in.at[batch_count * j + other],
+                    x_ref.at[j, own_rows],
+                    row_send,
+                    row_recv.at[j],
+                    my_band,
+                    other,
+                )
+            own_row_copy(j).start()
+
+        def send_cot(i, carry):
+            other = lax.rem(my_band + i, band_count)
+            send(
+                cot_in.at[:, pl.ds(pl.multiple_of(other * piece, piece), piece)],
+                band_cot.at[pl.ds(my_band * slot_dev, slot_dev)],
+                cot_send,
+                cot_recv,
+                other,
+                my_batch,
+            )
+            return carry
+
+        lax.fori_loop(1, band_count, send_cot, 0)
+        own_cot_copy().start()
+        wpt_ref[...] = flipped(wp_ref)
+        wgt_ref[...] = flipped(wg_ref)
+        wot_ref[...] = flipped(wo_ref)
+        w1t_ref[...] = flipped(w1_ref)
+        w2t_ref[...] = flipped(w2_ref)
+        band_wpt_ref[...] = flipped(band_wp_ref)
+        band_wgt_ref[...] = flipped(band_wg_ref)
+        band_wot_ref[...] = flipped(band_wo_ref)
+        band_w1t_ref[...] = flipped(band_w1_ref)
+        band_w2t_ref[...] = flipped(band_w2_ref)
 
     @pl.when(head == 0)
     def before():
+        for j in range(held):
+
+            @pl.when(slot == j)
+            def arrived():
+                await_bytes(x_ref.at[j, pl.ds(0, (batch_count - 1) * frame_dev)], row_recv.at[j])
+                own_row_copy(j).wait()
+
+        gain = column(g1_ref)
+
         def block(i, carry):
             at = pl.ds(pl.multiple_of(i * BLOCK, BLOCK), BLOCK)
-            rows = x_ref[0, at, :].astype(F32).T
+            held_rows = x_ref[slot, at, :]
+            rows_ref[0, at, :] = held_rows
+            rows = held_rows.astype(F32).T
             xt_ref[:, at] = rows
-            normed = norm_forward(rows, g1_ref[...])
+            normed = norm_forward(rows, gain)
             n_ref[0, :, at] = normed
             queries, keys, values = project_block(
                 normed, wpt_ref, cos_ref[:, at], sin_ref[:, at], inner, LOG2E * size**-0.5
@@ -552,21 +695,54 @@
 
     @pl.when(head == heads - 1)
     def after():
+        gain = column(g2_ref)
+        to_slot = my_band * slot_dev + batch_count * slot + my_batch
+
         def block(i, carry):
             at = pl.ds(pl.multiple_of(i * BLOCK, BLOCK), BLOCK)
             middle = xt_ref[:, at] + dg(wot_ref[...], mixed_ref[0, :, at], NN)
             mid_ref[0, :, at] = middle
-            normed = norm_forward(middle, g2_ref[...])
+            normed = norm_forward(middle, gain)
             nf_ref[0, :, at] = normed
             active, slope = gelu_pair(dg(w1t_ref[...], normed, NN))
             active = active.astype(BF16)
             act_ref[0, :, at] = active
             slope_ref[0, :, at] = slope.astype(BF16)
             result = middle + dg(w2t_ref[...], active, NN)
-            result_ref[0, at, :] = result.T.astype(BF16)
+            result_ref[slot, at, :] = result.T.astype(BF16)
+
+            def send_result(j, carry):
+                other = lax.rem(my_band + j, band_count)
+                source = result_ref.at[slot, pl.ds(pl.multiple_of(i * frame_dev + other * piece, piece), piece)]
+                mine = (other == my_band) & (i == my_batch)
+
+                @pl.when(mine)
+                def keep():
+                    pltpu.make_async_copy(source, band_rows.at[to_slot], local_sem.at[held + 1]).start()
+
+                @pl.when(jnp.logical_not(mine))
+                def give():
+                    send(source, band_rows.at[to_slot], result_send, result_recv, other, i)
+
+                return carry
+
+            lax.fori_loop(1, band_count + 1, send_result, 0)
             return carry
 
         lax.fori_loop(0, frames // BLOCK, block, 0)
+
+    @pl.when((slot == slots - 1) & (head == heads - 1))
+    def finish():
+        others = held * (band_count * batch_count - 1)
+        others_cot = (band_count - 1) * slot_dev
+        others_rows = (batch_count - 1) * frame_dev
+        await_bytes(band_cot.at[pl.ds(0, others_cot)], cot_recv)
+        await_bytes(band_cot.at[pl.ds(0, others_cot)], cot_send)
+        own_cot_copy().wait()
+        await_bytes(x_ref.at[:, pl.ds(0, others_rows)], row_send)
+        await_bytes(band_rows.at[pl.ds(0, others)], result_send)
+        await_bytes(band_rows.at[pl.ds(0, held)], local_sem.at[held + 1])
+        await_bytes(band_rows.at[pl.ds(0, others)], result_recv)
 
 
 def sum_shapes(*shapes):
@@ -586,11 +762,13 @@
     return pl.BlockSpec(array.shape, lambda *ids: (0,) * nd, pipeline_mode=pl.Buffered(1))
 
 
-def time_forward(rows, bias, cos, sin, g1, g2, wpt, wgt, wot, w1t, w2t):
-    slots, frames, model = rows.shape
-    heads = wgt.shape[0]
-    inner = wot.shape[1]
-    hidden = w1t.shape[0]
+def time_forward(activations, cotangent, bias, cos, sin, params, band_params, band_count, batch_count):
+    g1, wp, wg, wo, g2, w1, w2 = params
+    _, bwp, bwg, bwo, _, bw1, bw2 = band_params
+    slot_dev, frame_dev, model = activations.shape
+    slots, frames = slot_dev // batch_count, frame_dev * batch_count
+    heads, inner, hidden = wg.shape[1], wo.shape[0], w1.shape[1]
+    piece = frame_dev // band_count
 
     def per_slot(*shape):
         return pl.BlockSpec((1,) + shape, lambda s, h: (s,) + (0,) * len(shape))
@@ -611,7 +789,11 @@
         ((hidden, frames), BF16),
         ((hidden, frames), BF16),
     ]
-    shapes, specs = [], []
+    flips = [(w.shape[1], w.shape[0]) for w in (bwp, bwg, bwo, bw1, bw2)]
+    own_flips = [(w.shape[1], w.shape[0]) for w in (wp, wg, wo, w1, w2)]
+    exchanged = jax.ShapeDtypeStruct((slot_dev * band_count, piece, model), BF16)
+    anywhere = pl.BlockSpec(memory_space=pl.ANY)
+    shapes, specs = [exchanged, exchanged], [anywhere, anywhere]
     for entry in outs:
         if entry is None:
             shapes.append(jax.ShapeDtypeStruct((slots, heads, frames, frames), BF16))
@@ -619,18 +801,30 @@
         else:
             shapes.append(jax.ShapeDtypeStruct((slots,) + entry[0], entry[1]))
             specs.append(per_slot(*entry[0]))
-    consts = (bias, cos, sin, g1, g2, wpt, wgt, wot, w1t, w2t)
+    for shape in flips:
+        shapes.append(jax.ShapeDtypeStruct(shape, BF16))
+        specs.append(pl.BlockSpec(shape, lambda s, h: (0, 0), pipeline_mode=pl.Buffered(1)))
+    consts = (bias, cos, sin, g1, g2, wp, wg, wo, w1, w2, bwp, bwg, bwo, bw1, bw2)
+    dma = pltpu.SemaphoreType.DMA
     return pl.pallas_call(
-        lambda *refs: time_forward_kernel(heads, *refs),
+        lambda *refs: time_forward_kernel(heads, batch_count, band_count, *refs),
         grid=(slots, heads),
         out_shape=shapes,
-        in_specs=[per_slot(frames, model)] + [whole_spec(c) for c in consts],
+        in_specs=[anywhere, anywhere] + [whole_spec(c) for c in consts],
         out_specs=specs,
-        scratch_shapes=[pltpu.VMEM((model, frames), F32)],
-        compiler_params=pltpu.CompilerParams(vmem_limit_bytes=VMEM_BYTES),
+        scratch_shapes=[
+            pltpu.VMEM((model, frames), F32),
+            pltpu.VMEM((slots, frames, model), BF16),
+            pltpu.VMEM((slots, frames, model), BF16),
+        ]
+        + [pltpu.VMEM(shape, BF16) for shape in own_flips]
+        + [dma, dma((slots,)), dma, dma, dma, dma, dma((slots + 2,))],
+        compiler_params=pltpu.CompilerParams(
+            vmem_limit_bytes=VMEM_BYTES, collective_id=0, has_side_effects=True
+        ),
         cost_estimate=cost(2.0e6 * 4 * slots * frames, 2 * slots * heads * frames * frames, 60e6),
         name="time_forward",
-    )(rows, *consts)
+    )(activations, cotangent, *consts)
 
 
 def ffn_backward(grad, act, slope, normed, middle, gain, w1_ref, w2_ref, dw1_ref, dw2t_ref, dg2_ref):
@@ -700,7 +894,7 @@
 
     grad = grad_ref[0].astype(F32).T
     d_middle = ffn_backward(
-        grad, act_ref[0], slope_ref[0], nf_ref[0], mid_ref[0], g2_ref[...], w1_ref, w2_ref, dw1_ref, dw2t_ref, dg2_ref
+        grad, act_ref[0], slope_ref[0], nf_ref[0], mid_ref[0], column(g2_ref), w1_ref, w2_ref, dw1_ref, dw2t_ref, dg2_ref
     )
     dmid_ref[0] = d_middle
     branch = d_middle.astype(BF16)
@@ -824,12 +1018,13 @@
         d_logit = jnp.concatenate([dlogit_ref[0], jnp.zeros_like(dlogit_ref[0])], axis=0).astype(BF16)
         dwp_ref[...] += dg(n_ref[0], dproj_ref[...], NT)
         dwg_ref[...] += dg(n_ref[0], d_logit, NT)[:, :heads]
+        gain = column(g1_ref)
 
         def block(i, carry):
             at = pl.ds(pl.multiple_of(i * BLOCK, BLOCK), BLOCK)
             logit = dlogit_ref[0, :, at].astype(BF16)
             d_normed = dg(wp_ref[...], dproj_ref[:, at], NN) + dg(wg_ref[...], logit, NN)
-            d_rows, terms = norm_backward(x_ref[0, at, :].astype(F32).T, g1_ref[...], d_normed)
+            d_rows, terms = norm_backward(x_ref[0, at, :].astype(F32).T, gain, d_normed)
             dg1_ref[...] += jnp.sum(terms, axis=1, keepdims=True)
             out_ref[0, at, :] = (dmid_ref[0, :, at] + d_rows).T.astype(BF16)
             return carry
@@ -879,6 +1074,8 @@
 
 def band_kernel(
     heads,
+    batch_count,
+    band_count,
     x_ref,
     cot_ref,
     mask_ref,
@@ -897,8 +1094,8 @@
     wo_ref,
     w1_ref,
     w2_ref,
-    y_ref,
-    dx_ref,
+    y_out,
+    dx_out,
     dwp_out,
     dw1_out,
     dw2_out,
@@ -925,12 +1122,67 @@
     dwg_ref,
     dg1_ref,
     dg2_ref,
+    xs_ref,
+    cots_ref,
+    ys_ref,
+    dxs_ref,
+    y_buf,
+    dx_buf,
+    y_send,
+    y_recv,
+    dx_send,
+    dx_recv,
+    local_sem,
 ):
     step = pl.program_id(0)
-    tokens, model = x_ref.shape
-    inner = q_ref.shape[0]
+    slot_count, part_frames, model = x_ref.shape
+    inner, tokens = q_ref.shape
     size = inner // heads
     groups = tokens // BLOCK
+    taken = tokens // slot_count
+    per_part = part_frames // taken
+    part = step // per_part
+    first = lax.rem(step, per_part) * taken
+    my_band, my_batch = lax.axis_index("band"), lax.axis_index("batch")
+    slot_dev = slot_count // band_count
+    slots = slot_dev // batch_count
+    part_at = pl.multiple_of(part * part_frames, part_frames)
+    own_at = pl.multiple_of(my_band * (y_out.shape[1] // band_count) + part * part_frames, part_frames)
+    own_chunk = my_batch * band_count + my_band
+    chunks = band_count * batch_count
+
+    columns = [slice(at, at + 128) for at in range(0, model, 128)]
+
+    def tokens_of(ref):
+        return jnp.concatenate(
+            [
+                jnp.concatenate(
+                    [ref[c, pl.ds(first + i, slot_count, stride=part_frames), :] for i in range(taken)], axis=0
+                ).T
+                for c in range(len(columns))
+            ],
+            axis=0,
+        )
+
+    def put_tokens(ref, values):
+        for c, at in enumerate(columns):
+            turned = values[at].T
+            for i in range(taken):
+                ref[c, pl.ds(first + i, slot_count, stride=part_frames), :] = turned[
+                    i * slot_count : (i + 1) * slot_count
+                ]
+
+    @pl.when(step == 0)
+    def enter():
+        greet_all(band_count, batch_count)
+
+    @pl.when(lax.rem(step, per_part) == 0)
+    def unpack():
+        for c, at in enumerate(columns):
+            xs_ref[c] = x_ref[:, :, at].astype(F32).reshape(xs_ref.shape[1:])
+            cots_ref[c] = cot_ref[:, :, at].astype(F32).reshape(cots_ref.shape[1:])
+
+    gain1, gain2 = column(g1_ref), column(g2_ref)
     sums_refs = (dwp_out, dw1_out, dw2_out, dwo_out, narrow_out)
 
     @pl.when(step == 0)
@@ -938,8 +1190,8 @@
         for ref in (dwp_ref, dw1_ref, dw2t_ref, dwot_ref, dwg_ref, dg1_ref, dg2_ref):
             ref[...] = jnp.zeros_like(ref)
 
-    rows = x_ref[...].astype(F32).T
-    normed = norm_forward(rows, g1_ref[...])
+    rows = tokens_of(xs_ref)
+    normed = norm_forward(rows, gain1)
     q_ref[...], k_ref[...], v_ref[...] = project_block(
         normed, wpt_ref, cos_ref[...], sin_ref[...], inner, LOG2E * size**-0.5
     )
@@ -965,13 +1217,13 @@
 
     lax.fori_loop(0, heads, attend, 0)
     middle = rows + dg(wot_ref[...], mixed_ref[...], NN)
-    normed_ffn = norm_forward(middle, g2_ref[...])
+    normed_ffn = norm_forward(middle, gain2)
 
     hidden = w1t_ref.shape[0]
-    part = hidden // 4
+    quarter = hidden // 4
 
     def expand(i, carry):
-        at = pl.ds(pl.multiple_of(i * part, part), part)
+        at = pl.ds(pl.multiple_of(i * quarter, quarter), quarter)
         active, slope = gelu_pair(dg(w1t_ref[at, :], normed_ffn, NN))
         act_ref[at, :] = active.astype(BF16)
         slope_ref[at, :] = slope.astype(BF16)
@@ -980,11 +1232,35 @@
     lax.fori_loop(0, 4, expand, 0)
     mask = mask_ref[0]
     result = (middle + dg(w2t_ref[...], act_ref[...], NN)) * mask
-    y_ref[...] = result.T.astype(BF16)
-
-    grad = cot_ref[...].astype(F32).T * mask
+    put_tokens(ys_ref, result)
+
+    @pl.when(lax.rem(step, per_part) == per_part - 1)
+    def send_rows():
+        for c, at in enumerate(columns):
+            y_buf[part, :, :, at] = ys_ref[c].reshape(slot_count, part_frames, 128).astype(BF16)
+
+        def give(i, carry):
+            other = lax.rem(my_band + i, band_count)
+            send(
+                y_buf.at[part, pl.ds(other * slot_dev, slot_dev)],
+                y_out.at[:, pl.ds(own_at, part_frames)],
+                y_send,
+                y_recv,
+                other,
+                my_batch,
+            )
+            return carry
+
+        lax.fori_loop(1, band_count, give, 0)
+        pltpu.make_async_copy(
+            y_buf.at[part, pl.ds(my_band * slot_dev, slot_dev)],
+            y_out.at[:, pl.ds(own_at, part_frames)],
+            local_sem.at[0],
+        ).start()
+
+    grad = tokens_of(cots_ref) * mask
     d_middle = ffn_backward(
-        grad, act_ref[...], slope_ref[...], normed_ffn, middle, g2_ref[...], w1_ref, w2_ref, dw1_ref, dw2t_ref, dg2_ref
+        grad, act_ref[...], slope_ref[...], normed_ffn, middle, gain2, w1_ref, w2_ref, dw1_ref, dw2t_ref, dg2_ref
     )
     branch = d_middle.astype(BF16)
     dwot_ref[...] += dg(branch, mixed_ref[...], NT)
@@ -1019,9 +1295,36 @@
     dwp_ref[...] += dg(normed, dproj_ref[...], NT)
     dwg_ref[...] += dg(normed, d_logit, NT)[:, :heads]
     d_normed = dg(wp_ref[...], dproj_ref[...], NN) + dg(wg_ref[...], dlogit_ref[...].astype(BF16), NN)
-    d_rows, terms = norm_backward(rows, g1_ref[...], d_normed)
+    d_rows, terms = norm_backward(rows, gain1, d_normed)
     dg1_ref[...] += jnp.sum(terms, axis=1, keepdims=True)
-    dx_ref[...] = (d_middle + d_rows).T.astype(BF16)
+    put_tokens(dxs_ref, d_middle + d_rows)
+
+    @pl.when(lax.rem(step, per_part) == per_part - 1)
+    def send_grads():
+        for c, at in enumerate(columns):
+            dx_buf[part, :, :, at] = dxs_ref[c].reshape(slot_count, part_frames, 128).astype(BF16)
+
+        def give(i, carry):
+            other = lax.rem(my_band * batch_count + my_batch + i, chunks)
+            band, batch = other // batch_count, lax.rem(other, batch_count)
+            for j in range(slots):
+                send(
+                    dx_buf.at[part, band * slot_dev + batch_count * j + batch],
+                    dx_out.at[j * chunks + own_chunk, pl.ds(part_at, part_frames)],
+                    dx_send,
+                    dx_recv,
+                    band,
+                    batch,
+                )
+            return carry
+
+        lax.fori_loop(1, chunks, give, 0)
+        for j in range(slots):
+            pltpu.make_async_copy(
+                dx_buf.at[part, my_band * slot_dev + batch_count * j + my_batch],
+                dx_out.at[j * chunks + own_chunk, pl.ds(part_at, part_frames)],
+                local_sem.at[1],
+            ).start()
 
     @pl.when(step == pl.num_programs(0) - 1)
     def finish():
@@ -1029,28 +1332,41 @@
             sums_refs,
             ((dwp_ref, False), (dw1_ref, False), (dw2t_ref, True), (dwot_ref, True), dwg_ref, dg1_ref, dg2_ref),
         )
-
-
-def band_layer(x, cot, mask, bias, cos, sin, params, turned):
+        piece = y_out.shape[1] // band_count
+        await_bytes(y_out.at[:, pl.ds(0, piece)], local_sem.at[0])
+        await_bytes(dx_out.at[pl.ds(0, slots)], local_sem.at[1])
+        for sem in (y_send, y_recv):
+            await_bytes(y_out.at[:, pl.ds(0, piece * (band_count - 1))], sem)
+        for sem in (dx_send, dx_recv):
+            await_bytes(dx_out.at[pl.ds(0, slots * (chunks - 1))], sem)
+
+
+def band_layer(rows, cot, mask, bias, cos, sin, params, flips, band_count, batch_count):
     prenorm, project, gating, output_weight, midnorm, expand, shrink = params
-    wpt, wgt, wot, w1t, w2t, g1, g2 = turned
-    total, model = x.shape
+    slot_count, piece, model = rows.shape
     steps, _, tokens = mask.shape
     heads, inner, hidden = gating.shape[1], output_weight.shape[0], expand.shape[1]
     groups = tokens // BLOCK
-    consts = (bias, cos, sin, g1, g2, wpt, wgt, wot, w1t, w2t, project, gating, output_weight, expand, shrink)
+    taken = tokens // slot_count
+    part_frames = 16
+    per_part = part_frames // taken
+    parts = piece // part_frames
+    slot_dev = slot_count // band_count
+    consts = (bias, cos, sin, prenorm, midnorm) + flips + (project, gating, output_weight, expand, shrink)
     sums = ((model, 3 * inner), (model, hidden), (hidden, model), (inner, model), (model, 128))
-    rows = pl.BlockSpec((tokens, model), lambda i: (i, 0))
+    blocks = pl.BlockSpec((slot_count, part_frames, model), lambda i: (0, i // per_part, 0))
+    anywhere = pl.BlockSpec(memory_space=pl.ANY)
+    dma = pltpu.SemaphoreType.DMA
     return pl.pallas_call(
-        lambda *refs: band_kernel(heads, *refs),
+        lambda *refs: band_kernel(heads, batch_count, band_count, *refs),
         grid=(steps,),
         out_shape=[
-            jax.ShapeDtypeStruct((total, model), BF16),
-            jax.ShapeDtypeStruct((total, model), BF16),
+            jax.ShapeDtypeStruct((slot_dev, piece * band_count, model), BF16),
+            jax.ShapeDtypeStruct((slot_count, piece, model), BF16),
         ]
         + sum_shapes(*sums),
-        in_specs=[rows, rows, pl.BlockSpec((1, 1, tokens), lambda i: (i, 0, 0))] + [whole_spec(c) for c in consts],
-        out_specs=[rows, rows] + sum_specs(*sums),
+        in_specs=[blocks, blocks, pl.BlockSpec((1, 1, tokens), lambda i: (i, 0, 0))] + [whole_spec(c) for c in consts],
+        out_specs=[anywhere, anywhere] + sum_specs(*sums),
         scratch_shapes=[
             pltpu.VMEM((inner, tokens), BF16),
             pltpu.VMEM((inner, tokens), BF16),
@@ -1073,24 +1389,24 @@
             pltpu.VMEM((model, heads), F32),
             pltpu.VMEM((model, 1), F32),
             pltpu.VMEM((model, 1), F32),
+            pltpu.VMEM((model // 128, slot_count * part_frames, 128), F32),
+            pltpu.VMEM((model // 128, slot_count * part_frames, 128), F32),
+            pltpu.VMEM((model // 128, slot_count * part_frames, 128), F32),
+            pltpu.VMEM((model // 128, slot_count * part_frames, 128), F32),
+            pltpu.VMEM((parts, slot_count, part_frames, model), BF16),
+            pltpu.VMEM((parts, slot_count, part_frames, model), BF16),
+            dma,
+            dma,
+            dma,
+            dma,
+            dma((2,)),
         ],
-        compiler_params=pltpu.CompilerParams(vmem_limit_bytes=VMEM_BYTES),
-        cost_estimate=cost(30.0e6 * total, 0, 60e6),
+        compiler_params=pltpu.CompilerParams(
+            vmem_limit_bytes=VMEM_BYTES, collective_id=1, has_side_effects=True
+        ),
+        cost_estimate=cost(30.0e6 * slot_count * piece, 0, 60e6),
         name="band_layer",
-    )(x, cot, mask, *consts)
-
-
-def turned_params(params):
-    prenorm, project, gating, output_weight, midnorm, expand, shrink = params
-    return (
-        project.T,
-        gating.T,
-        output_weight.T,
-        expand.T,
-        shrink.T,
-        prenorm.astype(F32)[:, None],
-        midnorm.astype(F32)[:, None],
-    )
+    )(rows, cot, mask, *consts)
 
 
 def slot_shards(activations, cotangent, frame_counts, slot_bands, *weights):
@@ -1100,6 +1416,7 @@
     frames = frame_dev * batch
     piece = frame_dev // band
     slots = slot_dev // batch
+    weights = tuple(w[None] if w.ndim == 1 else w for w in weights)
     time_params, band_params = weights[:7], weights[7:]
     heads, inner, hidden = time_params[2].shape[1], time_params[3].shape[0], time_params[5].shape[1]
     size = inner // heads
@@ -1121,52 +1438,40 @@
     mask = ((own_frames < frame_counts[0])[:, None] & slot_valid[None, :]).astype(F32)
     mask = mask.reshape(piece * slot_count // tokens, 1, tokens)
 
-    time_turned = turned_params(time_params)
-    band_turned = turned_params(band_params)
-    rows = lax.all_to_all(
-        activations.reshape(slot_dev, frame_dev, model), "batch", split_axis=0, concat_axis=1, tiled=True
-    )
-    cot_rows = lax.all_to_all(
-        cotangent.reshape(slot_dev, frame_dev, model), "band", split_axis=1, concat_axis=0, tiled=True
-    )
-    cot_rows = cot_rows.transpose(1, 0, 2).reshape(piece * slot_count, model)
-    wpt, wgt, wot, w1t, w2t, g1, g2 = time_turned
-    result, n, q, k, v, p, linv, gate, att, mixed, mid, nf, act, slope = time_forward(
-        rows, time_bias, time_cos.T, time_sin.T, g1, g2, wpt, wgt, wot, w1t, w2t
-    )
-    result = result.reshape(slots, batch, band, piece, model).transpose(0, 2, 1, 3, 4)
-    frame_rows = lax.all_to_all(
-        result.reshape(slots, frames, model), ("band", "batch"), split_axis=1, concat_axis=0, tiled=True
-    )
-    frame_rows = frame_rows.transpose(1, 0, 2).reshape(piece * slot_count, model)
-    y, dx, *band_sums = band_layer(
-        frame_rows,
-        cot_rows,
+    band_rows, band_cot, rows, n, q, k, v, p, linv, gate, att, mixed, mid, nf, act, slope, *flips = time_forward(
+        activations.reshape(slot_dev, frame_dev, model),
+        cotangent.reshape(slot_dev, frame_dev, model),
+        time_bias,
+        time_cos.T,
+        time_sin.T,
+        time_params,
+        band_params,
+        band,
+        batch,
+    )
+    layer_output, slot_grad, *band_sums = band_layer(
+        band_rows,
+        band_cot,
         mask,
         band_bias,
         jnp.tile(band_cos.T, (1, copies)),
         jnp.tile(band_sin.T, (1, copies)),
         band_params,
-        band_turned,
-    )
-    band_sums = lax.psum(band_sums, ("band", "batch"))
-    dx = dx.reshape(piece, slot_count, model).transpose(1, 0, 2)
-    slot_grad = lax.all_to_all(dx, ("band", "batch"), split_axis=0, concat_axis=1, tiled=True)
-    slot_grad = slot_grad.reshape(slots, band, batch, piece, model).transpose(0, 2, 1, 3, 4)
+        tuple(flips),
+        band,
+        batch,
+    )
     slot_grad = slot_grad.reshape(slots, frames, model)
-    y = y.reshape(piece, slot_count, model).transpose(1, 0, 2)
-    layer_output = lax.all_to_all(y, "band", split_axis=0, concat_axis=1, tiled=True)
+    g1, g2 = time_params[0], time_params[4]
     dmid, datt, minus, dlogit, *ffn_sums = time_ffn_backward(
         slot_grad, act, slope, nf, mid, mixed, att, gate, linv, g2, time_params[5], time_params[6], time_params[3]
     )
-    ffn_sums, band_sums = lax.optimization_barrier((ffn_sums, band_sums))
-    ffn_sums = lax.psum(ffn_sums, ("band", "batch"))
     grads, *attn_sums = time_attention_backward(
         p, q, k, v, datt, minus, dlogit, n, rows, dmid, time_cos.T, time_sin.T, g1, time_params[1], time_params[2]
     )
     input_grad = lax.all_to_all(grads, "batch", split_axis=1, concat_axis=0, tiled=True)
-    attn_sums, ffn_sums = lax.optimization_barrier((attn_sums, ffn_sums))
-    attn_sums = lax.psum(attn_sums, ("band", "batch"))
+    input_grad = input_grad.reshape(batch, slots, frame_dev, model).transpose(1, 0, 2, 3)
+    attn_sums, ffn_sums, band_sums = lax.psum((attn_sums, ffn_sums, band_sums), ("band", "batch"))
 
     dwp, attn_narrow = (part.astype(F32) for part in attn_sums)
     dw1, dw2, dwo, ffn_narrow = (part.astype(F32) for part in ffn_sums)
@@ -1197,9 +1502,10 @@
     fits = (
         clips == 1
         and slot_dev % batch == 0
-        and frame_dev % band == 0
-        and (frame_dev * batch) % (2 * BLOCK) == 0
-        and BLOCK % slot_bands.shape[0] == 0
+        and frame_dev == BLOCK
+        and frame_dev % (16 * band) == 0
+        and slot_bands.shape[0] == 64
+        and activations.shape[-1] % 128 == 0
         and (frame_dev // band * slot_bands.shape[0]) % (2 * BLOCK) == 0
         and weights[2].shape[1] == 8
     )

time: 765 us -> 546 us (0.71); the launches traced: 757 us -> 545 us
  waiting for transfers between devices: 393 us -> 185 us
  Pallas kernels: 245 us -> 301 us
  local copies, waits for them, and re-layouts: 54.5 us -> 19.7 us
  starting transfers between devices: 28.4 us -> 3.6 us
    psum x3 -> x1, waiting for transfers between devices: 310 us -> 151 us  [slot_shards(): lax.psum((attn_sums, ffn_sums, band_sums), ('band', 'batch'))]
    all_to_all x5 -> x0, waiting for transfers between devices: 81.8 us -> none  [the longest x1 45.2 us: slot_shards(): lax.all_to_all(dx, ('band', 'batch'), split_axis=0, concat_axis=1, tiled=...]
    pallas_call x2, Pallas kernels: 168 us -> 223 us  [the longest x1 130 us: band_layer(): pl.pallas_call(lambda *refs: band_kernel(heads, batch_count, band_count,...]
    all_to_all x1, waiting for transfers between devices: 0.01 us -> 34.2 us  [slot_shards(): lax.all_to_all(grads, 'batch', split_axis=1, concat_axis=0, tiled=True)]
    all_to_all x5 -> x0, starting transfers between devices: 24.5 us -> none  [the longest x1 6.74 us: slot_shards(): lax.all_to_all(cotangent.reshape(slot_dev, frame_dev, model), 'band', spl...]
    unnamed x49 -> x25, local copies, waits for them, and re-layouts: 21.7 us -> 7.05 us
    reshape x4 -> x0, local copies, waits for them, and re-layouts: 9.95 us -> none  [the longest x1 3.47 us: slot_shards(): dx = dx.reshape(piece, slot_count, model).transpose(1, 0, 2)]
  transfers between devices with their start and end apart: 9 -> 2, of which waited for: 6 -> 2; matrix products, arithmetic and copies ran while one was open for 8% -> 1% of each run, Pallas kernels for 20% -> 0%
where the time goes in v3:
time: 546 us; the launch traced here: 545 us
  Pallas kernels  301 us (55%)
  waiting for transfers between devices  185 us (34%)
  other arithmetic  21.9 us (4%)
  local copies, waits for them, and re-layouts  19.7 us (4%)
  between operations  14.8 us (3%)
    psum x1, waiting for transfers between devices, slot_shards(): lax.psum((attn_sums, ffn_sums, band_sums), ('band', 'batch'))  151 us
    pallas_call x1, Pallas kernels, band_layer(): pl.pallas_call(lambda *refs: band_kernel(heads, batch_count, band_count,...  130 us
    pallas_call x1, Pallas kernels, time_forward(): pl.pallas_call(lambda *refs: time_forward_kernel(heads, batch_count, band...  92.7 us
    pallas_call x1, Pallas kernels, time_attention_backward(): pl.pallas_call(lambda *refs: time_attention_backward_kernel(heads, *refs)...  54.1 us
    all_to_all x1, waiting for transfers between devices, slot_shards(): lax.all_to_all(grads, 'batch', split_axis=1, concat_axis=0, tiled=True)  34.2 us
    pallas_call x1, Pallas kernels, time_ffn_backward(): pl.pallas_call(lambda *refs: time_ffn_backward_kernel(heads, *refs), grid...  23.9 us
  transfers between devices with their start and end apart: 2, of which 2 were waited for; matrix products, arithmetic and copies ran while one was open for 1% of the time, Pallas kernels for 0%

profile of v3, /device:TPU:0, one launch (start us, length us, event | category | flops | bytes accessed | tf_op | source)
XLA Modules:
  0.0 545.4 jit_solution(1662861801464833056)
XLA Ops:
  9.4 1.2 broadcast_in_dim.40.refs_5_.refs_12_
  10.7 1.2 broadcast_in_dim.41.refs_6_.refs_9_
  11.9 1.2 broadcast_in_dim.44.refs_6_
  13.1 1.2 broadcast_in_dim.45.refs_7_
  15.2 1.5 copy.60.refs_8_.refs_14_
  16.6 1.5 copy.61.refs_13_.refs_14_
  19.7 1.2 multiply_sine_fusion
  22.4 92.7 %time_forward.1 = (bf16[64,32,384]{2,1,0:T(8,128)(2,1)}, bf16[64,32,384]{2,1,0:T(8,128)(2,1)}, bf16[2,1024,384]{2,1,0:T(8,128)(2,1)}, bf16[2,384,1024]{2,1,0:T(8...) custom-call(bf16[8,256,384]{2,1,0:T(8,128)(2,1)} %bitcast.16, ...), custom_call_target="tpu_custom_call" | custom-call | flops 16384000000 | bytes 60000000 | tf_op jit(solution)/shard_map/time_forward/pallas_call | solution.py:809
  115.2 129.9 %band_layer.1 = (bf16[8,256,384]{2,1,0:T(8,128)(2,1)}, bf16[64,32,384]{2,1,0:T(8,128)(2,1)}, bf16[384,1536]{1,0:T(8,128)(2,1)}, bf16[384,1536]{1,0:T(8,128)(2,1)...) custom-call(bf16[64,32,384]{2,1,0:T(8,128)(2,1)} %get-tuple-element.55.refs_0_, ...), custom_call_target="tpu_custom_call" | custom-call | flops 61440000000 | bytes 60000000 | tf_op jit(solution)/shard_map/band_layer/pallas_call | solution.py:1360
  245.1 23.9 %time_ffn_backward.1 = (f32[2,384,1024]{2,1,0:T(8,128)}, bf16[2,512,1024]{2,1,0:T(8,128)(2,1)}, f32[2,8,1024]{2,1,0:T(8,128)}, f32[2,8,1024]{2,1,0:T(8,128)}, bf...) custom-call(bf16[2,1024,384]{2,1,0:T(8,128)(2,1)} %bitcast.18, ...), custom_call_target="tpu_custom_call" | custom-call | flops 16384000000 | bytes 30000000 | tf_op jit(solution)/shard_map/time_ffn_backward/pallas_call | solution.py:942
  269.0 54.1 %time_attention_backward.1 = (bf16[2,1024,384]{2,1,0:T(8,128)(2,1)}, bf16[384,1536]{1,0:T(8,128)(2,1)}, bf16[384,128]{1,0:T(8,128)(2,1)}) custom-call(bf16[2,8,1024,1024]{3,2,1,0:T(8,128)(2,1)} %get-tuple-element.63.refs_0_, bf16[2,512,1024]{2,1,0:T(8,128)(2,1)} %get-tuple-element.64.refs_1_, bf16[2,512,1024]{2,1,0:T(8,128)(2,1)} %get-tuple-element.65.refs_2_, ...), custom_call_target="tpu_custom_call" | custom-call | flops 40960000000 | bytes 60000000 | tf_op jit(solution)/shard_map/time_attention_backward/pallas_call | solution.py:1049
  323.1 1.4 copy-done.1
  324.5 2.8 copy.65
  327.3 3.6 all-to-all-start
  330.8 34.2 %all-to-all-done = bf16[2,1024,384]{2,0,1:T(2,128)(2,1)S(1)} async-done(((bf16[2,1024,384]{2,0,1:T(2,128)(2,1)}), bf16[2,1024,384]{2,0,1:T(2,128)(2,1)S(1)}, u32[]{:S(2)}, u32[]{:S(2)}) %all-to-all-start) | async-done | bytes 1572896 | tf_op jit(solution)/shard_map/all_to_all | solution.py:1472
  365.2 1.9 convert.4
  367.1 150.5 %all-reduce.3.cloned.1.call-done = (bf16[384,128]{1,0:T(8,128)(2,1)}, bf16[384,1536]{1,0:T(8,128)(2,1)}, bf16[512,384]{1,0:T(8,128)(2,1)}, bf16[384,128]{1,0:T(8...) async-done(((bf16[384,128]{1,0:T(8,128)(2,1)}, ...) | async-done | bytes 8159248 | tf_op jit(solution)/shard_map/psum | solution.py:1474
  521.5 1.6 convert_reduce_fusion
  526.4 1.7 convert_element_type.74
  528.1 1.7 convert_element_type.76
  529.8 1.6 convert_element_type.77
  531.5 1.7 convert_element_type.79
  533.2 1.7 convert_element_type.81
  534.9 1.6 convert_element_type.82
  (52 shorter events, 15.0 us)
Async XLA Ops:
  7.2 510.5 %all-reduce.3.cloned.1.call-start = ((), (), s32[]{:S(2)}) async-start(), calls=%async_computation.1 | async-start | bytes 16318464 | tf_op jit(solution)/shard_map/psum | solution.py:1474
  323.1 1.4 copy-start.1
  327.3 37.8 %all-to-all-start = ((bf16[2,1024,384]{2,0,1:T(2,128)(2,1)}), bf16[2,1024,384]{2,0,1:T(2,128)(2,1)S(1)}, u32[]{:S(2)}, u32[]{:S(2)}) async-start(bf16[2,1024,384]{2,0,1:T(2,128)(2,1)} %copy.65), calls=%async_computation | async-start | bytes 3145728 | tf_op jit(solution)/shard_map/all_to_all | solution.py:1472
  517.7 6.8 %copy-start.9 = (bf16[512,384]{1,0:T(8,128)(2,1)S(1)}, bf16[512,384]{1,0:T(8,128)(2,1)}, u32[]{:S(2)}) copy-start(bf16[512,384]{1,0:T(8,128)(2,1)} %get-tuple-element.162) | copy-start | bytes 1179652
  517.7 7.7 %copy-start.8 = (bf16[512,384]{1,0:T(8,128)(2,1)S(1)}, bf16[512,384]{1,0:T(8,128)(2,1)}, u32[]{:S(2)}) copy-start(bf16[512,384]{1,0:T(8,128)(2,1)} %get-tuple-element.168) | copy-start | bytes 1179652
  520.5 5.9 %copy-start.7 = (bf16[384,1536]{1,0:T(8,128)(2,1)S(1)}, bf16[384,1536]{1,0:T(8,128)(2,1)}, u32[]{:S(2)}) copy-start(bf16[384,1536]{1,0:T(8,128)(2,1)} %get-tuple-element.161) | copy-start | bytes 3538948
  526.4 1.7 copy-start.6
  528.1 1.7 copy-start.5
  529.8 1.7 copy-start.4
  531.5 1.7 copy-start.3
  533.2 1.7 copy-start.2
  534.9 2.6 copy-start
Sparse Core Ops, SparseCore 0:
  323.3 194.3 all-reduce.2

commit v4 on v3

--- a/solution.py
+++ b/solution.py
@@ -522,6 +522,138 @@
 
 def await_bytes(ref, sem):
     pltpu.make_async_copy(ref, ref, sem).wait()
+
+
+class Place:
+    def __init__(self):
+        self.band, self.batch = lax.axis_index("band"), lax.axis_index("batch")
+        self.bits = {
+            "core": lax.rem(self.batch, 2),
+            "x": self.batch // 2,
+            "y": lax.rem(self.band, 2),
+        }
+        self.z = self.band // 2
+
+    def across(self, axis):
+        bit = self.bits[axis]
+        if axis == "core":
+            return self.band, self.batch + 1 - 2 * bit
+        if axis == "x":
+            return self.band, self.batch + 2 - 4 * bit
+        return self.band + 1 - 2 * bit, self.batch
+
+    def along_z(self, step):
+        other = lax.rem(self.z + step, Z_COUNT)
+        return other, (other * 2 + self.bits["y"], self.batch)
+
+
+Z_COUNT = 4
+
+
+def greet(others):
+    barrier = pltpu.get_barrier_semaphore()
+    for other in others:
+        pl.semaphore_signal(barrier, inc=1, device_id=other, device_id_type=pl.DeviceIdType.MESH)
+    pl.semaphore_wait(barrier, len(others))
+
+
+class Total:
+    def __init__(self, place, order, sends, recvs):
+        self.place = place
+        self.order = order
+        self.sends, self.recvs = sends, recvs
+        self.core = place.bits["core"]
+        self.first, self.second = (place.bits[axis] for axis in order)
+
+    def give(self, step, source, target, other):
+        send(source, target, self.sends.at[step], self.recvs.at[step], *other)
+
+    def took(self, step, ref):
+        await_bytes(ref, self.recvs.at[step])
+        await_bytes(ref, self.sends.at[step])
+
+    def add(self, ref, rows, part):
+        ref[rows] = (ref[rows].astype(F32) + part.astype(F32)).astype(BF16)
+
+    def start_core(self, source, recv):
+        self.give(0, source.at[1 - self.core], recv, self.place.across("core"))
+
+    def end_core(self, held, recv):
+        self.took(0, recv)
+        held[...] = (held[...].astype(F32) + recv[...].astype(F32)).astype(BF16)
+
+    def half_rows(self, held, level):
+        rows = held.shape[0] // 2
+        base = 0
+        if level == 2:
+            base, rows = self.first * rows, rows // 2
+        bit = self.first if level == 1 else self.second
+        keep = pl.ds(pl.multiple_of(base + bit * rows, rows), rows)
+        away = pl.ds(pl.multiple_of(base + (1 - bit) * rows, rows), rows)
+        return keep, away
+
+    def start_half(self, level, held, recv):
+        away = self.half_rows(held, level)[1]
+        self.give(level, held.at[away], recv, self.place.across(self.order[level - 1]))
+
+    def end_half(self, level, held, recv):
+        self.took(level, recv)
+        self.add(held, self.half_rows(held, level)[0], recv[...])
+
+    def start_z(self, piece, recv):
+        width = recv.shape[2]
+        for step in range(1, Z_COUNT):
+            index, other = self.place.along_z(step)
+            lanes = pl.ds(pl.multiple_of(index * width, 128), width)
+            self.give(3, piece.at[:, lanes], recv.at[step - 1], other)
+
+    def z_lanes(self, width):
+        return pl.ds(pl.multiple_of(self.place.z * width, 128), width)
+
+    def end_z(self, piece, recv):
+        self.took(3, recv)
+        lanes = self.z_lanes(recv.shape[2])
+        sums = piece[:, lanes].astype(F32)
+        for step in range(Z_COUNT - 1):
+            sums = sums + recv[step].astype(F32)
+        piece[:, lanes] = sums.astype(BF16)
+
+    def own_copy(self, piece, target, width, sem):
+        lanes = self.z_lanes(width)
+        return pltpu.make_async_copy(piece.at[:, lanes], target.at[:, lanes], sem)
+
+    def start_z_back(self, piece, target, width, sem):
+        lanes = self.z_lanes(width)
+        for step in range(1, Z_COUNT):
+            _, other = self.place.along_z(step)
+            self.give(4, piece.at[:, lanes], target.at[:, lanes], other)
+        self.own_copy(piece, target, width, sem).start()
+
+    def end_z_back(self, piece, target, width, sem):
+        self.took(4, target.at[:, pl.ds(0, (Z_COUNT - 1) * width)])
+        self.own_copy(piece, target, width, sem).wait()
+
+    def back_rows(self, out, level):
+        rows = out.shape[0] // 2
+        base = self.core * rows
+        if level >= 1:
+            rows = rows // 2
+            base = base + self.first * rows
+        if level >= 2:
+            rows = rows // 2
+            base = base + self.second * rows
+        return pl.ds(pl.multiple_of(base, rows), rows)
+
+    def start_back(self, level, out, source=None):
+        rows = self.back_rows(out, level)
+        axis = "core" if level == 0 else self.order[level - 1]
+        self.give(7 - level, out.at[rows] if source is None else source, out.at[rows], self.place.across(axis))
+
+    def end_back(self, level, out):
+        self.took(7 - level, out.at[self.back_rows(out, level)])
+
+
+TOTAL_STEPS = 8
 
 
 def time_forward_kernel(
@@ -745,14 +877,6 @@
         await_bytes(band_rows.at[pl.ds(0, others)], result_recv)
 
 
-def sum_shapes(*shapes):
-    return [jax.ShapeDtypeStruct(shape, BF16) for shape in shapes]
-
-
-def sum_specs(*shapes):
-    return [pl.BlockSpec(shape, lambda *ids: (0, 0)) for shape in shapes]
-
-
 def cost(flops, exps=0, moved=0):
     return pl.CostEstimate(flops=int(flops), bytes_accessed=int(moved), transcendentals=int(exps))
 
@@ -863,6 +987,7 @@
 
 def time_ffn_backward_kernel(
     heads,
+    orders,
     grad_ref,
     act_ref,
     slope_ref,
@@ -876,13 +1001,26 @@
     w1_ref,
     w2_ref,
     wo_ref,
+    part_refs,
     dmid_ref,
     datt_ref,
     minus_ref,
     dlogit_ref,
-    *refs,
+    sums_refs,
+    dg2_out,
+    region_refs,
+    dw1_ref,
+    dw2t_ref,
+    dwot_ref,
+    dg2_ref,
+    piece_refs,
+    z_recvs,
+    sends,
+    recvs,
+    local_sem,
 ):
-    sums_refs, (dw1_ref, dw2t_ref, dwot_ref, dg2_ref) = refs[:4], refs[4:]
+    place = Place()
+    totals = [Total(place, order, sends.at[i], recvs.at[i]) for i, order in enumerate(orders)]
     step = pl.program_id(0) * pl.num_programs(1) + pl.program_id(1)
     last = pl.num_programs(0) * pl.num_programs(1) - 1
     size = wo_ref.shape[0] // heads
@@ -891,6 +1029,16 @@
     def clear():
         for ref in (dw1_ref, dw2t_ref, dwot_ref, dg2_ref):
             ref[...] = jnp.zeros_like(ref)
+        greet([place.along_z(i)[1] for i in range(1, Z_COUNT)])
+        for total, part, piece, recv in zip(totals, part_refs, piece_refs, z_recvs):
+            piece[...] = part[...]
+            total.start_z(piece, recv)
+
+    @pl.when(step == last // 2 + 1)
+    def gather():
+        for i, (total, piece, recv, region) in enumerate(zip(totals, piece_refs, z_recvs, region_refs)):
+            total.end_z(piece, recv)
+            total.start_z_back(piece, region, recv.shape[2], local_sem.at[i])
 
     grad = grad_ref[0].astype(F32).T
     d_middle = ffn_backward(
@@ -914,21 +1062,30 @@
 
     @pl.when(step == last)
     def finish():
-        finish_sums(sums_refs, ((dw1_ref, False), (dw2t_ref, True), (dwot_ref, True), dg2_ref))
-
-
-def finish_sums(outs, parts):
-    narrow = []
-    for out_ref, (ref, flipped) in zip(outs[:-1], parts):
-        out_ref[...] = (ref[...].T if flipped else ref[...]).astype(BF16)
-    for ref in parts[len(outs) - 1 :]:
-        narrow.append(ref[...])
-    used = sum(part.shape[1] for part in narrow)
-    narrow.append(jnp.zeros((outs[-1].shape[0], 128 - used), F32))
-    outs[-1][...] = jnp.concatenate(narrow, axis=1).astype(BF16)
-
-
-def time_ffn_backward(grad, act, slope, nf, mid, mixed, att, gate, linv, g2, w1, w2, wo):
+        first, second = sums_refs
+        lay_halves(first, 0, dw1_ref)
+        lay_halves(first, dw1_ref.shape[1], dwot_ref)
+        lay_halves(second, 0, dw2t_ref)
+        dg2_out[...] = dg2_ref[...]
+        for i, (total, piece, recv, region) in enumerate(zip(totals, piece_refs, z_recvs, region_refs)):
+            total.end_z_back(piece, region, recv.shape[2], local_sem.at[i])
+
+
+def narrow_tile(parts, rows):
+    used = sum(part.shape[1] for part in parts)
+    return jnp.concatenate(list(parts) + [jnp.zeros((rows, 128 - used), F32)], axis=1)
+
+
+def lay_halves(target, at, ref):
+    rows, width = ref.shape
+    for half in range(2):
+        target[half, :, at : at + width] = ref[half * rows // 2 : (half + 1) * rows // 2].astype(BF16)
+
+
+ORDERS = (("x", "y"), ("y", "x"))
+
+
+def time_ffn_backward(grad, act, slope, nf, mid, mixed, att, gate, linv, g2, w1, w2, wo, parts):
     slots, frames, model = grad.shape
     heads = gate.shape[1]
     inner, hidden = wo.shape[0], w1.shape[1]
@@ -937,139 +1094,531 @@
     def cut(rows):
         return pl.BlockSpec((1, rows, tokens), lambda s, c: (s, 0, c))
 
+    def whole(*shape):
+        return pl.BlockSpec(shape, lambda s, c: (0,) * len(shape))
+
     consts = (g2, w1, w2, wo)
-    sums = ((model, hidden), (hidden, model), (inner, model), (model, 128))
+    anywhere = pl.BlockSpec(memory_space=pl.ANY)
+    halves = [(2, model // 2, hidden + inner), (2, model // 2, hidden)]
+    eighth = parts[0].shape[0]
+    widths = [part.shape[1] for part in parts]
+    dma = pltpu.SemaphoreType.DMA
     return pl.pallas_call(
-        lambda *refs: time_ffn_backward_kernel(heads, *refs),
+        lambda *refs: time_ffn_backward_kernel(heads, ORDERS, *refs),
         grid=(slots, frames // tokens),
-        out_shape=[
+        out_shape=(
             jax.ShapeDtypeStruct((slots, model, frames), F32),
             jax.ShapeDtypeStruct((slots, inner, frames), BF16),
             jax.ShapeDtypeStruct((slots, heads, frames), F32),
             jax.ShapeDtypeStruct((slots, heads, frames), F32),
-        ]
-        + sum_shapes(*sums),
+            [jax.ShapeDtypeStruct(shape, BF16) for shape in halves],
+            jax.ShapeDtypeStruct((model, 1), F32),
+            [jax.ShapeDtypeStruct(part.shape, BF16) for part in parts],
+        ),
         in_specs=[pl.BlockSpec((1, tokens, model), lambda s, c: (s, c, 0))]
         + [cut(a.shape[1]) for a in (act, slope, nf, mid, mixed, att, gate, linv)]
-        + [whole_spec(c) for c in consts],
-        out_specs=[cut(model), cut(inner), cut(heads), cut(heads)] + sum_specs(*sums),
+        + [whole_spec(c) for c in consts]
+        + [[whole_spec(part) for part in parts]],
+        out_specs=(
+            cut(model),
+            cut(inner),
+            cut(heads),
+            cut(heads),
+            [whole(*shape) for shape in halves],
+            whole(model, 1),
+            [anywhere for _ in parts],
+        ),
         scratch_shapes=[
             pltpu.VMEM((model, hidden), F32),
             pltpu.VMEM((model, hidden), F32),
             pltpu.VMEM((model, inner), F32),
             pltpu.VMEM((model, 1), F32),
+            [pltpu.VMEM((eighth, width), BF16) for width in widths],
+            [pltpu.VMEM((Z_COUNT - 1, eighth, width // Z_COUNT), BF16) for width in widths],
+            dma((len(parts), TOTAL_STEPS)),
+            dma((len(parts), TOTAL_STEPS)),
+            dma((len(parts),)),
         ],
-        compiler_params=pltpu.CompilerParams(vmem_limit_bytes=VMEM_BYTES),
+        compiler_params=pltpu.CompilerParams(
+            vmem_limit_bytes=VMEM_BYTES, collective_id=2, has_side_effects=True
+        ),
         cost_estimate=cost(8.0e6 * slots * frames, 0, 30e6),
         name="time_ffn_backward",
-    )(grad, act, slope, nf, mid, mixed, att, gate, linv, *consts)
+    )(grad, act, slope, nf, mid, mixed, att, gate, linv, *consts, list(parts))
 
 
 def time_attention_backward_kernel(
     heads,
+    slots,
+    batch_count,
     p_ref,
     q_ref,
     k_ref,
     v_ref,
     datt_ref,
     minus_ref,
-    dlogit_ref,
-    n_ref,
     x_ref,
     dmid_ref,
+    logit_block_ref,
+    n_ref,
+    dlogit_ref,
     cos_ref,
     sin_ref,
     g1_ref,
     wp_ref,
     wg_ref,
-    out_ref,
-    *refs,
+    narrow_ref,
+    dg2_ref,
+    region_refs,
+    ffn_refs,
+    grad_out,
+    band_outs,
+    ffn_outs,
+    pair_outs,
+    dproj_ref,
+    wp_turned_ref,
+    grad_buf,
+    held_refs,
+    ffn_recvs,
+    pair_refs,
+    pair_recvs,
+    band_sems,
+    ffn_sems,
+    pair_sems,
+    grad_sems,
+    local_sem,
 ):
-    sums_refs, (dproj_ref, dwp_ref, dwg_ref, dg1_ref) = refs[:2], refs[2:]
-    slot, head = pl.program_id(0), pl.program_id(1)
-    inner = q_ref.shape[1]
-    size = inner // heads
-    frames = q_ref.shape[2]
-
-    @pl.when((slot == 0) & (head == 0))
-    def clear():
-        for ref in (dwp_ref, dwg_ref, dg1_ref):
-            ref[...] = jnp.zeros_like(ref)
-
-    start = pl.multiple_of(head * size, size)
-    at = pl.ds(start, size)
-    d_queries, d_keys, d_values = scores_backward(
-        q_ref[0, at, :],
-        k_ref[0, at, :],
-        v_ref[0, at, :],
-        p_ref[0, 0],
-        datt_ref[0, at, :],
-        minus_ref[0, pl.ds(head, 1), :],
-        cos_ref[...],
-        sin_ref[...],
-        size**-0.5,
-    )
-    dproj_ref[at, :] = d_queries.astype(BF16)
-    dproj_ref[pl.ds(inner + start, size), :] = d_keys.astype(BF16)
-    dproj_ref[pl.ds(2 * inner + start, size), :] = d_values.astype(BF16)
-
-    @pl.when(head == heads - 1)
-    def after():
-        d_logit = jnp.concatenate([dlogit_ref[0], jnp.zeros_like(dlogit_ref[0])], axis=0).astype(BF16)
-        dwp_ref[...] += dg(n_ref[0], dproj_ref[...], NT)
-        dwg_ref[...] += dg(n_ref[0], d_logit, NT)[:, :heads]
-        gain = column(g1_ref)
-
-        def block(i, carry):
-            at = pl.ds(pl.multiple_of(i * BLOCK, BLOCK), BLOCK)
-            logit = dlogit_ref[0, :, at].astype(BF16)
-            d_normed = dg(wp_ref[...], dproj_ref[:, at], NN) + dg(wg_ref[...], logit, NN)
-            d_rows, terms = norm_backward(x_ref[0, at, :].astype(F32).T, gain, d_normed)
-            dg1_ref[...] += jnp.sum(terms, axis=1, keepdims=True)
-            out_ref[0, at, :] = (dmid_ref[0, :, at] + d_rows).T.astype(BF16)
-            return carry
-
-        lax.fori_loop(0, frames // BLOCK, block, 0)
-
-    @pl.when((slot == pl.num_programs(0) - 1) & (head == heads - 1))
+    place = Place()
+    step = pl.program_id(0)
+    steps = heads * slots
+    head, slot = step // slots, lax.rem(step, slots)
+    size, frames = q_ref.shape[1:]
+    model = n_ref.shape[1]
+    inner = heads * size
+    pairs = heads // 2
+    pair_rows = 6 * size
+    blocks = frames // BLOCK
+    last = pl.num_programs(0) - 1
+    my_band, my_batch = place.band, place.batch
+
+    bands = [Total(place, order, band_sems[0].at[i], band_sems[1].at[i]) for i, order in enumerate(ORDERS)]
+    ffns = [Total(place, order, ffn_sems[0].at[i], ffn_sems[1].at[i]) for i, order in enumerate(ORDERS)]
+    own = [
+        Total(place, ORDERS[i % 2], pair_sems[0].at[i], pair_sems[1].at[i]) for i in range(pairs)
+    ]
+
+    def region_copy(i):
+        rows = bands[i].back_rows(band_outs[i], 2)
+        return pltpu.make_async_copy(region_refs[i], band_outs[i].at[rows], local_sem.at[i])
+
+    def half_copy(i):
+        return pltpu.make_async_copy(ffn_refs[i].at[place.bits["core"]], held_refs[i], local_sem.at[2 + i])
+
+    def eighth(total, held):
+        return held.at[total.half_rows(held, 2)[0]]
+
+    def all_steps(total, source, held, recvs, out, sem):
+        width = recvs[3].shape[2]
+
+        def back_region():
+            return out.at[total.back_rows(out, 2)]
+
+        def s0():
+            total.start_core(source, recvs[0])
+
+        def s1():
+            total.end_core(held, recvs[0])
+            total.start_half(1, held, recvs[1])
+
+        def s2():
+            total.end_half(1, held, recvs[1])
+            total.start_half(2, held, recvs[2])
+
+        def s3():
+            total.end_half(2, held, recvs[2])
+            total.start_z(eighth(total, held), recvs[3])
+
+        def s4():
+            total.end_z(eighth(total, held), recvs[3])
+            total.start_z_back(eighth(total, held), back_region(), width, sem)
+
+        def s5():
+            total.end_z_back(eighth(total, held), back_region(), width, sem)
+            total.start_back(2, out)
+
+        def s6():
+            total.end_back(2, out)
+            total.start_back(1, out)
+
+        def s7():
+            total.end_back(1, out)
+            total.start_back(0, out)
+
+        def s8():
+            total.end_back(0, out)
+
+        return [s0, s1, s2, s3, s4, s5, s6, s7, s8]
+
+    plan = {}
+
+    def at_step(index, action):
+        plan.setdefault(index, []).append(action)
+
+    def enter():
+        others = [(my_band, lax.rem(my_batch + i, batch_count)) for i in range(1, batch_count)]
+        others += [place.across("y")] + [place.along_z(i)[1] for i in range(1, Z_COUNT)]
+        greet(others)
+        for i in range(2):
+            region_copy(i).start()
+            bands[i].start_back(2, band_outs[i], region_refs[i])
+            half_copy(i).start()
+
+    at_step(0, enter)
+    for i in range(2):
+        for at, action in zip(
+            (2, 4, 6),
+            (
+                lambda i=i: (
+                    region_copy(i).wait(),
+                    bands[i].end_back(2, band_outs[i]),
+                    bands[i].start_back(1, band_outs[i]),
+                ),
+                lambda i=i: (bands[i].end_back(1, band_outs[i]), bands[i].start_back(0, band_outs[i])),
+                lambda i=i: bands[i].end_back(0, band_outs[i]),
+            ),
+        ):
+            at_step(at, action)
+        actions = all_steps(ffns[i], ffn_refs[i], held_refs[i], ffn_recvs[i], ffn_outs[i], local_sem.at[4 + i])
+        at_step(0, actions[0])
+        at_step(2, lambda i=i: half_copy(i).wait())
+        for at, action in zip((2, 4, 6, 8, 10, 12, 14, 16), actions[1:]):
+            at_step(at, action)
+    for i in range(pairs):
+        actions = all_steps(
+            own[i],
+            pair_refs.at[i],
+            pair_refs.at[i, place.bits["core"]],
+            [ref.at[i] for ref in pair_recvs],
+            pair_outs.at[i],
+            local_sem.at[6 + i],
+        )
+        begin = (i + 1) * 2 * slots
+        stride = 2 if i + 1 < pairs else 1
+        for n, action in enumerate(actions):
+            at_step(min(begin + n * stride, steps + slots * blocks - 1 + (n == len(actions) - 1)), action)
+
+    for index in sorted(plan):
+        if index <= steps + slots * blocks - 1:
+
+            @pl.when(step == index)
+            def work(index=index):
+                for action in plan[index]:
+                    action()
+
+    @pl.when(step < steps)
+    def attention():
+        d_queries, d_keys, d_values = scores_backward(
+            q_ref[0],
+            k_ref[0],
+            v_ref[0],
+            p_ref[0, 0],
+            datt_ref[0],
+            minus_ref[0, pl.ds(head, 1), :],
+            cos_ref[...],
+            sin_ref[...],
+            size**-0.5,
+        )
+        start = pl.multiple_of((head // 2) * pair_rows + lax.rem(head, 2) * size, size)
+        dproj_ref[slot, pl.ds(start, size), :] = d_queries.astype(BF16)
+        dproj_ref[slot, pl.ds(start + 2 * size, size), :] = d_keys.astype(BF16)
+        dproj_ref[slot, pl.ds(start + 4 * size, size), :] = d_values.astype(BF16)
+
+    @pl.when((step < steps) & (lax.rem(step, 2 * slots) == 2 * slots - 1))
+    def pair_done():
+        pair = head // 2
+        rows = pl.ds(pl.multiple_of(pair * pair_rows, pair_rows), pair_rows)
+        sums = dg(n_ref[0], dproj_ref[0, rows, :], NT)
+        for j in range(1, slots):
+            sums = sums + dg(n_ref[j], dproj_ref[j, rows, :], NT)
+        for half in range(2):
+            at = slice(half * model // 2, (half + 1) * model // 2)
+            pair_refs[pair, half, :, 0:pair_rows] = sums[at].astype(BF16)
+
+    @pl.when(step == 2 * slots - 1)
+    def narrow_done():
+        gates = 0.0
+        for j in range(slots):
+            logit = jnp.concatenate([dlogit_ref[j], jnp.zeros_like(dlogit_ref[j])], axis=0).astype(BF16)
+            gates = gates + dg(n_ref[j], logit, NT)[:, :heads]
+        tile = narrow_tile([narrow_ref[:, : heads + 2], gates, dg2_ref[...]], model)
+        for half in range(2):
+            at = slice(half * model // 2, (half + 1) * model // 2)
+            pair_refs[0, half, :, pair_rows:] = tile[at].astype(BF16)
+            for i in range(1, pairs):
+                pair_refs[i, half, :, pair_rows:] = jnp.zeros_like(tile[at]).astype(BF16)
+        for pair in range(pairs):
+            for part in range(3):
+                to = pair * pair_rows + part * 2 * size
+                source = part * inner + pair * 2 * size
+                wp_turned_ref[:, to : to + 2 * size] = wp_ref[:, source : source + 2 * size]
+
+    def message(index):
+        j, i = index // blocks, lax.rem(index, blocks)
+        source = grad_buf.at[index]
+        target = grad_out.at[batch_count * j + my_batch]
+        return i, source, target
+
+    @pl.when(step >= steps)
+    def rows_done():
+        index = step - steps
+        j, i = index // blocks, lax.rem(index, blocks)
+        at = pl.ds(pl.multiple_of(i * BLOCK, BLOCK), BLOCK)
+        logit = logit_block_ref[0].astype(BF16)
+        d_normed = dg(wp_turned_ref[...], dproj_ref[j, :, at], NN) + dg(wg_ref[...], logit, NN)
+        d_rows, _ = norm_backward(x_ref[0].astype(F32).T, column(g1_ref), d_normed)
+        grad_buf[index] = (dmid_ref[0] + d_rows).T.astype(BF16)
+        i, source, target = message(index)
+
+        @pl.when(i == my_batch)
+        def keep():
+            pltpu.make_async_copy(source, target, local_sem.at[6 + pairs]).start()
+
+        @pl.when(i != my_batch)
+        def give():
+            send(source, target, grad_sems.at[0], grad_sems.at[1], my_band, i)
+
+    @pl.when(step == last)
     def finish():
-        finish_sums(sums_refs, ((dwp_ref, False), dwg_ref, dg1_ref))
-
-
-def time_attention_backward(p, q, k, v, datt, minus, dlogit, n, x, dmid, cos, sin, g1, wp, wg):
+        for action in plan.get(steps + slots * blocks, []):
+            action()
+        await_bytes(grad_buf.at[pl.ds(0, slots)], local_sem.at[6 + pairs])
+        others = grad_buf.at[pl.ds(0, slots * (batch_count - 1))]
+        await_bytes(others, grad_sems.at[0])
+        await_bytes(others, grad_sems.at[1])
+
+
+def time_attention_backward(
+    p, q, k, v, datt, minus, dlogit, n, x, dmid, cos, sin, g1, wp, wg, narrow, dg2, regions, ffn_sums, batch_count
+):
     slots, inner, frames = q.shape
     heads = minus.shape[1]
+    size = inner // heads
     model = n.shape[1]
-
-    def per_slot(array):
-        return pl.BlockSpec((1,) + array.shape[1:], lambda s, h: (s, 0, 0))
-
-    consts = (cos, sin, g1, wp, wg)
-    sums = ((model, 3 * inner), (model, 128))
+    pairs = heads // 2
+    steps = heads * slots
+    blocks = frames // BLOCK
+
+    def clamp(t):
+        return jnp.minimum(t, steps - 1)
+
+    def tail(t):
+        return jnp.maximum(t - steps, 0)
+
+    def per_head(rows, columns):
+        return pl.BlockSpec((1, rows, columns), lambda t: (lax.rem(clamp(t), slots), clamp(t) // slots, 0))
+
+    consts = (n, dlogit, cos, sin, g1, wp, wg, narrow, dg2)
+    anywhere = pl.BlockSpec(memory_space=pl.ANY)
+    dma = pltpu.SemaphoreType.DMA
+    widths = [a.shape[2] for a in ffn_sums]
+    pair_width = 8 * size
+
+    def recv_buffers(width, *lead):
+        rows = model // 2
+        shapes = [(rows, width), (rows // 2, width), (rows // 4, width), (Z_COUNT - 1, rows // 4, width // Z_COUNT)]
+        return [pltpu.VMEM(lead + shape, BF16) for shape in shapes]
+
     return pl.pallas_call(
-        lambda *refs: time_attention_backward_kernel(heads, *refs),
-        grid=(slots, heads),
-        out_shape=[
-            jax.ShapeDtypeStruct((slots, frames, model), BF16),
+        lambda *refs: time_attention_backward_kernel(heads, slots, batch_count, *refs),
+        grid=(steps + slots * blocks,),
+        out_shape=(
+            jax.ShapeDtypeStruct((batch_count * slots, BLOCK, model), BF16),
+            [jax.ShapeDtypeStruct((model, a.shape[1]), BF16) for a in regions],
+            [jax.ShapeDtypeStruct((model, width), BF16) for width in widths],
+            jax.ShapeDtypeStruct((pairs, model, pair_width), BF16),
+        ),
+        in_specs=[
+            pl.BlockSpec((1, 1, frames, frames), lambda t: (lax.rem(clamp(t), slots), clamp(t) // slots, 0, 0)),
+            per_head(size, frames),
+            per_head(size, frames),
+            per_head(size, frames),
+            per_head(size, frames),
+            pl.BlockSpec((1, heads, frames), lambda t: (lax.rem(clamp(t), slots), 0, 0)),
+            pl.BlockSpec((1, BLOCK, model), lambda t: (tail(t) // blocks, lax.rem(tail(t), blocks), 0)),
+            pl.BlockSpec((1, model, BLOCK), lambda t: (tail(t) // blocks, 0, lax.rem(tail(t), blocks))),
+            pl.BlockSpec((1, heads, BLOCK), lambda t: (tail(t) // blocks, 0, lax.rem(tail(t), blocks))),
         ]
-        + sum_shapes(*sums),
-        in_specs=[pl.BlockSpec((1, 1, frames, frames), lambda s, h: (s, h, 0, 0))]
-        + [per_slot(a) for a in (q, k, v, datt, minus, dlogit, n, x, dmid)]
-        + [whole_spec(c) for c in consts],
-        out_specs=[
-            pl.BlockSpec((1, frames, model), lambda s, h: (s, 0, 0)),
-        ]
-        + sum_specs(*sums),
+        + [whole_spec(c) for c in consts]
+        + [[anywhere] * len(regions), [anywhere] * len(ffn_sums)],
+        out_specs=(anywhere, [anywhere] * len(regions), [anywhere] * len(ffn_sums), anywhere),
         scratch_shapes=[
-            pltpu.VMEM((3 * inner, frames), BF16),
-            pltpu.VMEM((model, 3 * inner), F32),
-            pltpu.VMEM((model, heads), F32),
-            pltpu.VMEM((model, 1), F32),
+            pltpu.VMEM((slots, 3 * inner, frames), BF16),
+            pltpu.VMEM((model, 3 * inner), BF16),
+            pltpu.VMEM((slots * blocks, BLOCK, model), BF16),
+            [pltpu.VMEM((model // 2, width), BF16) for width in widths],
+            [recv_buffers(width) for width in widths],
+            pltpu.VMEM((pairs, 2, model // 2, pair_width), BF16),
+            recv_buffers(pair_width, pairs),
+            [dma((2, TOTAL_STEPS)), dma((2, TOTAL_STEPS))],
+            [dma((2, TOTAL_STEPS)), dma((2, TOTAL_STEPS))],
+            [dma((pairs, TOTAL_STEPS)), dma((pairs, TOTAL_STEPS))],
+            dma((2,)),
+            dma((7 + pairs,)),
         ],
-        compiler_params=pltpu.CompilerParams(vmem_limit_bytes=VMEM_BYTES),
+        compiler_params=pltpu.CompilerParams(
+            vmem_limit_bytes=VMEM_BYTES, collective_id=3, has_side_effects=True
+        ),
         cost_estimate=cost(20.0e6 * slots * frames, 0, 60e6),
         name="time_attention_backward",
-    )(p, q, k, v, datt, minus, dlogit, n, x, dmid, *consts)
+    )(p, q, k, v, datt, minus, x, dmid, dlogit, *consts, list(regions), list(ffn_sums))
+
+
+def finish_kernel(
+    heads,
+    grad_ref,
+    bwp_ref,
+    bw1_ref,
+    bw2t_ref,
+    bwot_ref,
+    w1_ref,
+    wot_ref,
+    w2t_ref,
+    pair_ref,
+    first_pair_ref,
+    wp_ref,
+    wg_ref,
+    g1_ref,
+    grad_out,
+    dg1_out,
+    dwp_out,
+    dwg_out,
+    dwo_out,
+    dg2_out,
+    dw1_out,
+    dw2_out,
+    bg1_out,
+    bwp_out,
+    bwg_out,
+    bwo_out,
+    bg2_out,
+    bw1_out,
+    bw2_out,
+    scaled_ref,
+):
+    pair = pl.program_id(0)
+    inner = wp_ref.shape[1] // 3
+    width = inner // pl.num_programs(0)
+    grad_out[...] = grad_ref[...].astype(F32)
+    bwp_out[...] = bwp_ref[...].astype(F32)
+    bw1_out[...] = bw1_ref[...].astype(F32)
+    bw2_out[...] = bw2t_ref[...].astype(F32).T
+    bwo_out[...] = bwot_ref[...].astype(F32).T
+    dw1_out[...] = w1_ref[...].astype(F32)
+    dw2_out[...] = w2t_ref[...].astype(F32).T
+    dwo_out[...] = wot_ref[...].astype(F32).T
+
+    @pl.when(pair == 0)
+    def clear():
+        scaled_ref[...] = jnp.zeros_like(scaled_ref)
+
+    for part in range(3):
+        at = pl.ds(pl.multiple_of(part * inner + pair * width, 128), width)
+        values = pair_ref[0, :, part * width : (part + 1) * width].astype(F32)
+        dwp_out[:, at] = values
+        scaled_ref[...] += values * wp_ref[:, at].astype(F32)
+
+    @pl.when(pair == pl.num_programs(0) - 1)
+    def narrow():
+        tile = first_pair_ref[0, :, 3 * width :].astype(F32)
+        rows = tile.T
+        bwg_out[...] = tile[:, :heads]
+        bg1_out[...] = rows[heads : heads + 1]
+        bg2_out[...] = rows[heads + 1 : heads + 2]
+        gates = tile[:, heads + 2 : 2 * heads + 2]
+        dwg_out[...] = gates
+        dg2_out[...] = rows[2 * heads + 2 : 2 * heads + 3]
+        sums = jnp.sum(scaled_ref[...], axis=1, keepdims=True)
+        sums = sums + jnp.sum(gates * wg_ref[...].astype(F32), axis=1, keepdims=True)
+        dg1_out[...] = jnp.broadcast_to(sums, (sums.shape[0], 128)).T[:1] / g1_ref[...].astype(F32)
+
+
+def finish_sums(grads, band_sums, ffn_sums, pair_sums, params, band_params):
+    g1, wp, wg, wo, g2, w1, w2 = params
+    model, hidden = w1.shape
+    inner, heads = wo.shape[0], wg.shape[1]
+    pairs = pair_sums.shape[0]
+    split = hidden // pairs
+    out_split = inner // pairs
+    slot_dev, frame_dev, _ = grads.shape
+
+    def lanes(array, start, width):
+        first = start // width
+        return pl.BlockSpec((model, width), lambda i: (0, first + i))
+
+    def whole(*shape):
+        return pl.BlockSpec(shape, lambda i: (0,) * len(shape))
+
+    def cut_rows(rows):
+        return pl.BlockSpec((rows, model), lambda i: (i, 0))
+
+    band_first, band_second = band_sums
+    ffn_first, ffn_second = ffn_sums
+    grad_block = pl.BlockSpec((slot_dev // pairs, frame_dev, model), lambda i: (i, 0, 0))
+    narrow = [((1, model), whole(1, model)), ((model, heads), whole(model, heads))]
+    per_layer = [
+        narrow[0],
+        ((model, 3 * inner), None),
+        narrow[1],
+        ((inner, model), cut_rows(out_split)),
+        narrow[0],
+        ((model, hidden), lanes(None, 0, split)),
+        ((hidden, model), cut_rows(split)),
+    ]
+    shapes, specs = [jax.ShapeDtypeStruct(grads.shape, F32)], [grad_block]
+    for layer in range(2):
+        for shape, spec in per_layer:
+            shapes.append(jax.ShapeDtypeStruct(shape, F32))
+            if spec is None:
+                spec = whole(*shape) if layer == 0 else lanes(None, 0, 3 * inner // pairs)
+            specs.append(spec)
+    return pl.pallas_call(
+        lambda *refs: finish_kernel(heads, *refs),
+        grid=(pairs,),
+        out_shape=shapes,
+        in_specs=[
+            grad_block,
+            lanes(band_first, 0, 3 * inner // pairs),
+            lanes(band_second, 0, split),
+            lanes(band_second, hidden, split),
+            lanes(band_first, 3 * inner, out_split),
+            lanes(ffn_first, 0, split),
+            lanes(ffn_first, hidden, out_split),
+            lanes(ffn_second, 0, split),
+            pl.BlockSpec((1, model, pair_sums.shape[2]), lambda i: (i, 0, 0)),
+            pl.BlockSpec((1, model, pair_sums.shape[2]), lambda i: (0, 0, 0)),
+            whole_spec(wp),
+            whole_spec(wg),
+            whole_spec(g1),
+        ],
+        out_specs=specs,
+        scratch_shapes=[pltpu.VMEM((model, inner // pairs), F32)],
+        compiler_params=pltpu.CompilerParams(vmem_limit_bytes=VMEM_BYTES),
+        name="finish_sums",
+    )(
+        grads,
+        band_first,
+        band_second,
+        band_second,
+        band_first,
+        ffn_first,
+        ffn_first,
+        ffn_second,
+        pair_sums,
+        pair_sums,
+        wp,
+        wg,
+        g1,
+    )
 
 
 def band_kernel(
@@ -1096,10 +1645,7 @@
     w2_ref,
     y_out,
     dx_out,
-    dwp_out,
-    dw1_out,
-    dw2_out,
-    dwo_out,
+    part_outs,
     narrow_out,
     q_ref,
     k_ref,
@@ -1133,6 +1679,11 @@
     dx_send,
     dx_recv,
     local_sem,
+    halves,
+    half_recvs,
+    sum_sends,
+    sum_recvs,
+    part_sem,
 ):
     step = pl.program_id(0)
     slot_count, part_frames, model = x_ref.shape
@@ -1183,7 +1734,8 @@
             cots_ref[c] = cot_ref[:, :, at].astype(F32).reshape(cots_ref.shape[1:])
 
     gain1, gain2 = column(g1_ref), column(g2_ref)
-    sums_refs = (dwp_out, dw1_out, dw2_out, dwo_out, narrow_out)
+    place = Place()
+    totals = [Total(place, order, sum_sends.at[i], sum_recvs.at[i]) for i, order in enumerate(ORDERS)]
 
     @pl.when(step == 0)
     def clear():
@@ -1328,10 +1880,28 @@
 
     @pl.when(step == pl.num_programs(0) - 1)
     def finish():
-        finish_sums(
-            sums_refs,
-            ((dwp_ref, False), (dw1_ref, False), (dw2t_ref, True), (dwot_ref, True), dwg_ref, dg1_ref, dg2_ref),
-        )
+        narrow_out[...] = narrow_tile([dwg_ref[...], dg1_ref[...], dg2_ref[...]], model)
+        core = place.bits["core"]
+        lay_halves(halves[0], 0, dwp_ref)
+        lay_halves(halves[0], dwp_ref.shape[1], dwot_ref)
+        totals[0].start_core(halves[0], half_recvs[0][0])
+        lay_halves(halves[1], 0, dw1_ref)
+        lay_halves(halves[1], dw1_ref.shape[1], dw2t_ref)
+        totals[1].start_core(halves[1], half_recvs[1][0])
+        held = [half.at[core] for half in halves]
+        for i, total in enumerate(totals):
+            total.end_core(held[i], half_recvs[i][0])
+            total.start_half(1, held[i], half_recvs[i][1])
+        for i, total in enumerate(totals):
+            total.end_half(1, held[i], half_recvs[i][1])
+            total.start_half(2, held[i], half_recvs[i][2])
+        for i, total in enumerate(totals):
+            total.end_half(2, held[i], half_recvs[i][2])
+            rows = total.half_rows(held[i], 2)[0]
+            pltpu.make_async_copy(held[i].at[rows], part_outs[i], part_sem.at[i]).start()
+        for i, total in enumerate(totals):
+            rows = total.half_rows(held[i], 2)[0]
+            pltpu.make_async_copy(held[i].at[rows], part_outs[i], part_sem.at[i]).wait()
         piece = y_out.shape[1] // band_count
         await_bytes(y_out.at[:, pl.ds(0, piece)], local_sem.at[0])
         await_bytes(dx_out.at[pl.ds(0, slots)], local_sem.at[1])
@@ -1353,20 +1923,22 @@
     parts = piece // part_frames
     slot_dev = slot_count // band_count
     consts = (bias, cos, sin, prenorm, midnorm) + flips + (project, gating, output_weight, expand, shrink)
-    sums = ((model, 3 * inner), (model, hidden), (hidden, model), (inner, model), (model, 128))
+    widths = (3 * inner + inner, 2 * hidden)
+    eighth = model // 8
     blocks = pl.BlockSpec((slot_count, part_frames, model), lambda i: (0, i // per_part, 0))
     anywhere = pl.BlockSpec(memory_space=pl.ANY)
     dma = pltpu.SemaphoreType.DMA
     return pl.pallas_call(
         lambda *refs: band_kernel(heads, batch_count, band_count, *refs),
         grid=(steps,),
-        out_shape=[
+        out_shape=(
             jax.ShapeDtypeStruct((slot_dev, piece * band_count, model), BF16),
             jax.ShapeDtypeStruct((slot_count, piece, model), BF16),
-        ]
-        + sum_shapes(*sums),
+            [jax.ShapeDtypeStruct((eighth, width), BF16) for width in widths],
+            jax.ShapeDtypeStruct((model, 128), F32),
+        ),
         in_specs=[blocks, blocks, pl.BlockSpec((1, 1, tokens), lambda i: (i, 0, 0))] + [whole_spec(c) for c in consts],
-        out_specs=[anywhere, anywhere] + sum_specs(*sums),
+        out_specs=(anywhere, anywhere, [anywhere] * 2, pl.BlockSpec((model, 128), lambda i: (0, 0))),
         scratch_shapes=[
             pltpu.VMEM((inner, tokens), BF16),
             pltpu.VMEM((inner, tokens), BF16),
@@ -1400,6 +1972,14 @@
             dma,
             dma,
             dma((2,)),
+            [pltpu.VMEM((2, model // 2, width), BF16) for width in widths],
+            [
+                [pltpu.VMEM((rows, width), BF16) for rows in (model // 2, model // 4, model // 8)]
+                for width in widths
+            ],
+            dma((2, TOTAL_STEPS)),
+            dma((2, TOTAL_STEPS)),
+            dma((2,)),
         ],
         compiler_params=pltpu.CompilerParams(
             vmem_limit_bytes=VMEM_BYTES, collective_id=1, has_side_effects=True
@@ -1449,7 +2029,7 @@
         band,
         batch,
     )
-    layer_output, slot_grad, *band_sums = band_layer(
+    layer_output, slot_grad, band_parts, band_narrow = band_layer(
         band_rows,
         band_cot,
         mask,
@@ -1463,37 +2043,47 @@
     )
     slot_grad = slot_grad.reshape(slots, frames, model)
     g1, g2 = time_params[0], time_params[4]
-    dmid, datt, minus, dlogit, *ffn_sums = time_ffn_backward(
-        slot_grad, act, slope, nf, mid, mixed, att, gate, linv, g2, time_params[5], time_params[6], time_params[3]
-    )
-    grads, *attn_sums = time_attention_backward(
-        p, q, k, v, datt, minus, dlogit, n, rows, dmid, time_cos.T, time_sin.T, g1, time_params[1], time_params[2]
-    )
-    input_grad = lax.all_to_all(grads, "batch", split_axis=1, concat_axis=0, tiled=True)
-    input_grad = input_grad.reshape(batch, slots, frame_dev, model).transpose(1, 0, 2, 3)
-    attn_sums, ffn_sums, band_sums = lax.psum((attn_sums, ffn_sums, band_sums), ("band", "batch"))
-
-    dwp, attn_narrow = (part.astype(F32) for part in attn_sums)
-    dw1, dw2, dwo, ffn_narrow = (part.astype(F32) for part in ffn_sums)
-    bwp, bw1, bw2, bwo, band_narrow = (part.astype(F32) for part in band_sums)
-    return (
-        layer_output.reshape(activations.shape),
-        input_grad.astype(F32).reshape(activations.shape),
-        attn_narrow[:, heads],
-        dwp,
-        attn_narrow[:, :heads],
-        dwo,
-        ffn_narrow[:, 0],
-        dw1,
-        dw2,
-        band_narrow[:, heads],
-        bwp,
-        band_narrow[:, :heads],
-        bwo,
-        band_narrow[:, heads + 1],
-        bw1,
-        bw2,
-    )
+    dmid, datt, minus, dlogit, ffn_sums, dg2, regions = time_ffn_backward(
+        slot_grad,
+        act,
+        slope,
+        nf,
+        mid,
+        mixed,
+        att,
+        gate,
+        linv,
+        g2,
+        time_params[5],
+        time_params[6],
+        time_params[3],
+        band_parts,
+    )
+    input_grad, band_sums, ffn_sums, pair_sums = time_attention_backward(
+        p,
+        q,
+        k,
+        v,
+        datt,
+        minus,
+        dlogit,
+        n,
+        rows,
+        dmid,
+        time_cos.T,
+        time_sin.T,
+        g1,
+        time_params[1],
+        time_params[2],
+        band_narrow,
+        dg2,
+        regions,
+        ffn_sums,
+        batch,
+    )
+    input_grad, *grads = finish_sums(input_grad, band_sums, ffn_sums, pair_sums, time_params, band_params)
+    grads = [g[0] if g.shape[0] == 1 else g for g in grads]
+    return (layer_output.reshape(activations.shape), input_grad.reshape(activations.shape), *grads)
 
 
 def shards(activations, cotangent, frame_counts, slot_bands, *weights):
@@ -1501,6 +2091,8 @@
     batch, band = lax.axis_size("batch"), lax.axis_size("band")
     fits = (
         clips == 1
+        and batch == 4
+        and band == 2 * Z_COUNT
         and slot_dev % batch == 0
         and frame_dev == BLOCK
         and frame_dev % (16 * band) == 0

time: 546 us -> 434 us (0.79)
  waiting for transfers between devices: 185 us -> 0 us
  Pallas kernels: 301 us -> 408 us
  between operations: 14.8 us -> 1.37 us
  other arithmetic: 21.9 us -> 9.85 us
  local copies, waits for them, and re-layouts: 19.7 us -> 14.1 us
    psum x1 -> x0, waiting for transfers between devices: 151 us -> none  [slot_shards(): lax.psum((attn_sums, ffn_sums, band_sums), ('band', 'batch'))]
    pallas_call x2 -> x3, Pallas kernels: 78 us -> 170 us  [the longest x1 124 us: time_attention_backward(): pl.pallas_call(lambda *refs: time_attention_backward_kernel(heads, slots,...]
    all_to_all x1 -> x0, waiting for transfers between devices: 34.2 us -> none  [slot_shards(): lax.all_to_all(grads, 'batch', split_axis=1, concat_axis=0, tiled=True)]
    pallas_call x1, Pallas kernels: 130 us -> 144 us  [band_layer(): pl.pallas_call(lambda *refs: band_kernel(heads, batch_count, band_count,...]
    convert_element_type x10 -> x0, other arithmetic: 13.7 us -> none  [the longest x5 6.88 us: slot_shards(): bwp, bw1, bw2, bwo, band_narrow = (part.astype(F32) for part in band_sums)]
  transfers between devices with their start and end apart: 2 -> 0, of which waited for: 2 -> 0; matrix products, arithmetic and copies ran while one was open for 1% -> 0% of each run, Pallas kernels for 0% -> 0%
where the time goes in v4:
time: 434 us; the launch traced here: 433 us
  Pallas kernels  408 us (94%)
  local copies, waits for them, and re-layouts  14.1 us (3%)
  other arithmetic  9.85 us (2%)
    pallas_call x1, Pallas kernels, band_layer(): pl.pallas_call(lambda *refs: band_kernel(heads, batch_count, band_count,...  144 us
    pallas_call x1, Pallas kernels, time_attention_backward(): pl.pallas_call(lambda *refs: time_attention_backward_kernel(heads, slots,...  124 us
    pallas_call x1, Pallas kernels, time_forward(): pl.pallas_call(lambda *refs: time_forward_kernel(heads, batch_count, band...  93 us
    pallas_call x1, Pallas kernels, time_ffn_backward(): pl.pallas_call(lambda *refs: time_ffn_backward_kernel(heads, ORDERS, *ref...  33.4 us
    pallas_call x1, Pallas kernels, finish_sums(): pl.pallas_call(lambda *refs: finish_kernel(heads, *refs), grid=(pairs,),...  13.2 us

profile of v4, /device:TPU:0, one launch (start us, length us, event | category | flops | bytes accessed | tf_op | source)
XLA Modules:
  0.0 433.0 jit_solution(7903002010597981762)
XLA Ops:
  1.3 0.7 broadcast_compare_fusion
  2.2 0.7 maximum_convert_fusion
  2.8 1.2 broadcast_in_dim.40.refs_5_.refs_13_.refs_12_
  4.1 1.2 broadcast_in_dim.41.refs_6_.refs_9_
  5.3 1.2 broadcast_in_dim.44.refs_6_
  6.6 1.2 broadcast_in_dim.45.refs_7_
  9.3 1.5 copy.43.refs_8_.refs_15_.refs_11_
  10.8 1.5 copy.44.refs_13_.refs_14_
  12.3 0.7 tile.28.refs_5_
  13.0 0.7 tile.12.refs_4_
  13.7 1.2 multiply_sine_fusion
  15.0 0.8 and_select_fusion.refs_3_
  15.8 93.0 %time_forward.1 = (bf16[64,32,384]{2,1,0:T(8,128)(2,1)}, bf16[64,32,384]{2,1,0:T(8,128)(2,1)}, bf16[2,1024,384]{2,1,0:T(8,128)(2,1)}, bf16[2,384,1024]{2,1,0:T(8...) custom-call(bf16[8,256,384]{2,1,0:T(8,128)(2,1)} %bitcast.14, ...), custom_call_target="tpu_custom_call" | custom-call | flops 16384000000 | bytes 60000000 | tf_op jit(solution)/shard_map/time_forward/pallas_call | solution.py:933
  108.8 144.2 %band_layer.1 = (bf16[8,256,384]{2,1,0:T(8,128)(2,1)}, bf16[64,32,384]{2,1,0:T(8,128)(2,1)}, bf16[48,2048]{1,0:T(8,128)(2,1)}, bf16[48,3072]{1,0:T(8,128)(2,1)}, f32[384,128]{1,0:T(8,128)}) custom-call(bf16[64,32,384]{2,1,0:T(8,128)(2,1)} %get-tuple-element.72.refs_0_, bf16[64,32,384]{2,1,0:T(8,128)(2,1)} %get-tuple-element.73.refs_1_, ...), custom_call_target="tpu_custom_call" | custom-call | flops 61440000000 | bytes 60000000 | tf_op jit(solution)/shard_map/band_layer/pallas_call | solution.py:1931
  253.0 33.4 %time_ffn_backward.1 = (f32[2,384,1024]{2,1,0:T(8,128)}, bf16[2,512,1024]{2,1,0:T(8,128)(2,1)}, f32[2,8,1024]{2,1,0:T(8,128)}, f32[2,8,1024]{2,1,0:T(8,128)}, bf...) custom-call(bf16[2,1024,384]{2,1,0:T(8,128)(2,1)} %bitcast.16, ...), custom_call_target="tpu_custom_call" | custom-call | flops 16384000000 | bytes 30000000 | tf_op jit(solution)/shard_map/time_ffn_backward/pallas_call | solution.py:1106
  286.5 123.9 %time_attention_backward.1 = (bf16[8,256,384]{2,1,0:T(8,128)(2,1)}, bf16[384,2048]{1,0:T(8,128)(2,1)}, bf16[384,3072]{1,0:T(8,128)(2,1)}, bf16[384,2048]{1,0:T(8...) custom-call(bf16[2,8,1024,1024]{3,2,1,0:T(8,128)(2,1)} %get-tuple-element.80.refs_0_, ...), custom_call_target="tpu_custom_call" | custom-call | flops 40960000000 | bytes 60000000 | tf_op jit(solution)/shard_map/time_attention_backward/pallas_call | solution.py:1431
  410.4 13.2 %finish_sums.1 = (f32[8,256,384]{2,1,0:T(8,128)}, f32[1,384]{1,0:T(1,128)}, f32[384,1536]{1,0:T(8,128)}, f32[384,8]{1,0:T(8,128)}, f32[512,384]{1,0:T(8,128)}, /...) custom-call(bf16[8,256,384]{2,1,0:T(8,128)(2,1)} %get-tuple-element., ...), custom_call_target="tpu_custom_call" | custom-call | tf_op jit(solution)/shard_map/finish_sums/pallas_call | solution.py:1584
  423.6 1.3 reduce
  424.8 1.3 reduce.1
  426.1 1.3 reduce.2
  427.4 1.3 reduce.3
  428.6 1.6 copy.51
  430.3 1.6 copy.52
  431.9 1.1 copy.55
  (17 shorter events, 1.7 us)
Async XLA Ops:
  410.4 21.5 %copy-start = (bf16[8,256,384]{2,1,0:T(8,128)(2,1)S(1)}, bf16[8,256,384]{2,1,0:T(8,128)(2,1)}, u32[]{:S(2)}) copy-start(bf16[8,256,384]{2,1,0:T(8,128)(2,1)} %get-tuple-element.79) | copy-start | bytes 4718596

commit v5 on v4

--- a/solution.py
+++ b/solution.py
@@ -481,9 +481,15 @@
     return queries.astype(BF16), keys.astype(BF16), values.astype(BF16)
 
 
-def column(row_ref):
-    row = row_ref[...].astype(F32)
+def column(gain_ref):
+    row = gain_ref[...].astype(F32).reshape(1, gain_ref.shape[0])
     return jnp.broadcast_to(row, (8, row.shape[1])).T[:, :1]
+
+
+def rotary_rows(positions, half):
+    rank = lax.broadcasted_iota(jnp.int32, (half, positions.shape[1]), 0).astype(F32)
+    angles = positions * jnp.exp(-math.log(10000.0) * rank / half)
+    return jnp.cos(angles), jnp.sin(angles)
 
 
 def flipped(ref):
@@ -563,7 +569,8 @@
         self.order = order
         self.sends, self.recvs = sends, recvs
         self.core = place.bits["core"]
-        self.first, self.second = (place.bits[axis] for axis in order)
+        if order is not None:
+            self.first, self.second = (place.bits[axis] for axis in order)
 
     def give(self, step, source, target, other):
         send(source, target, self.sends.at[step], self.recvs.at[step], *other)
@@ -632,6 +639,48 @@
     def end_z_back(self, piece, target, width, sem):
         self.took(4, target.at[:, pl.ds(0, (Z_COUNT - 1) * width)])
         self.own_copy(piece, target, width, sem).wait()
+
+    def around(self):
+        found = []
+        for step in range(1, 4 * Z_COUNT):
+            x = lax.rem(self.place.bits["x"] + step // 2 % 2, 2)
+            y = lax.rem(self.place.bits["y"] + step % 2, 2)
+            z = lax.rem(self.place.z + step // 4, Z_COUNT)
+            found.append((2 * x + y, z, (2 * z + y, 2 * x + self.core)))
+        return found
+
+    def tile(self, ref, base, quarter, z, shape):
+        rows = pl.ds(pl.multiple_of(base + quarter * shape[0], shape[0]), shape[0])
+        return ref.at[rows, pl.ds(pl.multiple_of(z * shape[1], 128), shape[1])]
+
+    def start_around(self, held, recv):
+        for i, (quarter, z, other) in enumerate(self.around()):
+            self.give(1, self.tile(held, 0, quarter, z, recv.shape[1:]), recv.at[i], other)
+
+    def own_tile(self, ref, base, shape):
+        return self.tile(ref, base, 2 * self.place.bits["x"] + self.place.bits["y"], self.place.z, shape)
+
+    def end_around(self, held, recv):
+        self.took(1, recv)
+        own = self.own_tile(held, 0, recv.shape[1:])
+        sums = own[...].astype(F32)
+        for i in range(recv.shape[0]):
+            sums = sums + recv[i].astype(F32)
+        own[...] = sums.astype(BF16)
+
+    def start_around_back(self, held, recv, out, sem):
+        shape = recv.shape[1:]
+        own = self.own_tile(held, 0, shape)
+        target = self.own_tile(out, self.core * (out.shape[0] // 2), shape)
+        for _, _, other in self.around():
+            self.give(2, own, target, other)
+        pltpu.make_async_copy(own, target, sem).start()
+
+    def end_around_back(self, held, recv, out, sem):
+        shape = recv.shape[1:]
+        self.took(2, recv)
+        target = self.own_tile(out, self.core * (out.shape[0] // 2), shape)
+        pltpu.make_async_copy(self.own_tile(held, 0, shape), target, sem).wait()
 
     def back_rows(self, out, level):
         rows = out.shape[0] // 2
@@ -662,18 +711,15 @@
     band_count,
     act_in,
     cot_in,
-    bias_ref,
-    cos_ref,
-    sin_ref,
+    count_ref,
     g1_ref,
     g2_ref,
+    wgt_ref,
     wp_ref,
-    wg_ref,
     wo_ref,
     w1_ref,
     w2_ref,
     band_wp_ref,
-    band_wg_ref,
     band_wo_ref,
     band_w1_ref,
     band_w2_ref,
@@ -694,15 +740,15 @@
     act_ref,
     slope_ref,
     band_wpt_ref,
-    band_wgt_ref,
     band_wot_ref,
     band_w1t_ref,
     band_w2t_ref,
+    cos_ref,
+    sin_ref,
     xt_ref,
     x_ref,
     result_ref,
     wpt_ref,
-    wgt_ref,
     wot_ref,
     w1t_ref,
     w2t_ref,
@@ -725,6 +771,11 @@
     piece = frame_dev // band_count
     own_rows = pl.ds(pl.multiple_of(my_batch * frame_dev, frame_dev), frame_dev)
     held = x_ref.shape[0]
+    frame_index = lax.broadcasted_iota(jnp.int32, (1, frames), 1)
+
+    def neighbour(i):
+        core, x = lax.rem(my_batch, 2), my_batch // 2
+        return lax.rem(x + i // 2, 2) * 2 + lax.rem(core + lax.rem(i, 2), 2)
 
     def own_row_copy(j):
         return pltpu.make_async_copy(
@@ -743,12 +794,12 @@
         greet_all(band_count, batch_count)
         for j in range(held):
             for i in range(1, batch_count):
-                other = lax.rem(my_batch + i, batch_count)
+                other = neighbour(i)
                 send(
                     act_in.at[batch_count * j + other],
                     x_ref.at[j, own_rows],
                     row_send,
-                    row_recv.at[j],
+                    row_recv.at[j, i],
                     my_band,
                     other,
                 )
@@ -768,30 +819,35 @@
 
         lax.fori_loop(1, band_count, send_cot, 0)
         own_cot_copy().start()
+        cos_ref[...], sin_ref[...] = rotary_rows(frame_index.astype(F32), size // 2)
         wpt_ref[...] = flipped(wp_ref)
-        wgt_ref[...] = flipped(wg_ref)
         wot_ref[...] = flipped(wo_ref)
         w1t_ref[...] = flipped(w1_ref)
         w2t_ref[...] = flipped(w2_ref)
         band_wpt_ref[...] = flipped(band_wp_ref)
-        band_wgt_ref[...] = flipped(band_wg_ref)
         band_wot_ref[...] = flipped(band_wo_ref)
         band_w1t_ref[...] = flipped(band_w1_ref)
         band_w2t_ref[...] = flipped(band_w2_ref)
 
     @pl.when(head == 0)
     def before():
-        for j in range(held):
-
-            @pl.when(slot == j)
+        gain = column(g1_ref)
+
+        def block(i, carry):
+            at = pl.ds(pl.multiple_of(neighbour(i) * BLOCK, BLOCK), BLOCK)
+
+            @pl.when(i == 0)
+            def own():
+                for j in range(held):
+
+                    @pl.when(slot == j)
+                    def kept():
+                        own_row_copy(j).wait()
+
+            @pl.when(i > 0)
             def arrived():
-                await_bytes(x_ref.at[j, pl.ds(0, (batch_count - 1) * frame_dev)], row_recv.at[j])
-                own_row_copy(j).wait()
-
-        gain = column(g1_ref)
-
-        def block(i, carry):
-            at = pl.ds(pl.multiple_of(i * BLOCK, BLOCK), BLOCK)
+                await_bytes(x_ref.at[slot, at], row_recv.at[slot, i])
+
             held_rows = x_ref[slot, at, :]
             rows_ref[0, at, :] = held_rows
             rows = held_rows.astype(F32).T
@@ -812,7 +868,7 @@
     at_head = pl.ds(pl.multiple_of(head * size, size), size)
     ones = jnp.ones((1, frames), F32)
     queries = jnp.concatenate([q_ref[0, at_head, :], extra_rows([ones], frames)], axis=0)
-    keys = jnp.concatenate([k_ref[0, at_head, :], extra_rows([bias_ref[...]], frames)], axis=0)
+    keys = jnp.concatenate([k_ref[0, at_head, :], extra_rows([jnp.where(frame_index < count_ref[0], 0.0, NEG_FILL)], frames)], axis=0)
     values = jnp.concatenate([v_ref[0, at_head, :], extra_rows([ones], frames)], axis=0)
     scores = dg(keys, queries, TN)
     weights = jnp.exp2(scores - jnp.max(scores, axis=0, keepdims=True)).astype(BF16)
@@ -886,12 +942,12 @@
     return pl.BlockSpec(array.shape, lambda *ids: (0,) * nd, pipeline_mode=pl.Buffered(1))
 
 
-def time_forward(activations, cotangent, bias, cos, sin, params, band_params, band_count, batch_count):
-    g1, wp, wg, wo, g2, w1, w2 = params
-    _, bwp, bwg, bwo, _, bw1, bw2 = band_params
+def time_forward(activations, cotangent, counts, g1, g2, params, band_params, band_count, batch_count):
+    wp, wgt, wo, w1, w2 = params
+    bwp, _, bwo, bw1, bw2 = band_params
     slot_dev, frame_dev, model = activations.shape
     slots, frames = slot_dev // batch_count, frame_dev * batch_count
-    heads, inner, hidden = wg.shape[1], wo.shape[0], w1.shape[1]
+    heads, inner, hidden = wgt.shape[0], wo.shape[0], w1.shape[1]
     piece = frame_dev // band_count
 
     def per_slot(*shape):
@@ -913,8 +969,8 @@
         ((hidden, frames), BF16),
         ((hidden, frames), BF16),
     ]
-    flips = [(w.shape[1], w.shape[0]) for w in (bwp, bwg, bwo, bw1, bw2)]
-    own_flips = [(w.shape[1], w.shape[0]) for w in (wp, wg, wo, w1, w2)]
+    flips = [(w.shape[1], w.shape[0]) for w in (bwp, bwo, bw1, bw2)]
+    own_flips = [(w.shape[1], w.shape[0]) for w in (wp, wo, w1, w2)]
     exchanged = jax.ShapeDtypeStruct((slot_dev * band_count, piece, model), BF16)
     anywhere = pl.BlockSpec(memory_space=pl.ANY)
     shapes, specs = [exchanged, exchanged], [anywhere, anywhere]
@@ -928,13 +984,17 @@
     for shape in flips:
         shapes.append(jax.ShapeDtypeStruct(shape, BF16))
         specs.append(pl.BlockSpec(shape, lambda s, h: (0, 0), pipeline_mode=pl.Buffered(1)))
-    consts = (bias, cos, sin, g1, g2, wp, wg, wo, w1, w2, bwp, bwg, bwo, bw1, bw2)
+    consts = (g1, g2, wgt, wp, wo, w1, w2, bwp, bwo, bw1, bw2)
+    half = inner // heads // 2
+    for _ in range(2):
+        shapes.append(jax.ShapeDtypeStruct((half, frames), F32))
+        specs.append(pl.BlockSpec((half, frames), lambda s, h: (0, 0)))
     dma = pltpu.SemaphoreType.DMA
     return pl.pallas_call(
         lambda *refs: time_forward_kernel(heads, batch_count, band_count, *refs),
         grid=(slots, heads),
         out_shape=shapes,
-        in_specs=[anywhere, anywhere] + [whole_spec(c) for c in consts],
+        in_specs=[anywhere, anywhere, pl.BlockSpec(memory_space=pltpu.SMEM)] + [whole_spec(c) for c in consts],
         out_specs=specs,
         scratch_shapes=[
             pltpu.VMEM((model, frames), F32),
@@ -942,13 +1002,13 @@
             pltpu.VMEM((slots, frames, model), BF16),
         ]
         + [pltpu.VMEM(shape, BF16) for shape in own_flips]
-        + [dma, dma((slots,)), dma, dma, dma, dma, dma((slots + 2,))],
+        + [dma, dma((slots, batch_count)), dma, dma, dma, dma, dma((slots + 2,))],
         compiler_params=pltpu.CompilerParams(
             vmem_limit_bytes=VMEM_BYTES, collective_id=0, has_side_effects=True
         ),
         cost_estimate=cost(2.0e6 * 4 * slots * frames, 2 * slots * heads * frames * frames, 60e6),
         name="time_forward",
-    )(activations, cotangent, *consts)
+    )(activations, cotangent, counts, *consts)
 
 
 def ffn_backward(grad, act, slope, normed, middle, gain, w1_ref, w2_ref, dw1_ref, dw2t_ref, dg2_ref):
@@ -987,7 +1047,6 @@
 
 def time_ffn_backward_kernel(
     heads,
-    orders,
     grad_ref,
     act_ref,
     slope_ref,
@@ -1001,26 +1060,37 @@
     w1_ref,
     w2_ref,
     wo_ref,
-    part_refs,
+    half_refs,
     dmid_ref,
     datt_ref,
     minus_ref,
     dlogit_ref,
     sums_refs,
     dg2_out,
-    region_refs,
+    part_refs,
     dw1_ref,
     dw2t_ref,
     dwot_ref,
     dg2_ref,
-    piece_refs,
+    held_refs,
+    half_recvs,
     z_recvs,
     sends,
     recvs,
     local_sem,
 ):
     place = Place()
-    totals = [Total(place, order, sends.at[i], recvs.at[i]) for i, order in enumerate(orders)]
+    totals = [Total(place, order, sends.at[i], recvs.at[i]) for i, order in enumerate(BAND_ORDERS)]
+    early = len(z_recvs)
+    work = list(zip(totals, half_refs, held_refs, half_recvs))
+
+    def half_copy(i):
+        return pltpu.make_async_copy(half_refs[i], held_refs[i], local_sem.at[i])
+
+    def part_copy(i):
+        rows = totals[i].half_rows(held_refs[i], 2)[0]
+        return pltpu.make_async_copy(held_refs[i].at[rows], part_refs[i], local_sem.at[len(totals) + i])
+
     step = pl.program_id(0) * pl.num_programs(1) + pl.program_id(1)
     last = pl.num_programs(0) * pl.num_programs(1) - 1
     size = wo_ref.shape[0] // heads
@@ -1029,18 +1099,40 @@
     def clear():
         for ref in (dw1_ref, dw2t_ref, dwot_ref, dg2_ref):
             ref[...] = jnp.zeros_like(ref)
-        greet([place.along_z(i)[1] for i in range(1, Z_COUNT)])
-        for total, part, piece, recv in zip(totals, part_refs, piece_refs, z_recvs):
-            piece[...] = part[...]
-            total.start_z(piece, recv)
-
-    @pl.when(step == last // 2 + 1)
-    def gather():
-        for i, (total, piece, recv, region) in enumerate(zip(totals, piece_refs, z_recvs, region_refs)):
-            total.end_z(piece, recv)
-            total.start_z_back(piece, region, recv.shape[2], local_sem.at[i])
-
-    grad = grad_ref[0].astype(F32).T
+        greet([place.across("x"), place.across("y")] + [place.along_z(i)[1] for i in range(1, Z_COUNT)])
+        for i, (total, halves, held, recv) in enumerate(work):
+            half_copy(i).start()
+            total.start_half(1, halves, recv[0])
+
+    def eighth(i):
+        return held_refs[i].at[totals[i].half_rows(held_refs[i], 2)[0]]
+
+    @pl.when(step == last - 1)
+    def first_half():
+        for i, (total, halves, held, recv) in list(enumerate(work))[:early]:
+            half_copy(i).wait()
+            total.end_half(1, held, recv[0])
+            total.start_half(2, held, recv[1])
+
+    @pl.when(step == last)
+    def second_half():
+        for i, (total, halves, held, recv) in list(enumerate(work))[early:]:
+            half_copy(i).wait()
+            total.end_half(1, held, recv[0])
+            total.start_half(2, held, recv[1])
+        for i, (total, halves, held, recv) in list(enumerate(work))[:early]:
+            total.end_half(2, held, recv[1])
+            total.start_z(eighth(i), z_recvs[i])
+
+    slot = pl.program_id(0)
+    chunks, parts, rows, model = grad_ref.shape
+    slots = pl.num_programs(0)
+    taken = rows // slots
+    both = grad_ref[...].astype(F32).reshape(chunks * parts, slots, taken, model)
+    grad = both[:, 0]
+    for j in range(1, slots):
+        grad = jnp.where(slot == j, both[:, j], grad)
+    grad = grad.reshape(chunks * parts * taken, model).T
     d_middle = ffn_backward(
         grad, act_ref[0], slope_ref[0], nf_ref[0], mid_ref[0], column(g2_ref), w1_ref, w2_ref, dw1_ref, dw2t_ref, dg2_ref
     )
@@ -1062,13 +1154,17 @@
 
     @pl.when(step == last)
     def finish():
-        first, second = sums_refs
-        lay_halves(first, 0, dw1_ref)
-        lay_halves(first, dw1_ref.shape[1], dwot_ref)
-        lay_halves(second, 0, dw2t_ref)
+        for sums, ref in zip(sums_refs, (dw2t_ref, dw1_ref, dwot_ref)):
+            lay_halves(sums, 0, ref)
         dg2_out[...] = dg2_ref[...]
-        for i, (total, piece, recv, region) in enumerate(zip(totals, piece_refs, z_recvs, region_refs)):
-            total.end_z_back(piece, region, recv.shape[2], local_sem.at[i])
+        for i, (total, halves, held, recv) in list(enumerate(work))[early:]:
+            total.end_half(2, held, recv[1])
+            part_copy(i).start()
+        for i, (total, halves, held, recv) in list(enumerate(work))[:early]:
+            total.end_z(eighth(i), z_recvs[i])
+            part_copy(i).start()
+        for i in range(len(work)):
+            part_copy(i).wait()
 
 
 def narrow_tile(parts, rows):
@@ -1082,14 +1178,19 @@
         target[half, :, at : at + width] = ref[half * rows // 2 : (half + 1) * rows // 2].astype(BF16)
 
 
-ORDERS = (("x", "y"), ("y", "x"))
-
-
-def time_ffn_backward(grad, act, slope, nf, mid, mixed, att, gate, linv, g2, w1, w2, wo, parts):
-    slots, frames, model = grad.shape
+XY, YX = ("x", "y"), ("y", "x")
+BAND_ORDERS = (YX, XY, YX, XY)
+BAND_EARLY = 2
+FFN_ORDERS = (YX, XY, YX)
+PAIR_ORDERS = (YX, YX, YX, None)
+
+
+def time_ffn_backward(grad, act, slope, nf, mid, mixed, att, gate, linv, g2, w1, w2, wo, halves_in):
+    slots, model, frames = mid.shape
     heads = gate.shape[1]
     inner, hidden = wo.shape[0], w1.shape[1]
-    tokens = min(frames, 512)
+    chunks, parts, _, _ = grad.shape
+    tokens = frames // 2
 
     def cut(rows):
         return pl.BlockSpec((1, rows, tokens), lambda s, c: (s, 0, c))
@@ -1099,12 +1200,11 @@
 
     consts = (g2, w1, w2, wo)
     anywhere = pl.BlockSpec(memory_space=pl.ANY)
-    halves = [(2, model // 2, hidden + inner), (2, model // 2, hidden)]
-    eighth = parts[0].shape[0]
-    widths = [part.shape[1] for part in parts]
+    halves = [(2, model // 2, width) for width in (hidden, hidden, inner)]
+    widths = [a.shape[1] for a in halves_in]
     dma = pltpu.SemaphoreType.DMA
     return pl.pallas_call(
-        lambda *refs: time_ffn_backward_kernel(heads, ORDERS, *refs),
+        lambda *refs: time_ffn_backward_kernel(heads, *refs),
         grid=(slots, frames // tokens),
         out_shape=(
             jax.ShapeDtypeStruct((slots, model, frames), F32),
@@ -1113,12 +1213,12 @@
             jax.ShapeDtypeStruct((slots, heads, frames), F32),
             [jax.ShapeDtypeStruct(shape, BF16) for shape in halves],
             jax.ShapeDtypeStruct((model, 1), F32),
-            [jax.ShapeDtypeStruct(part.shape, BF16) for part in parts],
+            [jax.ShapeDtypeStruct((model // 8, width), BF16) for width in widths],
         ),
-        in_specs=[pl.BlockSpec((1, tokens, model), lambda s, c: (s, c, 0))]
+        in_specs=[pl.BlockSpec((chunks // 2,) + grad.shape[1:], lambda s, c: (c, 0, 0, 0))]
         + [cut(a.shape[1]) for a in (act, slope, nf, mid, mixed, att, gate, linv)]
         + [whole_spec(c) for c in consts]
-        + [[whole_spec(part) for part in parts]],
+        + [[anywhere for _ in widths]],
         out_specs=(
             cut(model),
             cut(inner),
@@ -1126,25 +1226,39 @@
             cut(heads),
             [whole(*shape) for shape in halves],
             whole(model, 1),
-            [anywhere for _ in parts],
+            [anywhere for _ in widths],
         ),
         scratch_shapes=[
             pltpu.VMEM((model, hidden), F32),
             pltpu.VMEM((model, hidden), F32),
             pltpu.VMEM((model, inner), F32),
             pltpu.VMEM((model, 1), F32),
-            [pltpu.VMEM((eighth, width), BF16) for width in widths],
-            [pltpu.VMEM((Z_COUNT - 1, eighth, width // Z_COUNT), BF16) for width in widths],
-            dma((len(parts), TOTAL_STEPS)),
-            dma((len(parts), TOTAL_STEPS)),
-            dma((len(parts),)),
+            [pltpu.VMEM((model // 2, width), BF16) for width in widths],
+            [
+                [pltpu.VMEM((rows, width), BF16) for rows in (model // 4, model // 8)]
+                for width in widths
+            ],
+            [pltpu.VMEM((Z_COUNT - 1, model // 8, width // Z_COUNT), BF16) for width in widths[:BAND_EARLY]],
+            dma((len(widths), TOTAL_STEPS)),
+            dma((len(widths), TOTAL_STEPS)),
+            dma((2 * len(widths),)),
         ],
         compiler_params=pltpu.CompilerParams(
             vmem_limit_bytes=VMEM_BYTES, collective_id=2, has_side_effects=True
         ),
         cost_estimate=cost(8.0e6 * slots * frames, 0, 30e6),
         name="time_ffn_backward",
-    )(grad, act, slope, nf, mid, mixed, att, gate, linv, *consts, list(parts))
+    )(grad, act, slope, nf, mid, mixed, att, gate, linv, *consts, list(halves_in))
+
+
+BAND_PLACES = ((0, 4, 7, 11, 13), (0, 4, 7, 12, 14), (0, 4, 7, 11, 16, 18), (0, 5, 8, 12, 16, 18))
+FFN_PLACES = ((0, 1, 5, 8, 12, 15, 18, 24, 25), (0, 2, 6, 10, 13, 16, 20, 24, 25), (0, 2, 6, 9, 12, 15, 18, 22, 24))
+PAIR_PLACES = (
+    (4, 5, 8, 12, 15, 18, 22, 24, 25),
+    (8, 9, 12, 15, 17, 20, 23, 24, 25),
+    (12, 13, 15, 18, 21, 24, 25, 26, 27),
+    (16, 17, 21, 24, 25),
+)
 
 
 def time_attention_backward_kernel(
@@ -1166,10 +1280,10 @@
     sin_ref,
     g1_ref,
     wp_ref,
-    wg_ref,
+    wgt_ref,
     narrow_ref,
     dg2_ref,
-    region_refs,
+    part_refs,
     ffn_refs,
     grad_out,
     band_outs,
@@ -1178,10 +1292,13 @@
     dproj_ref,
     wp_turned_ref,
     grad_buf,
+    piece_refs,
+    band_recvs,
     held_refs,
     ffn_recvs,
     pair_refs,
     pair_recvs,
+    around_recv,
     band_sems,
     ffn_sems,
     pair_sems,
@@ -1201,18 +1318,14 @@
     last = pl.num_programs(0) - 1
     my_band, my_batch = place.band, place.batch
 
-    bands = [Total(place, order, band_sems[0].at[i], band_sems[1].at[i]) for i, order in enumerate(ORDERS)]
-    ffns = [Total(place, order, ffn_sems[0].at[i], ffn_sems[1].at[i]) for i, order in enumerate(ORDERS)]
+    bands = [Total(place, order, band_sems[0].at[i], band_sems[1].at[i]) for i, order in enumerate(BAND_ORDERS)]
+    ffns = [Total(place, order, ffn_sems[0].at[i], ffn_sems[1].at[i]) for i, order in enumerate(FFN_ORDERS)]
     own = [
-        Total(place, ORDERS[i % 2], pair_sems[0].at[i], pair_sems[1].at[i]) for i in range(pairs)
+        Total(place, PAIR_ORDERS[i], pair_sems[0].at[i], pair_sems[1].at[i]) for i in range(pairs)
     ]
 
-    def region_copy(i):
-        rows = bands[i].back_rows(band_outs[i], 2)
-        return pltpu.make_async_copy(region_refs[i], band_outs[i].at[rows], local_sem.at[i])
-
     def half_copy(i):
-        return pltpu.make_async_copy(ffn_refs[i].at[place.bits["core"]], held_refs[i], local_sem.at[2 + i])
+        return pltpu.make_async_copy(ffn_refs[i].at[place.bits["core"]], held_refs[i], local_sem.at[len(bands) + i])
 
     def eighth(total, held):
         return held.at[total.half_rows(held, 2)[0]]
@@ -1265,50 +1378,93 @@
         plan.setdefault(index, []).append(action)
 
     def enter():
-        others = [(my_band, lax.rem(my_batch + i, batch_count)) for i in range(1, batch_count)]
-        others += [place.across("y")] + [place.along_z(i)[1] for i in range(1, Z_COUNT)]
-        greet(others)
-        for i in range(2):
-            region_copy(i).start()
-            bands[i].start_back(2, band_outs[i], region_refs[i])
+        other_x = place.across("x")[1] // 2
+        diagonal = (my_band, 2 * other_x + 1 - place.bits["core"])
+        chips = [other for _, _, other in own[-1].around()]
+        greet(chips + [place.across("core"), diagonal])
+        for i in range(len(ffns)):
             half_copy(i).start()
 
+    tail = steps + slots * blocks
     at_step(0, enter)
-    for i in range(2):
-        for at, action in zip(
-            (2, 4, 6),
-            (
-                lambda i=i: (
-                    region_copy(i).wait(),
-                    bands[i].end_back(2, band_outs[i]),
-                    bands[i].start_back(1, band_outs[i]),
-                ),
-                lambda i=i: (bands[i].end_back(1, band_outs[i]), bands[i].start_back(0, band_outs[i])),
-                lambda i=i: bands[i].end_back(0, band_outs[i]),
-            ),
-        ):
+
+    def schedule(actions, places):
+        for at, action in zip(places, actions):
             at_step(at, action)
-        actions = all_steps(ffns[i], ffn_refs[i], held_refs[i], ffn_recvs[i], ffn_outs[i], local_sem.at[4 + i])
-        at_step(0, actions[0])
-        at_step(2, lambda i=i: half_copy(i).wait())
-        for at, action in zip((2, 4, 6, 8, 10, 12, 14, 16), actions[1:]):
-            at_step(at, action)
+
+    for i in range(len(bands)):
+        out = band_outs[i]
+        region = out.at[bands[i].back_rows(out, 2)]
+        quarter = band_outs[i].shape[1] // Z_COUNT
+
+        def z_begin(i=i):
+            piece_refs[i][...] = part_refs[i][...]
+            if i >= BAND_EARLY:
+                bands[i].start_z(piece_refs[i], band_recvs[i - BAND_EARLY])
+
+        def z_turn(i=i, region=region, quarter=quarter):
+            if i >= BAND_EARLY:
+                bands[i].end_z(piece_refs[i], band_recvs[i - BAND_EARLY])
+            bands[i].start_z_back(piece_refs[i], region, quarter, local_sem.at[i])
+
+        def z_end(i=i, region=region, quarter=quarter, out=out):
+            bands[i].end_z_back(piece_refs[i], region, quarter, local_sem.at[i])
+            bands[i].start_back(2, out)
+
+        def back_two(i=i, out=out):
+            bands[i].end_back(2, out)
+            bands[i].start_back(1, out)
+
+        def back_one(i=i, out=out):
+            bands[i].end_back(1, out)
+            bands[i].start_back(0, out)
+
+        actions = [z_begin, z_turn, z_end, back_two, back_one, lambda i=i, out=out: bands[i].end_back(0, out)]
+        if i < BAND_EARLY:
+            at_step(0, z_begin)
+            actions = actions[1:]
+        schedule(actions, BAND_PLACES[i])
+    ffn_at = len(bands) + len(ffns)
+    for i in range(len(ffns)):
+        sem = local_sem.at[ffn_at + i]
+        actions = all_steps(ffns[i], ffn_refs[i], held_refs[i], ffn_recvs[i], ffn_outs[i], sem)
+        at_step(FFN_PLACES[i][1], lambda i=i: half_copy(i).wait())
+        schedule(actions, FFN_PLACES[i])
+    pair_at = ffn_at + len(ffns)
+
+    def around_steps(total, source, held, recv, out, sem):
+        def s0():
+            total.start_core(source, recv[0])
+
+        def s1():
+            total.end_core(held, recv[0])
+            total.start_around(held, recv[1])
+
+        def s2():
+            total.end_around(held, recv[1])
+            total.start_around_back(held, recv[1], out, sem)
+
+        def s3():
+            total.end_around_back(held, recv[1], out, sem)
+            total.start_back(0, out)
+
+        def s4():
+            total.end_back(0, out)
+
+        return [s0, s1, s2, s3, s4]
+
     for i in range(pairs):
-        actions = all_steps(
-            own[i],
-            pair_refs.at[i],
-            pair_refs.at[i, place.bits["core"]],
-            [ref.at[i] for ref in pair_recvs],
-            pair_outs.at[i],
-            local_sem.at[6 + i],
-        )
-        begin = (i + 1) * 2 * slots
-        stride = 2 if i + 1 < pairs else 1
-        for n, action in enumerate(actions):
-            at_step(min(begin + n * stride, steps + slots * blocks - 1 + (n == len(actions) - 1)), action)
+        source, held = pair_refs.at[i], pair_refs.at[i, place.bits["core"]]
+        out, sem = pair_outs.at[i], local_sem.at[pair_at + i]
+        recv = [ref.at[i] for ref in pair_recvs]
+        if PAIR_ORDERS[i] is None:
+            actions = around_steps(own[i], source, held, [recv[0], around_recv], out, sem)
+        else:
+            actions = all_steps(own[i], source, held, recv, out, sem)
+        schedule(actions, PAIR_PLACES[i])
 
     for index in sorted(plan):
-        if index <= steps + slots * blocks - 1:
+        if index < tail:
 
             @pl.when(step == index)
             def work(index=index):
@@ -1374,14 +1530,14 @@
         j, i = index // blocks, lax.rem(index, blocks)
         at = pl.ds(pl.multiple_of(i * BLOCK, BLOCK), BLOCK)
         logit = logit_block_ref[0].astype(BF16)
-        d_normed = dg(wp_turned_ref[...], dproj_ref[j, :, at], NN) + dg(wg_ref[...], logit, NN)
+        d_normed = dg(wp_turned_ref[...], dproj_ref[j, :, at], NN) + dg(wgt_ref[...], logit, TN)
         d_rows, _ = norm_backward(x_ref[0].astype(F32).T, column(g1_ref), d_normed)
         grad_buf[index] = (dmid_ref[0] + d_rows).T.astype(BF16)
         i, source, target = message(index)
 
         @pl.when(i == my_batch)
         def keep():
-            pltpu.make_async_copy(source, target, local_sem.at[6 + pairs]).start()
+            pltpu.make_async_copy(source, target, local_sem.at[pair_at + pairs]).start()
 
         @pl.when(i != my_batch)
         def give():
@@ -1389,16 +1545,18 @@
 
     @pl.when(step == last)
     def finish():
-        for action in plan.get(steps + slots * blocks, []):
-            action()
-        await_bytes(grad_buf.at[pl.ds(0, slots)], local_sem.at[6 + pairs])
+        for index in sorted(plan):
+            if index >= tail:
+                for action in plan[index]:
+                    action()
+        await_bytes(grad_buf.at[pl.ds(0, slots)], local_sem.at[pair_at + pairs])
         others = grad_buf.at[pl.ds(0, slots * (batch_count - 1))]
         await_bytes(others, grad_sems.at[0])
         await_bytes(others, grad_sems.at[1])
 
 
 def time_attention_backward(
-    p, q, k, v, datt, minus, dlogit, n, x, dmid, cos, sin, g1, wp, wg, narrow, dg2, regions, ffn_sums, batch_count
+    p, q, k, v, datt, minus, dlogit, n, x, dmid, cos, sin, g1, wp, wgt, narrow, dg2, parts, ffn_sums, batch_count
 ):
     slots, inner, frames = q.shape
     heads = minus.shape[1]
@@ -1417,7 +1575,7 @@
     def per_head(rows, columns):
         return pl.BlockSpec((1, rows, columns), lambda t: (lax.rem(clamp(t), slots), clamp(t) // slots, 0))
 
-    consts = (n, dlogit, cos, sin, g1, wp, wg, narrow, dg2)
+    consts = (n, dlogit, cos, sin, g1, wp, wgt, narrow, dg2)
     anywhere = pl.BlockSpec(memory_space=pl.ANY)
     dma = pltpu.SemaphoreType.DMA
     widths = [a.shape[2] for a in ffn_sums]
@@ -1433,7 +1591,7 @@
         grid=(steps + slots * blocks,),
         out_shape=(
             jax.ShapeDtypeStruct((batch_count * slots, BLOCK, model), BF16),
-            [jax.ShapeDtypeStruct((model, a.shape[1]), BF16) for a in regions],
+            [jax.ShapeDtypeStruct((model, a.shape[1]), BF16) for a in parts],
             [jax.ShapeDtypeStruct((model, width), BF16) for width in widths],
             jax.ShapeDtypeStruct((pairs, model, pair_width), BF16),
         ),
@@ -1449,28 +1607,31 @@
             pl.BlockSpec((1, heads, BLOCK), lambda t: (tail(t) // blocks, 0, lax.rem(tail(t), blocks))),
         ]
         + [whole_spec(c) for c in consts]
-        + [[anywhere] * len(regions), [anywhere] * len(ffn_sums)],
-        out_specs=(anywhere, [anywhere] * len(regions), [anywhere] * len(ffn_sums), anywhere),
+        + [[whole_spec(a) for a in parts], [anywhere] * len(ffn_sums)],
+        out_specs=(anywhere, [anywhere] * len(parts), [anywhere] * len(ffn_sums), anywhere),
         scratch_shapes=[
             pltpu.VMEM((slots, 3 * inner, frames), BF16),
             pltpu.VMEM((model, 3 * inner), BF16),
             pltpu.VMEM((slots * blocks, BLOCK, model), BF16),
+            [pltpu.VMEM(a.shape, BF16) for a in parts],
+            [pltpu.VMEM((Z_COUNT - 1, a.shape[0], a.shape[1] // Z_COUNT), BF16) for a in parts[BAND_EARLY:]],
             [pltpu.VMEM((model // 2, width), BF16) for width in widths],
             [recv_buffers(width) for width in widths],
             pltpu.VMEM((pairs, 2, model // 2, pair_width), BF16),
             recv_buffers(pair_width, pairs),
-            [dma((2, TOTAL_STEPS)), dma((2, TOTAL_STEPS))],
-            [dma((2, TOTAL_STEPS)), dma((2, TOTAL_STEPS))],
+            pltpu.VMEM((4 * Z_COUNT - 1, model // 8, pair_width // Z_COUNT), BF16),
+            [dma((len(parts), TOTAL_STEPS))] * 2,
+            [dma((len(widths), TOTAL_STEPS))] * 2,
             [dma((pairs, TOTAL_STEPS)), dma((pairs, TOTAL_STEPS))],
             dma((2,)),
-            dma((7 + pairs,)),
+            dma((len(parts) + 2 * len(widths) + pairs + 1,)),
         ],
         compiler_params=pltpu.CompilerParams(
             vmem_limit_bytes=VMEM_BYTES, collective_id=3, has_side_effects=True
         ),
         cost_estimate=cost(20.0e6 * slots * frames, 0, 60e6),
         name="time_attention_backward",
-    )(p, q, k, v, datt, minus, x, dmid, dlogit, *consts, list(regions), list(ffn_sums))
+    )(p, q, k, v, datt, minus, x, dmid, dlogit, *consts, list(parts), list(ffn_sums))
 
 
 def finish_kernel(
@@ -1486,8 +1647,10 @@
     pair_ref,
     first_pair_ref,
     wp_ref,
-    wg_ref,
+    wgt_ref,
     g1_ref,
+    y_ref,
+    y_out,
     grad_out,
     dg1_out,
     dwp_out,
@@ -1508,6 +1671,12 @@
     pair = pl.program_id(0)
     inner = wp_ref.shape[1] // 3
     width = inner // pl.num_programs(0)
+    pairs, bands, parts, rows, model = y_ref.shape
+    split = y_ref[...].astype(F32).reshape(pairs, bands, parts, 2, rows // 2, model)
+    for j in range(2):
+        values = split[:, :, :, j].reshape(pairs, bands * parts * rows // 2, model)
+        for i in range(pairs):
+            y_out[2 * i + j] = values[i].astype(BF16)
     grad_out[...] = grad_ref[...].astype(F32)
     bwp_out[...] = bwp_ref[...].astype(F32)
     bw1_out[...] = bw1_ref[...].astype(F32)
@@ -1531,29 +1700,28 @@
     def narrow():
         tile = first_pair_ref[0, :, 3 * width :].astype(F32)
         rows = tile.T
-        bwg_out[...] = tile[:, :heads]
-        bg1_out[...] = rows[heads : heads + 1]
-        bg2_out[...] = rows[heads + 1 : heads + 2]
+        bwg_out[...] = rows[:heads]
+        bg1_out[...] = rows[heads]
+        bg2_out[...] = rows[heads + 1]
         gates = tile[:, heads + 2 : 2 * heads + 2]
-        dwg_out[...] = gates
-        dg2_out[...] = rows[2 * heads + 2 : 2 * heads + 3]
+        dwg_out[...] = rows[heads + 2 : 2 * heads + 2]
+        dg2_out[...] = rows[2 * heads + 2]
         sums = jnp.sum(scaled_ref[...], axis=1, keepdims=True)
-        sums = sums + jnp.sum(gates * wg_ref[...].astype(F32), axis=1, keepdims=True)
-        dg1_out[...] = jnp.broadcast_to(sums, (sums.shape[0], 128)).T[:1] / g1_ref[...].astype(F32)
-
-
-def finish_sums(grads, band_sums, ffn_sums, pair_sums, params, band_params):
-    g1, wp, wg, wo, g2, w1, w2 = params
+        sums = sums + jnp.sum(gates * wgt_ref[...].astype(F32).T, axis=1, keepdims=True)
+        dg1_out[...] = jnp.broadcast_to(sums, (sums.shape[0], 128)).T[0] / g1_ref[...].astype(F32)
+
+
+def finish_sums(grads, y, band_sums, ffn_sums, pair_sums, g1, params):
+    wp, wgt, wo, w1, w2 = params
     model, hidden = w1.shape
-    inner, heads = wo.shape[0], wg.shape[1]
+    inner, heads = wo.shape[0], wgt.shape[0]
     pairs = pair_sums.shape[0]
     split = hidden // pairs
     out_split = inner // pairs
     slot_dev, frame_dev, _ = grads.shape
 
-    def lanes(array, start, width):
-        first = start // width
-        return pl.BlockSpec((model, width), lambda i: (0, first + i))
+    def lanes(width):
+        return pl.BlockSpec((model, width), lambda i: (0, i))
 
     def whole(*shape):
         return pl.BlockSpec(shape, lambda i: (0,) * len(shape))
@@ -1561,25 +1729,26 @@
     def cut_rows(rows):
         return pl.BlockSpec((rows, model), lambda i: (i, 0))
 
-    band_first, band_second = band_sums
-    ffn_first, ffn_second = ffn_sums
+    band_wp, band_w1, band_w2t, band_wot = band_sums
+    time_w2t, time_w1, time_wot = ffn_sums
     grad_block = pl.BlockSpec((slot_dev // pairs, frame_dev, model), lambda i: (i, 0, 0))
-    narrow = [((1, model), whole(1, model)), ((model, heads), whole(model, heads))]
+    narrow = [((model,), whole(model)), ((heads, model), whole(heads, model))]
     per_layer = [
         narrow[0],
         ((model, 3 * inner), None),
         narrow[1],
         ((inner, model), cut_rows(out_split)),
         narrow[0],
-        ((model, hidden), lanes(None, 0, split)),
+        ((model, hidden), lanes(split)),
         ((hidden, model), cut_rows(split)),
     ]
-    shapes, specs = [jax.ShapeDtypeStruct(grads.shape, F32)], [grad_block]
+    shapes, specs = [jax.ShapeDtypeStruct(grads.shape, BF16), jax.ShapeDtypeStruct(grads.shape, F32)], [grad_block] * 2
+    y_block = pl.BlockSpec((y.shape[0] // pairs,) + y.shape[1:], lambda i: (i, 0, 0, 0, 0))
     for layer in range(2):
         for shape, spec in per_layer:
             shapes.append(jax.ShapeDtypeStruct(shape, F32))
             if spec is None:
-                spec = whole(*shape) if layer == 0 else lanes(None, 0, 3 * inner // pairs)
+                spec = whole(*shape) if layer == 0 else lanes(3 * inner // pairs)
             specs.append(spec)
     return pl.pallas_call(
         lambda *refs: finish_kernel(heads, *refs),
@@ -1587,18 +1756,19 @@
         out_shape=shapes,
         in_specs=[
             grad_block,
-            lanes(band_first, 0, 3 * inner // pairs),
-            lanes(band_second, 0, split),
-            lanes(band_second, hidden, split),
-            lanes(band_first, 3 * inner, out_split),
-            lanes(ffn_first, 0, split),
-            lanes(ffn_first, hidden, out_split),
-            lanes(ffn_second, 0, split),
+            lanes(3 * inner // pairs),
+            lanes(split),
+            lanes(split),
+            lanes(out_split),
+            lanes(split),
+            lanes(out_split),
+            lanes(split),
             pl.BlockSpec((1, model, pair_sums.shape[2]), lambda i: (i, 0, 0)),
             pl.BlockSpec((1, model, pair_sums.shape[2]), lambda i: (0, 0, 0)),
             whole_spec(wp),
-            whole_spec(wg),
+            whole_spec(wgt),
             whole_spec(g1),
+            y_block,
         ],
         out_specs=specs,
         scratch_shapes=[pltpu.VMEM((model, inner // pairs), F32)],
@@ -1606,18 +1776,19 @@
         name="finish_sums",
     )(
         grads,
-        band_first,
-        band_second,
-        band_second,
-        band_first,
-        ffn_first,
-        ffn_first,
-        ffn_second,
+        band_wp,
+        band_w1,
+        band_w2t,
+        band_wot,
+        time_w1,
+        time_wot,
+        time_w2t,
         pair_sums,
         pair_sums,
         wp,
-        wg,
+        wgt,
         g1,
+        y,
     )
 
 
@@ -1627,25 +1798,22 @@
     band_count,
     x_ref,
     cot_ref,
-    mask_ref,
-    bias_ref,
-    cos_ref,
-    sin_ref,
+    count_ref,
+    slots_ref,
     g1_ref,
     g2_ref,
+    wgt_ref,
     wpt_ref,
-    wgt_ref,
     wot_ref,
     w1t_ref,
     w2t_ref,
     wp_ref,
-    wg_ref,
     wo_ref,
     w1_ref,
     w2_ref,
     y_out,
     dx_out,
-    part_outs,
+    half_outs,
     narrow_out,
     q_ref,
     k_ref,
@@ -1679,11 +1847,14 @@
     dx_send,
     dx_recv,
     local_sem,
+    bias_ref,
+    cos_ref,
+    sin_ref,
+    valid_ref,
     halves,
-    half_recvs,
-    sum_sends,
-    sum_recvs,
-    part_sem,
+    core_recvs,
+    core_sems,
+    half_sem,
 ):
     step = pl.program_id(0)
     slot_count, part_frames, model = x_ref.shape
@@ -1697,8 +1868,6 @@
     my_band, my_batch = lax.axis_index("band"), lax.axis_index("batch")
     slot_dev = slot_count // band_count
     slots = slot_dev // batch_count
-    part_at = pl.multiple_of(part * part_frames, part_frames)
-    own_at = pl.multiple_of(my_band * (y_out.shape[1] // band_count) + part * part_frames, part_frames)
     own_chunk = my_batch * band_count + my_band
     chunks = band_count * batch_count
 
@@ -1715,17 +1884,27 @@
             axis=0,
         )
 
-    def put_tokens(ref, values):
+    def put_tokens(ref, values, start, stride):
         for c, at in enumerate(columns):
             turned = values[at].T
             for i in range(taken):
-                ref[c, pl.ds(first + i, slot_count, stride=part_frames), :] = turned[
+                ref[c, pl.ds(start + i, slot_count, stride=stride), :] = turned[
                     i * slot_count : (i + 1) * slot_count
                 ]
 
     @pl.when(step == 0)
     def enter():
         greet_all(band_count, batch_count)
+        bands = slots_ref[...].reshape(1, slot_count)
+        cos, sin = rotary_rows(jnp.maximum(bands, 0).astype(F32), size // 2)
+        cos_ref[...] = jnp.concatenate([cos] * taken, axis=1)
+        sin_ref[...] = jnp.concatenate([sin] * taken, axis=1)
+        valid = jnp.concatenate([jnp.where(bands >= 0, 1.0, 0.0)] * taken, axis=1)
+        valid_ref[...] = valid
+        keys = jnp.broadcast_to(valid[:, :BLOCK], (8, BLOCK)).T[:, :1]
+        row = lax.broadcasted_iota(jnp.int32, (BLOCK, BLOCK), 0) // slot_count
+        column_index = lax.broadcasted_iota(jnp.int32, (BLOCK, BLOCK), 1) // slot_count
+        bias_ref[...] = jnp.where((row == column_index) & (keys > 0.5), 0.0, NEG_FILL)
 
     @pl.when(lax.rem(step, per_part) == 0)
     def unpack():
@@ -1733,9 +1912,13 @@
             xs_ref[c] = x_ref[:, :, at].astype(F32).reshape(xs_ref.shape[1:])
             cots_ref[c] = cot_ref[:, :, at].astype(F32).reshape(cots_ref.shape[1:])
 
+    place = Place()
+    totals = [
+        Total(place, order, core_sems.at[0, i], core_sems.at[1, i]) for i, order in enumerate(BAND_ORDERS)
+    ]
     gain1, gain2 = column(g1_ref), column(g2_ref)
-    place = Place()
-    totals = [Total(place, order, sum_sends.at[i], sum_recvs.at[i]) for i, order in enumerate(ORDERS)]
+    piece = part_frames * (pl.num_programs(0) // per_part)
+    own_start = (my_batch * band_count + my_band) * piece
 
     @pl.when(step == 0)
     def clear():
@@ -1782,33 +1965,31 @@
         return carry
 
     lax.fori_loop(0, 4, expand, 0)
-    mask = mask_ref[0]
+    frame = own_start + step * taken + lax.broadcasted_iota(jnp.int32, (1, tokens), 1) // slot_count
+    mask = jnp.where(frame < count_ref[0], valid_ref[...], 0.0)
     result = (middle + dg(w2t_ref[...], act_ref[...], NN)) * mask
-    put_tokens(ys_ref, result)
-
-    @pl.when(lax.rem(step, per_part) == per_part - 1)
-    def send_rows():
-        for c, at in enumerate(columns):
-            y_buf[part, :, :, at] = ys_ref[c].reshape(slot_count, part_frames, 128).astype(BF16)
-
-        def give(i, carry):
-            other = lax.rem(my_band + i, band_count)
-            send(
-                y_buf.at[part, pl.ds(other * slot_dev, slot_dev)],
-                y_out.at[:, pl.ds(own_at, part_frames)],
-                y_send,
-                y_recv,
-                other,
-                my_batch,
-            )
-            return carry
-
-        lax.fori_loop(1, band_count, give, 0)
-        pltpu.make_async_copy(
-            y_buf.at[part, pl.ds(my_band * slot_dev, slot_dev)],
-            y_out.at[:, pl.ds(own_at, part_frames)],
-            local_sem.at[0],
-        ).start()
+    put_tokens(ys_ref, result, 0, taken)
+
+    couples = slot_dev // 2
+    for c, at in enumerate(columns):
+        y_buf[step, :, :, at] = ys_ref[c].reshape(slot_count // 2, 2 * taken, 128).astype(BF16)
+
+    def give_row(i, carry):
+        other = lax.rem(my_band + i, band_count)
+        send(
+            y_buf.at[step, pl.ds(other * couples, couples)],
+            y_out.at[:, my_band, step],
+            y_send,
+            y_recv,
+            other,
+            my_batch,
+        )
+        return carry
+
+    lax.fori_loop(1, band_count, give_row, 0)
+    pltpu.make_async_copy(
+        y_buf.at[step, pl.ds(my_band * couples, couples)], y_out.at[:, my_band, step], local_sem.at[0]
+    ).start()
 
     grad = tokens_of(cots_ref) * mask
     d_middle = ffn_backward(
@@ -1846,85 +2027,67 @@
     d_logit = jnp.concatenate([dlogit_ref[...], jnp.zeros_like(dlogit_ref)], axis=0).astype(BF16)
     dwp_ref[...] += dg(normed, dproj_ref[...], NT)
     dwg_ref[...] += dg(normed, d_logit, NT)[:, :heads]
-    d_normed = dg(wp_ref[...], dproj_ref[...], NN) + dg(wg_ref[...], dlogit_ref[...].astype(BF16), NN)
+    d_normed = dg(wp_ref[...], dproj_ref[...], NN) + dg(wgt_ref[...], dlogit_ref[...].astype(BF16), TN)
     d_rows, terms = norm_backward(rows, gain1, d_normed)
     dg1_ref[...] += jnp.sum(terms, axis=1, keepdims=True)
-    put_tokens(dxs_ref, d_middle + d_rows)
-
-    @pl.when(lax.rem(step, per_part) == per_part - 1)
-    def send_grads():
-        for c, at in enumerate(columns):
-            dx_buf[part, :, :, at] = dxs_ref[c].reshape(slot_count, part_frames, 128).astype(BF16)
-
-        def give(i, carry):
-            other = lax.rem(my_band * batch_count + my_batch + i, chunks)
-            band, batch = other // batch_count, lax.rem(other, batch_count)
-            for j in range(slots):
-                send(
-                    dx_buf.at[part, band * slot_dev + batch_count * j + batch],
-                    dx_out.at[j * chunks + own_chunk, pl.ds(part_at, part_frames)],
-                    dx_send,
-                    dx_recv,
-                    band,
-                    batch,
-                )
-            return carry
-
-        lax.fori_loop(1, chunks, give, 0)
-        for j in range(slots):
-            pltpu.make_async_copy(
-                dx_buf.at[part, my_band * slot_dev + batch_count * j + my_batch],
-                dx_out.at[j * chunks + own_chunk, pl.ds(part_at, part_frames)],
-                local_sem.at[1],
-            ).start()
+    put_tokens(dxs_ref, d_middle + d_rows, 0, taken)
+    for c, at in enumerate(columns):
+        grouped = dxs_ref[c].reshape(band_count, slots, batch_count, taken, 128)
+        grouped = jnp.concatenate([grouped[:, j][:, :, None] for j in range(slots)], axis=2)
+        dx_buf[step, :, :, at] = grouped.reshape(chunks, slots * taken, 128).astype(BF16)
+
+    def give_grad(i, carry):
+        other = lax.rem(my_band * batch_count + my_batch + i, chunks)
+        send(
+            dx_buf.at[step, other],
+            dx_out.at[own_chunk, step],
+            dx_send,
+            dx_recv,
+            other // batch_count,
+            lax.rem(other, batch_count),
+        )
+        return carry
+
+    lax.fori_loop(1, chunks, give_grad, 0)
+    pltpu.make_async_copy(
+        dx_buf.at[step, my_band * batch_count + my_batch], dx_out.at[own_chunk, step], local_sem.at[1]
+    ).start()
 
     @pl.when(step == pl.num_programs(0) - 1)
     def finish():
         narrow_out[...] = narrow_tile([dwg_ref[...], dg1_ref[...], dg2_ref[...]], model)
         core = place.bits["core"]
-        lay_halves(halves[0], 0, dwp_ref)
-        lay_halves(halves[0], dwp_ref.shape[1], dwot_ref)
-        totals[0].start_core(halves[0], half_recvs[0][0])
-        lay_halves(halves[1], 0, dw1_ref)
-        lay_halves(halves[1], dw1_ref.shape[1], dw2t_ref)
-        totals[1].start_core(halves[1], half_recvs[1][0])
-        held = [half.at[core] for half in halves]
+        for i, ref in enumerate((dwp_ref, dw1_ref, dw2t_ref, dwot_ref)):
+            lay_halves(halves[i], 0, ref)
+            totals[i].start_core(halves[i], core_recvs[i])
         for i, total in enumerate(totals):
-            total.end_core(held[i], half_recvs[i][0])
-            total.start_half(1, held[i], half_recvs[i][1])
-        for i, total in enumerate(totals):
-            total.end_half(1, held[i], half_recvs[i][1])
-            total.start_half(2, held[i], half_recvs[i][2])
-        for i, total in enumerate(totals):
-            total.end_half(2, held[i], half_recvs[i][2])
-            rows = total.half_rows(held[i], 2)[0]
-            pltpu.make_async_copy(held[i].at[rows], part_outs[i], part_sem.at[i]).start()
-        for i, total in enumerate(totals):
-            rows = total.half_rows(held[i], 2)[0]
-            pltpu.make_async_copy(held[i].at[rows], part_outs[i], part_sem.at[i]).wait()
-        piece = y_out.shape[1] // band_count
-        await_bytes(y_out.at[:, pl.ds(0, piece)], local_sem.at[0])
-        await_bytes(dx_out.at[pl.ds(0, slots)], local_sem.at[1])
+            total.end_core(halves[i].at[core], core_recvs[i])
+            pltpu.make_async_copy(halves[i].at[core], half_outs[i], half_sem.at[i]).start()
+        for i in range(len(totals)):
+            pltpu.make_async_copy(halves[i].at[core], half_outs[i], half_sem.at[i]).wait()
+        await_bytes(y_out.at[:, 0], local_sem.at[0])
+        await_bytes(dx_out.at[0], local_sem.at[1])
         for sem in (y_send, y_recv):
-            await_bytes(y_out.at[:, pl.ds(0, piece * (band_count - 1))], sem)
+            await_bytes(y_out.at[:, pl.ds(0, band_count - 1)], sem)
         for sem in (dx_send, dx_recv):
-            await_bytes(dx_out.at[pl.ds(0, slots * (chunks - 1))], sem)
-
-
-def band_layer(rows, cot, mask, bias, cos, sin, params, flips, band_count, batch_count):
-    prenorm, project, gating, output_weight, midnorm, expand, shrink = params
+            await_bytes(dx_out.at[pl.ds(0, chunks - 1)], sem)
+
+
+def band_layer(rows, cot, counts, slot_bands, g1, g2, params, flips, band_count, batch_count):
+    project, gating, output_weight, expand, shrink = params
     slot_count, piece, model = rows.shape
-    steps, _, tokens = mask.shape
-    heads, inner, hidden = gating.shape[1], output_weight.shape[0], expand.shape[1]
+    tokens = 2 * BLOCK
+    steps = slot_count * piece // tokens
+    heads, inner, hidden = gating.shape[0], output_weight.shape[0], expand.shape[1]
     groups = tokens // BLOCK
     taken = tokens // slot_count
     part_frames = 16
     per_part = part_frames // taken
-    parts = piece // part_frames
+    slots = slot_count // (band_count * batch_count)
     slot_dev = slot_count // band_count
-    consts = (bias, cos, sin, prenorm, midnorm) + flips + (project, gating, output_weight, expand, shrink)
-    widths = (3 * inner + inner, 2 * hidden)
-    eighth = model // 8
+    consts = (slot_bands, g1, g2, gating) + flips + (project, output_weight, expand, shrink)
+    widths = (3 * inner, hidden, hidden, inner)
+    chunks = band_count * batch_count
     blocks = pl.BlockSpec((slot_count, part_frames, model), lambda i: (0, i // per_part, 0))
     anywhere = pl.BlockSpec(memory_space=pl.ANY)
     dma = pltpu.SemaphoreType.DMA
@@ -1932,13 +2095,18 @@
         lambda *refs: band_kernel(heads, batch_count, band_count, *refs),
         grid=(steps,),
         out_shape=(
-            jax.ShapeDtypeStruct((slot_dev, piece * band_count, model), BF16),
-            jax.ShapeDtypeStruct((slot_count, piece, model), BF16),
-            [jax.ShapeDtypeStruct((eighth, width), BF16) for width in widths],
+            jax.ShapeDtypeStruct((slot_dev // 2, band_count, steps, 2 * taken, model), BF16),
+            jax.ShapeDtypeStruct((chunks, steps, slots * taken, model), BF16),
+            [jax.ShapeDtypeStruct((model // 2, width), BF16) for width in widths],
             jax.ShapeDtypeStruct((model, 128), F32),
         ),
-        in_specs=[blocks, blocks, pl.BlockSpec((1, 1, tokens), lambda i: (i, 0, 0))] + [whole_spec(c) for c in consts],
-        out_specs=(anywhere, anywhere, [anywhere] * 2, pl.BlockSpec((model, 128), lambda i: (0, 0))),
+        in_specs=[blocks, blocks, pl.BlockSpec(memory_space=pltpu.SMEM)] + [whole_spec(c) for c in consts],
+        out_specs=(
+            anywhere,
+            anywhere,
+            [anywhere for _ in widths],
+            pl.BlockSpec((model, 128), lambda i: (0, 0)),
+        ),
         scratch_shapes=[
             pltpu.VMEM((inner, tokens), BF16),
             pltpu.VMEM((inner, tokens), BF16),
@@ -1963,101 +2131,66 @@
             pltpu.VMEM((model, 1), F32),
             pltpu.VMEM((model // 128, slot_count * part_frames, 128), F32),
             pltpu.VMEM((model // 128, slot_count * part_frames, 128), F32),
-            pltpu.VMEM((model // 128, slot_count * part_frames, 128), F32),
-            pltpu.VMEM((model // 128, slot_count * part_frames, 128), F32),
-            pltpu.VMEM((parts, slot_count, part_frames, model), BF16),
-            pltpu.VMEM((parts, slot_count, part_frames, model), BF16),
+            pltpu.VMEM((model // 128, tokens, 128), F32),
+            pltpu.VMEM((model // 128, tokens, 128), F32),
+            pltpu.VMEM((steps, slot_count // 2, 2 * taken, model), BF16),
+            pltpu.VMEM((steps, chunks, slots * taken, model), BF16),
             dma,
             dma,
             dma,
             dma,
             dma((2,)),
+            pltpu.VMEM((BLOCK, BLOCK), F32),
+            pltpu.VMEM((inner // heads // 2, tokens), F32),
+            pltpu.VMEM((inner // heads // 2, tokens), F32),
+            pltpu.VMEM((1, tokens), F32),
             [pltpu.VMEM((2, model // 2, width), BF16) for width in widths],
-            [
-                [pltpu.VMEM((rows, width), BF16) for rows in (model // 2, model // 4, model // 8)]
-                for width in widths
-            ],
-            dma((2, TOTAL_STEPS)),
-            dma((2, TOTAL_STEPS)),
-            dma((2,)),
+            [pltpu.VMEM((model // 2, width), BF16) for width in widths],
+            dma((2, len(widths), TOTAL_STEPS)),
+            dma((len(widths),)),
         ],
         compiler_params=pltpu.CompilerParams(
             vmem_limit_bytes=VMEM_BYTES, collective_id=1, has_side_effects=True
         ),
         cost_estimate=cost(30.0e6 * slot_count * piece, 0, 60e6),
         name="band_layer",
-    )(rows, cot, mask, *consts)
+    )(rows, cot, counts, *consts)
 
 
 def slot_shards(activations, cotangent, frame_counts, slot_bands, *weights):
     slot_dev, _, frame_dev, model = activations.shape
-    slot_count = slot_bands.shape[0]
     batch, band = lax.axis_size("batch"), lax.axis_size("band")
-    frames = frame_dev * batch
-    piece = frame_dev // band
-    slots = slot_dev // batch
-    weights = tuple(w[None] if w.ndim == 1 else w for w in weights)
-    time_params, band_params = weights[:7], weights[7:]
-    heads, inner, hidden = time_params[2].shape[1], time_params[3].shape[0], time_params[5].shape[1]
-    size = inner // heads
-
-    positions = jnp.arange(frames, dtype=jnp.int32)
-    time_cos, time_sin = rotary_tables(positions.astype(F32), size)
-    time_bias = jnp.where(positions[None, :] < frame_counts[:, None], 0.0, NEG_FILL).astype(F32)
-    band_cos, band_sin = rotary_tables(jnp.maximum(slot_bands, 0).astype(F32), size)
-    tokens = min(2 * BLOCK, piece * slot_count)
-    copies = tokens // slot_count
-    slot_valid = slot_bands >= 0
-    index = jnp.arange(BLOCK, dtype=jnp.int32)
-    together = (index[:, None] // slot_count == index[None, :] // slot_count) & jnp.tile(
-        slot_valid, BLOCK // slot_count
-    )[:, None]
-    band_bias = jnp.where(together, 0.0, NEG_FILL).astype(F32)
-    own_start = lax.axis_index("batch") * frame_dev + lax.axis_index("band") * piece
-    own_frames = own_start + jnp.arange(piece, dtype=jnp.int32)
-    mask = ((own_frames < frame_counts[0])[:, None] & slot_valid[None, :]).astype(F32)
-    mask = mask.reshape(piece * slot_count // tokens, 1, tokens)
-
-    band_rows, band_cot, rows, n, q, k, v, p, linv, gate, att, mixed, mid, nf, act, slope, *flips = time_forward(
+    g1, wp, wg, wo, g2, w1, w2 = weights[:7]
+    band_g1, band_wp, band_wg, band_wo, band_g2, band_w1, band_w2 = weights[7:]
+    heads = wg.shape[1]
+    time_params = (wp, wg.T, wo, w1, w2)
+    band_params = (band_wp, band_wg.T, band_wo, band_w1, band_w2)
+    band_rows, band_cot, rows, n, q, k, v, p, linv, gate, att, mixed, mid, nf, act, slope, *turned = time_forward(
         activations.reshape(slot_dev, frame_dev, model),
         cotangent.reshape(slot_dev, frame_dev, model),
-        time_bias,
-        time_cos.T,
-        time_sin.T,
+        frame_counts,
+        g1,
+        g2,
         time_params,
         band_params,
         band,
         batch,
     )
-    layer_output, slot_grad, band_parts, band_narrow = band_layer(
+    cos, sin = turned[-2:]
+    y, slot_grad, band_halves, band_narrow = band_layer(
         band_rows,
         band_cot,
-        mask,
-        band_bias,
-        jnp.tile(band_cos.T, (1, copies)),
-        jnp.tile(band_sin.T, (1, copies)),
+        frame_counts,
+        slot_bands,
+        band_g1,
+        band_g2,
         band_params,
-        tuple(flips),
+        tuple(turned[:-2]),
         band,
         batch,
     )
-    slot_grad = slot_grad.reshape(slots, frames, model)
-    g1, g2 = time_params[0], time_params[4]
-    dmid, datt, minus, dlogit, ffn_sums, dg2, regions = time_ffn_backward(
-        slot_grad,
-        act,
-        slope,
-        nf,
-        mid,
-        mixed,
-        att,
-        gate,
-        linv,
-        g2,
-        time_params[5],
-        time_params[6],
-        time_params[3],
-        band_parts,
+    dmid, datt, minus, dlogit, ffn_halves, dg2, band_parts = time_ffn_backward(
+        slot_grad, act, slope, nf, mid, mixed, att, gate, linv, g2, w1, w2, wo, band_halves
     )
     input_grad, band_sums, ffn_sums, pair_sums = time_attention_backward(
         p,
@@ -2070,19 +2203,21 @@
         n,
         rows,
         dmid,
-        time_cos.T,
-        time_sin.T,
+        cos,
+        sin,
         g1,
+        wp,
         time_params[1],
-        time_params[2],
         band_narrow,
         dg2,
-        regions,
-        ffn_sums,
+        band_parts,
+        ffn_halves,
         batch,
     )
-    input_grad, *grads = finish_sums(input_grad, band_sums, ffn_sums, pair_sums, time_params, band_params)
-    grads = [g[0] if g.shape[0] == 1 else g for g in grads]
+    layer_output, input_grad, *grads = finish_sums(
+        input_grad, y, band_sums, ffn_sums, pair_sums, g1, time_params
+    )
+    grads = [g.T if g.shape[0] == heads else g for g in grads]
     return (layer_output.reshape(activations.shape), input_grad.reshape(activations.shape), *grads)
 
 
@@ -2095,8 +2230,9 @@
         and band == 2 * Z_COUNT
         and slot_dev % batch == 0
         and frame_dev == BLOCK
-        and frame_dev % (16 * band) == 0
-        and slot_bands.shape[0] == 64
+        and frame_dev == 32 * band
+        and slot_bands.shape[0] == 64 == slot_dev * band
+        and slot_dev == 2 * batch
         and activations.shape[-1] % 128 == 0
         and (frame_dev // band * slot_bands.shape[0]) % (2 * BLOCK) == 0
         and weights[2].shape[1] == 8

time: 434 us -> 364 us (0.84)
  Pallas kernels: 408 us -> 362 us
  local copies, waits for them, and re-layouts: 14.1 us -> 0 us
  other arithmetic: 9.85 us -> 0 us
    pallas_call x1, Pallas kernels: 144 us -> 118 us  [band_layer(): pl.pallas_call(lambda *refs: band_kernel(heads, batch_count, band_count,...]
    pallas_call x1, Pallas kernels: 124 us -> 98.7 us  [time_attention_backward(): pl.pallas_call(lambda *refs: time_attention_backward_kernel(heads, slots,...]
    unnamed x7 -> x0, local copies, waits for them, and re-layouts: 7.33 us -> none
    pallas_call x4 -> x0, other arithmetic: 5.08 us -> none  [finish_sums(): pl.pallas_call(lambda *refs: finish_kernel(heads, *refs), grid=(pairs,),...]
    broadcast_in_dim x4 -> x0, local copies, waits for them, and re-layouts: 4.97 us -> none  [slot_shards(): weights = tuple((w[None] if w.ndim == 1 else w for w in weights))]
where the time goes in v5:
time: 364 us
  Pallas kernels  362 us (99%)
    pallas_call x1, Pallas kernels, band_layer(): pl.pallas_call(lambda *refs: band_kernel(heads, batch_count, band_count,...  118 us
    pallas_call x1, Pallas kernels, time_attention_backward(): pl.pallas_call(lambda *refs: time_attention_backward_kernel(heads, slots,...  98.7 us
    pallas_call x1, Pallas kernels, time_forward(): pl.pallas_call(lambda *refs: time_forward_kernel(heads, batch_count, band...  93.8 us
    pallas_call x1, Pallas kernels, time_ffn_backward(): pl.pallas_call(lambda *refs: time_ffn_backward_kernel(heads, *refs), grid...  37.1 us
    pallas_call x1, Pallas kernels, finish_sums(): pl.pallas_call(lambda *refs: finish_kernel(heads, *refs), grid=(pairs,),...  14.2 us

profile of v5, /device:TPU:0, one launch (start us, length us, event | category | flops | bytes accessed | tf_op | source)
XLA Modules:
  0.0 363.5 jit_solution(15866062103360320176)
XLA Ops:
  1.3 93.8 %time_forward.1 = (bf16[64,32,384]{2,1,0:T(8,128)(2,1)}, bf16[64,32,384]{2,1,0:T(8,128)(2,1)}, bf16[2,1024,384]{2,1,0:T(8,128)(2,1)}, bf16[2,384,1024]{2,1,0:T(8...) custom-call(bf16[8,256,384]{2,1,0:T(8,128)(2,1)} %bitcast.16, ...), custom_call_target="tpu_custom_call" | custom-call | flops 16384000000 | bytes 60000000 | tf_op jit(solution)/shard_map/time_forward/pallas_call | solution.py:993
  95.1 118.3 %band_layer.1 = (bf16[4,8,4,16,384]{4,3,2,1,0:T(8,128)(2,1)}, bf16[32,4,16,384]{3,2,1,0:T(8,128)(2,1)}, bf16[192,1536]{1,0:T(8,128)(2,1)}, bf16[192,1536]{1,0:T(...) custom-call(bf16[64,32,384]{2,1,0:T(8,128)(2,1)} %get-tuple-element.86.refs_0_, ...), custom_call_target="tpu_custom_call" | custom-call | flops 61440000000 | bytes 60000000 | tf_op jit(solution)/shard_map/band_layer/pallas_call | solution.py:2094
  213.4 37.1 %time_ffn_backward.1 = (f32[2,384,1024]{2,1,0:T(8,128)}, bf16[2,512,1024]{2,1,0:T(8,128)(2,1)}, f32[2,8,1024]{2,1,0:T(8,128)}, f32[2,8,1024]{2,1,0:T(8,128)}, bf...) custom-call(bf16[32,4,16,384]{3,2,1,0:T(8,128)(2,1)} %get-tuple-elem, ...), custom_call_target="tpu_custom_call" | custom-call | flops 16384000000 | bytes 30000000 | tf_op jit(solution)/shard_map/time_ffn_backward/pallas_call | solution.py:1206
  250.5 98.7 %time_attention_backward.1 = (bf16[8,256,384]{2,1,0:T(8,128)(2,1)}, bf16[384,1536]{1,0:T(8,128)(2,1)}, bf16[384,1536]{1,0:T(8,128)(2,1)}, bf16[384,1536]{1,0:T(8...) custom-call(bf16[2,8,1024,1024]{3,2,1,0:T(8,128)(2,1)} %get-tuple-el, ...), custom_call_target="tpu_custom_call" | custom-call | flops 40960000000 | bytes 60000000 | tf_op jit(solution)/shard_map/time_attention_backward/pallas_call | solution.py:1589
  349.2 14.2 %finish_sums.1 = (bf16[8,256,384]{2,1,0:T(8,128)(2,1)}, f32[8,256,384]{2,1,0:T(8,128)}, f32[384]{0:T(512)}, f32[384,1536]{1,0:T(8,128)}, f32[8,384]{1,0:T(8,128)...) custom-call(bf16[8,256,384]{2,1,0:T(8,128)(2,1)} %get-tuple-element., ...), custom_call_target="tpu_custom_call" | custom-call | tf_op jit(solution)/shard_map/finish_sums/pallas_call | solution.py:1753
